TPU v7x, 128 devices: a whole 4x4x4 slice. The times are simulated.
128 devices in a mesh: tok: 16 (over y_lo, x, core), tp: 8 (over z, y_hi).
Axes of the slice: x: 4, y: 4 (y_hi: 2, y_lo: 2; y = y_hi * 2 + y_lo), z: 4, core: 2. Of those that a mesh axis runs over, the one named last changes fastest.
Arguments:
- layer_input: bfloat16 [1536, 8192], P('tok'), may hold values from -45 to 45, as said below
- output_grad: bfloat16 [1536, 8192], P('tok'), may hold values from -45 to 45, as said below
- gate_weight: bfloat16 [8192, 16384], P('tok', 'tp'), may hold values from -0.0625 to 0.0625
- down_weight: bfloat16 [16384, 8192], P('tp', 'tok'), may hold values from -0.0625 to 0.0625
Outputs:
- input_gram: float32 [8192, 8192], P('tok', 'tp')
- grad_gram: float32 [16384, 16384], P('tp', 'tok')
Inputs may be any that keep to these rules, and one draw needn't show every extreme that they name: `layer_input`: token rows and feature columns carry scales of their own. `output_grad`: token rows and feature columns carry scales of their own.
All inputs are finite; a program needn't handle non-finite values.
Results may differ from a plain program's by a relative error of at most 0.0039.
Values may be sent and summed in bfloat16 or wider, within the bound.
No kernel may reach another device: no remote copies, remote signals or barrier semaphores. Data moves between devices by JAX's collectives and lax.ppermute only.
A program may use at most 128 MiB of HBM per device.

v0:
```python
import jax
import jax.numpy as jnp
from jax import lax
from jax.sharding import PartitionSpec as P

D = 8192


def contract_rows(left, right):
    return lax.dot_general(
        left, right, (((0,), (0,)), ((), ())), preferred_element_type=jnp.float32
    )


def contract_cols(left, right):
    return lax.dot_general(
        left, right, (((1,), (1,)), ((), ())), preferred_element_type=jnp.float32
    )


def shards(layer_input, output_grad, gate_weight, down_weight):
    tok_count = lax.axis_size("tok")
    local_rows = layer_input.shape[0]
    total_rows = local_rows * tok_count
    band_width = D // lax.axis_size("tp")
    input_cols, grad_cols = (
        lax.all_to_all(layer_input, "tok", split_axis=1, concat_axis=0, tiled=True),
        lax.all_to_all(output_grad, "tok", split_axis=1, concat_axis=0, tiled=True),
    )
    band_start = lax.axis_index("tp") * band_width
    own_band = lax.dynamic_slice_in_dim(layer_input, band_start, band_width, 1)
    rows = input_cols
    input_gram = (
        contract_rows(rows, lax.all_gather(own_band, "tok", axis=0, tiled=True)) / total_rows
    )
    rows = input_cols
    gate = lax.psum_scatter(
        jnp.dot(rows, gate_weight, preferred_element_type=jnp.float32),
        "tok",
        scatter_dimension=0,
        tiled=True,
    )
    rows = grad_cols
    hidden_grad = lax.psum_scatter(
        contract_cols(rows, down_weight), "tok", scatter_dimension=0, tiled=True
    )
    up_grad = (hidden_grad * jax.nn.silu(gate)).astype(jnp.bfloat16)
    all_units = lax.all_gather(up_grad, "tp", axis=1, tiled=True)
    unit_cols = lax.all_to_all(all_units, "tok", split_axis=1, concat_axis=0, tiled=True)
    rows = unit_cols
    grad_gram = contract_rows(lax.all_gather(up_grad, "tok", axis=0, tiled=True), rows) / total_rows
    return (input_gram, grad_gram)


def solution(mesh):
    placed = (P("tok", None), P("tok", None), P("tok", "tp"), P("tp", "tok"))
    return jax.shard_map(
        shards,
        mesh=mesh,
        in_specs=placed,
        out_specs=(P("tok", "tp"), P("tp", "tok")),
        check_vma=False,
    )
```

profile of v0, /device:TPU:1, one launch (start us, length us, event | category | flops | bytes accessed | tf_op | source)
XLA Modules:
  0.0 417.5 jit_solution(10285906680211302148)
XLA Ops:
  7.2 0.0 copy-start
  7.2 0.0 reduce-scatter.5.cloned.1.call-start
  7.2 1.7 copy.25
  8.9 27.7 %all_to_all.57 = bf16[96,16,512]{2,0,1:T(8,128)(2,1)S(1)} all-to-all(bf16[96,16,512]{2,0,1:T(8,128)(2,1)S(1)} %bitcast.31), channel_id=1, replica_groups=mesh['tok'=16,'tp'=8] {'tok'}, dimensions={1} | all-to-all | bytes 3145728 | tf_op jit(solution)/shard_map/all_to_all | solution.py:27
  36.7 0.0 copy-start.2
  36.7 1.1 copy-done.2
  37.8 0.0 copy-done
  37.8 6.4 %fusion.1 = f32[1536,2048]{1,0:T(8,128)} fusion(bf16[1536,512]{1,0:T(8,128)(2,1)S(1)} %bitcast.36, bf16[512,2048]{1,0:T(8,128)(2,1)S(1)} %copy-done), kind=kOutput, calls=%fused_computation.8 | convolution fusion | flops 3221225472 | bytes 16252928 | tf_op jit(solution)/shard_map/dot_general | solution.py:38
  44.2 0.0 reduce-scatter.5.cloned.1.call-update
  44.2 0.0 reduce-scatter.3.cloned.1.call-start
  44.3 1.6 copy.24
  45.9 0.0 copy-start.3
  45.9 31.5 %all_to_all.58 = bf16[96,16,512]{2,0,1:T(8,128)(2,1)S(1)} all-to-all(bf16[96,16,512]{2,0,1:T(8,128)(2,1)S(1)} %bitcast.32), channel_id=1, replica_groups=mesh['tok'=16,'tp'=8] {'tok'}, dimensions={1} | all-to-all | bytes 3145728 | tf_op jit(solution)/shard_map/all_to_all | solution.py:28
  77.3 0.0 copy-done.3
  77.3 6.5 %fusion = f32[1536,2048]{1,0:T(8,128)} fusion(bf16[1536,512]{1,0:T(8,128)(2,1)S(1)} %bitcast.38, bf16[2048,512]{1,0:T(8,128)(2,1)S(1)} %copy-done.3), kind=kOutput, calls=%fused_computation.7 | convolution fusion | flops 3221225472 | bytes 16252928 | tf_op jit(solution)/shard_map/dot_general | solution.py:16
  83.9 0.0 reduce-scatter.3.cloned.1.call-update
  83.9 0.0 all-gather.8.cloned.1.call-start
  84.0 53.7 %reduce-scatter.5.cloned.1.call-done = f32[96,2048]{1,0:T(8,128)} async-done(((f32[1536,2048]{1,0:T(8,128)}), f32[96,2048]{1,0:T(8,128)}) %reduce-scatter.5.cloned.1.call-update) | async-done | bytes 786448 | tf_op jit(solution)/shard_map/reduce_scatter | solution.py:37
  137.6 84.9 %reduce-scatter.3.cloned.1.call-done = f32[96,2048]{1,0:T(8,128)} async-done(((f32[1536,2048]{1,0:T(8,128)}), f32[96,2048]{1,0:T(8,128)}) %reduce-scatter.3.cloned.1.call-update) | async-done | bytes 786448 | tf_op jit(solution)/shard_map/reduce_scatter | solution.py:44
  222.5 2.4 multiply_convert_fusion
  224.8 0.0 all-gather.8.cloned.1.call-update
  224.9 0.0 all-gather.4.cloned.1.call-start
  224.9 1.6 constant_dynamic-slice_fusion
  226.6 0.0 all-gather.4.cloned.1.call-update
  226.6 0.0 all-gather.6.cloned.1.call-start
  226.6 0.5 all-gather.6.cloned.1.call-update
  227.2 62.3 %all-gather.8.cloned.1.call-done = bf16[96,16384]{1,0:T(8,128)(2,1)} async-done(((bf16[96,2048]{1,0:T(8,128)(2,1)}), bf16[96,16384]{1,0:T(8,128)(2,1)}) %all-gather.8.cloned.1.call-update) | async-done | bytes 3145744 | tf_op jit(solution)/shard_map/all_gather | solution.py:48
  289.5 4.0 copy.23
  293.5 5.4 %all-to-all-start.2 = ((bf16[96,16,1024]{2,0,1:T(8,128)(2,1)}), bf16[96,16,1024]{2,0,1:T(8,128)(2,1)}, u32[]{:S(2)}, u32[]{:S(2)}) async-start(bf16[96,16,1024]{2,0,1:T(8,128)(2,1)} %bitcast.28), calls=%async_computation.4 | async-start | bytes 6291456 | tf_op jit(solution)/shard_map/all_to_all | solution.py:49
  298.9 56.3 %all-gather.4.cloned.1.call-done = bf16[1536,1024]{1,0:T(8,128)(2,1)} async-done(((bf16[96,1024]{1,0:T(8,128)(2,1)}), bf16[1536,1024]{1,0:T(8,128)(2,1)}) %all-gather.4.cloned.1.call-update) | async-done | bytes 3145744 | tf_op jit(solution)/shard_map/all_gather | solution.py:34
  355.1 4.2 multiply_bitcast_fusion
  359.3 1.8 copy.16
  361.1 0.0 all-to-all-done.2
  361.1 37.9 %all-gather.6.cloned.1.call-done = bf16[1536,2048]{1,0:T(8,128)(2,1)} async-done(((bf16[96,2048]{1,0:T(8,128)(2,1)}), bf16[1536,2048]{1,0:T(8,128)(2,1)}) %all-gather.6.cloned.1.call-update) | async-done | bytes 6291472 | tf_op jit(solution)/shard_map/all_gather | solution.py:51
  399.0 0.0 copy-start.1
  399.0 12.0 %convolution_multiply_fusion = f32[2048,1024]{1,0:T(8,128)} fusion(bf16[1536,2048]{1,0:T(8,128)(2,1)} %all-gather.6.cloned.1.call-done, bf16[1536,1024]{1,0:T(8,128)(2,1)} %bitcast.7), kind=kOutput, calls=%fused_computation | convolution fusion | flops 6444548096 | bytes 17825792 | tf_op jit(solution)/shard_map/dot_general | solution.py:10
  411.0 0.0 copy-done.1
Async XLA Ops:
  7.2 30.7 %copy-start = (bf16[512,2048]{1,0:T(8,128)(2,1)S(1)}, bf16[512,2048]{1,0:T(8,128)(2,1)}, u32[]{:S(2)}) copy-start(bf16[512,2048]{1,0:T(8,128)(2,1)} %param.6) | copy-start | bytes 6291460
  7.2 130.4 %reduce-scatter.5.cloned.1.call-start = ((), (), s32[]{:S(2)}) async-start(), calls=%async_computation.7 | async-start | bytes 13369344 | tf_op jit(solution)/shard_map/reduce_scatter | solution.py:37
  36.7 1.1 copy-start.2
  44.2 178.2 %reduce-scatter.3.cloned.1.call-start = ((), (), s32[]{:S(2)}) async-start(), calls=%async_computation.6 | async-start | bytes 13369344 | tf_op jit(solution)/shard_map/reduce_scatter | solution.py:44
  45.9 31.5 %copy-start.3 = (bf16[2048,512]{1,0:T(8,128)(2,1)S(1)}, bf16[2048,512]{1,0:T(8,128)(2,1)}, u32[]{:S(2)}) copy-start(bf16[2048,512]{1,0:T(8,128)(2,1)} %param.7) | copy-start | bytes 6291460
  83.9 205.6 %all-gather.8.cloned.1.call-start = ((), (), s32[]{:S(2)}) async-start(), calls=%async_computation.9 | async-start | bytes 3538944 | tf_op jit(solution)/shard_map/all_gather | solution.py:48
  224.9 130.3 %all-gather.4.cloned.1.call-start = ((), (), s32[]{:S(2)}) async-start(), calls=%async_computation.5 | async-start | bytes 3342336 | tf_op jit(solution)/shard_map/all_gather | solution.py:34
  226.6 172.4 %all-gather.6.cloned.1.call-start = ((), (), s32[]{:S(2)}) async-start(), calls=%async_computation.8 | async-start | bytes 6684672 | tf_op jit(solution)/shard_map/all_gather | solution.py:51
  293.5 67.6 %all-to-all-start.2 = ((bf16[96,16,1024]{2,0,1:T(8,128)(2,1)}), bf16[96,16,1024]{2,0,1:T(8,128)(2,1)}, u32[]{:S(2)}, u32[]{:S(2)}) async-start(bf16[96,16,1024]{2,0,1:T(8,128)(2,1)} %bitcast.28), calls=%async_computation.4 | async-start | bytes 6291456 | tf_op jit(solution)/shard_map/all_to_all | solution.py:49
  399.0 12.0 %copy-start.1 = (bf16[512,2048]{1,0:T(8,128)(2,1)S(1)}, bf16[512,2048]{1,0:T(8,128)(2,1)}, u32[]{:S(2)}) copy-start(bf16[512,2048]{1,0:T(8,128)(2,1)} %param.6) | copy-start | bytes 6291460
Sparse Core Ops, SparseCore 0:
  44.4 93.1 reduce-scatter.4
  140.0 82.4 reduce-scatter.2
  225.0 64.4 all-gather.7
  291.1 64.0 all-gather.3
  356.7 42.2 all-gather.5
where the time goes:
time: 418 us; the launch traced here: 417 us
  waiting for transfers between devices  296 us (71%)
  blocking collectives  59.2 us (14%)
  matrix products  29.1 us (7%)
  between operations  13.8 us (3%)
  local copies, waits for them, and re-layouts  11.9 us (3%)
  starting transfers between devices  5.58 us (1%)
    reduce_scatter x1, waiting for transfers between devices, shards(): lax.psum_scatter(contract_cols(rows, down_weight), 'tok', scatter_dimensi...  84.9 us
    all_gather x1, waiting for transfers between devices, shards(): all_units = lax.all_gather(up_grad, 'tp', axis=1, tiled=True)  62.3 us
    all_gather x1, waiting for transfers between devices, shards(): lax.all_gather(own_band, 'tok', axis=0, tiled=True)  56.3 us
    reduce_scatter x1, waiting for transfers between devices, shards(): lax.psum_scatter(jnp.dot(rows, gate_weight, preferred_element_type=jnp.fl...  53.7 us
    all_gather x1, waiting for transfers between devices, shards(): lax.all_gather(up_grad, 'tok', axis=0, tiled=True)  37.9 us
    all_to_all x1, blocking collectives, shards(): lax.all_to_all(output_grad, 'tok', split_axis=1, concat_axis=0, tiled=True)  31.5 us
    all_to_all x1, blocking collectives, shards(): lax.all_to_all(layer_input, 'tok', split_axis=1, concat_axis=0, tiled=True)  27.7 us
    dot_general x2, matrix products, contract_rows(): lax.dot_general(left, right, (((0,), (0,)), ((), ())), preferred_element_...  16.1 us
  transfers between devices with their start and end apart: 6, of which 5 were waited for; matrix products, arithmetic and copies ran while one was open for 5% of the time, Pallas kernels for 0%

commit v1 on v0

v1 whole, which is shorter than its diff:
```python
import jax
import jax.numpy as jnp
from jax import lax
from jax.sharding import PartitionSpec as P

AXES = ("tok", "tp")
CHIPS = 8
CORES = 2
TOP = 32768.0
TINY = 1e-18


def contract_rows(left, right):
    return lax.dot_general(
        left, right, (((0,), (0,)), ((), ())), preferred_element_type=jnp.float32
    )


def contract_cols(left, right):
    return lax.dot_general(
        left, right, (((1,), (1,)), ((), ())), preferred_element_type=jnp.float32
    )


def routes(move):
    pairs = []
    for s in range(CHIPS):
        for c in range(CORES):
            for p in range(CHIPS):
                ns, nc, np_ = move(s, c, p)
                pairs.append(((s * CORES + c) * CHIPS + p, (ns * CORES + nc) * CHIPS + np_))
    return pairs


def send(value, move):
    return lax.ppermute(value, AXES, routes(move))


def swap_cores(value):
    return send(value, lambda s, c, p: (s, 1 - c, p))


SAME_CORE = [[s * CORES + c for s in range(CHIPS)] for c in range(CORES)]


def exchange(value, split_axis):
    return lax.all_to_all(
        value, "tok", split_axis, 0, axis_index_groups=SAME_CORE, tiled=True
    )


def in_core_order(core, own, other, axis):
    first = jnp.where(core == 0, own, other)
    second = jnp.where(core == 0, other, own)
    return jnp.concatenate([first, second], axis)


def largest(value, axis=None):
    return jnp.maximum(jnp.max(jnp.abs(value), axis=axis).astype(jnp.float32), TINY)


def reduce_partials(partial, row_top, weight_top, own_tops):
    depth = 1024.0
    scaled = (partial * (TOP / depth / (row_top[:, None] * weight_top))).astype(jnp.float16)
    parts = exchange(scaled, 0).reshape(CHIPS, -1, partial.shape[1])
    back = own_tops.T[:, :, None] * (weight_top * (depth / TOP))
    return jnp.sum(parts.astype(jnp.float32) * back, axis=0)


def shards(layer_input, output_grad, gate_weight, down_weight):
    rows = layer_input.shape[0]
    total = rows * CHIPS * CORES
    place = lax.axis_index("tok")
    chip, core = place // CORES, place % CORES
    band = lax.axis_index("tp")
    width = layer_input.shape[1] // CHIPS

    other_gate = swap_cores(gate_weight)
    other_down = swap_cores(down_weight)
    gate_full = in_core_order(core, gate_weight, other_gate, 0)
    down_full = in_core_order(core, down_weight, other_down, 1)
    tops = jnp.stack([largest(gate_full), largest(down_full)])
    for bit in (1, 2, 4):
        tops = jnp.maximum(tops, send(tops, lambda s, c, p: (s ^ bit, c, p)))
    own_input_tops = largest(layer_input.reshape(rows, CHIPS, width), 2)
    own_grad_tops = largest(output_grad.reshape(rows, CHIPS, width), 2)

    input_cols = exchange(layer_input, 1)
    gate = reduce_partials(
        jnp.dot(input_cols, gate_full, preferred_element_type=jnp.float32),
        largest(input_cols, 1),
        tops[0],
        own_input_tops,
    )
    grad_cols = exchange(output_grad, 1)
    hidden_grad = reduce_partials(
        contract_cols(grad_cols, down_full),
        largest(grad_cols, 1),
        tops[1],
        own_grad_tops,
    )

    own_band = lax.dynamic_slice_in_dim(layer_input, band * width, width, 1)
    band_rows = lax.all_gather(own_band, "tok", axis=0, tiled=True)
    half = width // CORES
    mine = lax.dynamic_slice_in_dim(input_cols, core * half, half, 1)
    theirs = swap_cores(lax.dynamic_slice_in_dim(input_cols, (1 - core) * half, half, 1))
    left = in_core_order(
        core, mine.reshape(CHIPS, 1, rows, half), theirs.reshape(CHIPS, 1, rows, half), 1
    ).reshape(total, half)
    input_gram = contract_rows(left, band_rows) / total

    up_grad = (hidden_grad * (gate / (1.0 + jnp.exp(-gate)))).astype(jnp.bfloat16)
    all_rows = lax.all_gather(up_grad, "tok", axis=0, tiled=True)
    moved = send(up_grad, lambda s, c, p: (s, c, s ^ p))
    moved = send(moved, lambda s, c, p: (s ^ p, c, p))
    units = up_grad.shape[1]
    gathered = jnp.zeros((CHIPS, rows, units), jnp.bfloat16)
    for k in range(CHIPS):
        piece = moved if k == 0 else send(moved, lambda s, c, p: (s, c, p ^ k))
        gathered = lax.dynamic_update_slice(
            gathered, piece[None], (jnp.bitwise_xor(jnp.bitwise_xor(band, chip), k), 0, 0)
        )
    half = units // CORES
    mine = lax.dynamic_slice_in_dim(gathered, core * half, half, 2)
    theirs = swap_cores(lax.dynamic_slice_in_dim(gathered, (1 - core) * half, half, 2))
    cols = in_core_order(core, mine[:, None], theirs[:, None], 1).reshape(total, half)
    grad_gram = contract_rows(all_rows, cols) / total
    return (input_gram, grad_gram)


def solution(mesh):
    placed = (P("tok", None), P("tok", None), P("tok", "tp"), P("tp", "tok"))
    return jax.shard_map(
        shards,
        mesh=mesh,
        in_specs=placed,
        out_specs=(P("tok", "tp"), P("tp", "tok")),
        check_vma=False,
    )
```

time: 418 us -> 306 us (0.73)
  waiting for transfers between devices: 296 us -> 112 us
  starting transfers between devices: 5.58 us -> 101 us
  blocking collectives: 59.2 us -> 0 us
  other arithmetic: 2.37 us -> 24.1 us
  local copies, waits for them, and re-layouts: 11.9 us -> 17.7 us
    all_gather x3 -> x2, waiting for transfers between devices: 156 us -> 0.02 us  [the longest x1 0.02 us: shards(): band_rows = lax.all_gather(own_band, 'tok', axis=0, tiled=True)]
    reduce_scatter x2 -> x0, waiting for transfers between devices: 139 us -> none  [the longest x1 84.9 us: shards(): lax.psum_scatter(contract_cols(rows, down_weight), 'tok', scatter_dimensi...]
    ppermute x0 -> x16, starting transfers between devices: none -> 78.2 us  [send(): return lax.ppermute(value, AXES, routes(move))]
    all_to_all x1 -> x4, waiting for transfers between devices: 0.01 us -> 77.6 us  [exchange(): lax.all_to_all(value, 'tok', split_axis, 0, axis_index_groups=SAME_CORE,...]
    all_to_all x2 -> x0, blocking collectives: 59.2 us -> none  [the longest x1 31.5 us: shards(): lax.all_to_all(output_grad, 'tok', split_axis=1, concat_axis=0, tiled=True)]
    ppermute x0 -> x16, waiting for transfers between devices: none -> 34.5 us  [send(): return lax.ppermute(value, AXES, routes(move))]
    all_to_all x1 -> x4, starting transfers between devices: 5.37 us -> 22.8 us  [exchange(): lax.all_to_all(value, 'tok', split_axis, 0, axis_index_groups=SAME_CORE,...]
    select_n x0 -> x4, other arithmetic: none -> 8.77 us  [in_core_order(): first = jnp.where(core == 0, own, other)]
  transfers between devices with their start and end apart: 6 -> 22, of which waited for: 5 -> 10; matrix products, arithmetic and copies ran while one was open for 5% -> 18% of each run, Pallas kernels for 0% -> 0%
where the time goes in v1:
time: 306 us; the launch traced here: 304 us
  waiting for transfers between devices  112 us (37%)
  starting transfers between devices  101 us (33%)
  matrix products  31.8 us (10%)
  other arithmetic  24.1 us (8%)
  local copies, waits for them, and re-layouts  17.7 us (6%)
  between operations  16.8 us (5%)
    ppermute x16, starting transfers between devices, send(): return lax.ppermute(value, AXES, routes(move))  78.2 us
    all_to_all x4, waiting for transfers between devices, exchange(): lax.all_to_all(value, 'tok', split_axis, 0, axis_index_groups=SAME_CORE,...  77.6 us
    ppermute x16, waiting for transfers between devices, send(): return lax.ppermute(value, AXES, routes(move))  34.5 us
    all_to_all x4, starting transfers between devices, exchange(): lax.all_to_all(value, 'tok', split_axis, 0, axis_index_groups=SAME_CORE,...  22.8 us
    dot_general x2, matrix products, contract_rows(): lax.dot_general(left, right, (((0,), (0,)), ((), ())), preferred_element_...  17 us
    unnamed x20, local copies, waits for them, and re-layouts  10.3 us
    select_n x4, other arithmetic, in_core_order(): first = jnp.where(core == 0, own, other)  8.77 us
    dot_general x1, matrix products, contract_cols(): lax.dot_general(left, right, (((1,), (1,)), ((), ())), preferred_element_...  7.78 us
  transfers between devices with their start and end apart: 22, of which 10 were waited for; matrix products, arithmetic and copies ran while one was open for 18% of the time, Pallas kernels for 0%

profile of v1, /device:TPU:1, one launch (start us, length us, event | category | flops | bytes accessed | tf_op | source)
XLA Modules:
  0.0 303.9 jit_solution(12728922811808352698)
XLA Ops:
  7.2 1.5 collective-permute-start.2
  8.7 2.8 copy.54
  11.5 5.1 %all-to-all-start = ((bf16[96,8,1024]{2,0,1:T(8,128)(2,1)}), bf16[96,8,1024]{2,0,1:T(8,128)(2,1)S(1)}, u32[]{:S(2)}, u32[]{:S(2)}) async-start(bf16[96,8,1024]{2,0,1:T(8,128)(2,1)} %bitcast.83), calls=%async_computation | async-start | bytes 3145728 | tf_op jit(solution)/shard_map/all_to_all | solution.py:47
  16.9 1.3 copy.53
  18.2 19.9 %all-to-all-done = bf16[96,8,1024]{2,0,1:T(8,128)(2,1)S(1)} async-done(((bf16[96,8,1024]{2,0,1:T(8,128)(2,1)}), bf16[96,8,1024]{2,0,1:T(8,128)(2,1)S(1)}, u32[]{:S(2)}, u32[]{:S(2)}) %all-to-all-start) | async-done | bytes 1572896 | tf_op jit(solution)/shard_map/all_to_all | solution.py:47
  38.1 4.6 %all-to-all-start.1 = ((bf16[96,8,1024]{2,0,1:T(8,128)(2,1)}), bf16[96,8,1024]{2,0,1:T(8,128)(2,1)S(1)}, u32[]{:S(2)}, u32[]{:S(2)}) async-start(bf16[96,8,1024]{2,0,1:T(8,128)(2,1)} %bitcast.82), calls=%async_computation.1 | async-start | bytes 3145728 | tf_op jit(solution)/shard_map/all_to_all | solution.py:47
  43.1 2.5 broadcast_select_fusion.1
  45.7 1.3 copy-done.4
  47.6 1.4 abs_reduce_fusion.1
  49.7 2.5 broadcast_select_fusion.3
  52.3 1.3 copy-done.2
  54.3 1.1 abs_reduce_fusion
  56.0 1.5 collective-permute-start.3
  57.5 2.7 collective-permute-done.3
  60.3 2.7 collective-permute-start.4
  63.0 1.5 collective-permute-done.4
  64.5 1.2 collective-permute-start.5
  65.7 1.2 collective-permute-done.5
  68.2 7.0 %multiply_convert_fusion = f16[2048,768]{0,1:T(8,128)(2,1)} fusion(bf16[768,1024]{1,0:T(8,128)(2,1)S(1)} %bitcast.74, f32[768]{0:T(1024)S(1)} %div.50, bf16[512,2048]{1,0:T(8,128)(2,1)} %copy-done.5, bf16[512,2048]{1,0:T(8,128)(2,1)} %copy-done.4), kind=kOutput, calls=%fused_computation.1 | convolution fusion | flops 3232759808 | bytes 8915968 | tf_op jit(solution)/shard_map/dot_general | solution.py:90
  75.2 1.2 copy-done.8
  76.5 4.7 %all-to-all-start.3 = ((f16[8,96,2048]{2,1,0:T(8,128)(2,1)}), f16[8,96,2048]{2,1,0:T(8,128)(2,1)}, u32[]{:S(2)}, u32[]{:S(2)}) async-start(f16[8,96,2048]{2,1,0:T(8,128)(2,1)} %bitcast.86), calls=%async_computation.3 | async-start | bytes 6291456 | tf_op jit(solution)/shard_map/all_to_all | solution.py:47
  82.0 1.8 fusion
  84.4 7.8 %multiply_convert_fusion.1 = f16[2048,768]{0,1:T(8,128)(2,1)} fusion(bf16[768,1024]{1,0:T(8,128)(2,1)} %bitcast.81, f32[768]{0:T(1024)S(1)} %div.48, bf16[2048,512]{1,0:T(8,128)(2,1)} %copy-done.3, bf16[2048,512]{1,0:T(8,128)(2,1)} %copy-done.2), kind=kOutput, calls=%fused_computation.3 | convolution fusion | flops 3232759808 | bytes 8915968 | tf_op jit(solution)/shard_map/dot_general | solution.py:20
  92.2 27.3 %all-to-all-done.3 = f16[8,96,2048]{2,1,0:T(8,128)(2,1)} async-done(((f16[8,96,2048]{2,1,0:T(8,128)(2,1)}), f16[8,96,2048]{2,1,0:T(8,128)(2,1)}, u32[]{:S(2)}, u32[]{:S(2)}) %all-to-all-start.3) | async-done | bytes 3145760 | tf_op jit(solution)/shard_map/all_to_all | solution.py:47
  119.6 8.4 %all-to-all-start.2 = ((f16[8,96,2048]{2,1,0:T(8,128)(2,1)}), f16[8,96,2048]{2,1,0:T(8,128)(2,1)}, u32[]{:S(2)}, u32[]{:S(2)}) async-start(f16[8,96,2048]{2,1,0:T(8,128)(2,1)} %bitcast.87), calls=%async_computation.2 | async-start | bytes 6291456 | tf_op jit(solution)/shard_map/all_to_all | solution.py:47
  128.2 1.0 copy.50
  129.6 2.4 copy.49
  133.7 2.7 multiply_reduce_fusion
  136.4 30.4 %all-to-all-done.2 = f16[8,96,2048]{2,1,0:T(8,128)(2,1)} async-done(((f16[8,96,2048]{2,1,0:T(8,128)(2,1)}), f16[8,96,2048]{2,1,0:T(8,128)(2,1)}, u32[]{:S(2)}, u32[]{:S(2)}) %all-to-all-start.2) | async-done | bytes 3145760 | tf_op jit(solution)/shard_map/all_to_all | solution.py:47
  166.7 2.6 multiply_reduce_fusion.1
  170.4 1.7 collective-permute-start.6
  173.7 2.7 collective-permute-start
  176.4 37.7 %collective-permute-start.8 = (bf16[96,2048]{1,0:T(8,128)(2,1)S(1)}, bf16[96,2048]{1,0:T(8,128)(2,1)S(1)}, u32[]{:S(2)}, u32[]{:S(2)}) collective-permute-start(bf16[96,2048]{1,0:T(8,128)(2,1)S(1)} %collective-permute-done.7), channel_id=1, source_target_pairs={{0,1},{1,0},{2,3},{3,2},{4,5},{5,4},{6,7},{7,6},{8,9},{9,8},{10,11... | collective-permute-start | bytes 1179656 | tf_op jit(solution)/shard_map/ppermute | solution.py:36
  214.1 1.2 collective-permute-start.10
  215.3 5.8 %collective-permute-start.11 = (bf16[96,2048]{1,0:T(8,128)(2,1)S(1)}, bf16[96,2048]{1,0:T(8,128)(2,1)S(1)}, u32[]{:S(2)}, u32[]{:S(2)}) collective-permute-start(bf16[96,2048]{1,0:T(8,128)(2,1)S(1)} %collective-permute-done.7), channel_id=1, source_target_pairs={{0,4},{1,5},{2,6},{3,7},{4,0},{5,1},{6,2},{7,3},{8,12},{9,13},{10,... | collective-permute-start | bytes 1179656 | tf_op jit(solution)/shard_map/ppermute | solution.py:36
  221.5 8.9 %collective-permute-done.8 = bf16[96,2048]{1,0:T(8,128)(2,1)S(1)} collective-permute-done((bf16[96,2048]{1,0:T(8,128)(2,1)S(1)}, bf16[96,2048]{1,0:T(8,128)(2,1)S(1)}, u32[]{:S(2)}, u32[]{:S(2)}) %collective-permute-start.8) | collective-permute-done | bytes 393248 | tf_op jit(solution)/shard_map/ppermute | solution.py:36
  230.4 7.4 %collective-permute-start.12 = (bf16[96,2048]{1,0:T(8,128)(2,1)S(1)}, bf16[96,2048]{1,0:T(8,128)(2,1)S(1)}, u32[]{:S(2)}, u32[]{:S(2)}) collective-permute-start(bf16[96,2048]{1,0:T(8,128)(2,1)S(1)} %collective-permute-done.7), channel_id=1, source_target_pairs={{0,5},{1,4},{2,7},{3,6},{4,1},{5,0},{6,3},{7,2},{8,13},{9,12},{10,... | collective-permute-start | bytes 1179656 | tf_op jit(solution)/shard_map/ppermute | solution.py:36
  238.0 1.5 collective-permute-done.10
  239.4 12.7 %collective-permute-start.14 = (bf16[96,2048]{1,0:T(8,128)(2,1)S(1)}, bf16[96,2048]{1,0:T(8,128)(2,1)S(1)}, u32[]{:S(2)}, u32[]{:S(2)}) collective-permute-start(bf16[96,2048]{1,0:T(8,128)(2,1)S(1)} %collective-permute-done.7), channel_id=1, source_target_pairs={{0,7},{1,6},{2,5},{3,4},{4,3},{5,2},{6,1},{7,0},{8,15},{9,14},{10,... | collective-permute-start | bytes 1179656 | tf_op jit(solution)/shard_map/ppermute | solution.py:36
  252.2 9.4 %collective-permute-done.12 = bf16[96,2048]{1,0:T(8,128)(2,1)S(1)} collective-permute-done((bf16[96,2048]{1,0:T(8,128)(2,1)S(1)}, bf16[96,2048]{1,0:T(8,128)(2,1)S(1)}, u32[]{:S(2)}, u32[]{:S(2)}) %collective-permute-start.12) | collective-permute-done | bytes 393248 | tf_op jit(solution)/shard_map/ppermute | solution.py:36
  261.7 9.3 %collective-permute-done.14 = bf16[96,2048]{1,0:T(8,128)(2,1)S(1)} collective-permute-done((bf16[96,2048]{1,0:T(8,128)(2,1)S(1)}, bf16[96,2048]{1,0:T(8,128)(2,1)S(1)}, u32[]{:S(2)}, u32[]{:S(2)}) %collective-permute-start.14) | collective-permute-done | bytes 393248 | tf_op jit(solution)/shard_map/ppermute | solution.py:36
  271.1 1.7 copy-done
  272.8 1.2 collective-permute-start.15
  274.0 1.5 broadcast_select_fusion.5
  275.7 5.2 %convolution_multiply_fusion.1 = f32[512,1024]{1,0:T(8,128)} fusion(bf16[1536,512]{1,0:T(8,128)(2,1)S(1)} %bitcast.91, bf16[1536,1024]{1,0:T(8,128)(2,1)} %all-gather.3.cloned.1.call-done), kind=kOutput, calls=%fused_computation.14 | convolution fusion | flops 1611137024 | bytes 6815744 | tf_op jit(solution)/shard_map/dot_general | solution.py:14
  280.9 2.3 select_bitcast_fusion.1
  283.2 2.0 pad_maximum_fusion.2
  285.2 11.8 %convolution_multiply_fusion = f32[2048,1024]{1,0:T(8,128)} fusion(bf16[1536,2048]{1,0:T(8,128)(2,1)} %all-gather.5.cloned.1.call-done, bf16[1536,1024]{1,0:T(8,128)(2,1)} %bitcast.88), kind=kOutput, calls=%fused_computation.4 | convolution fusion | flops 6444548096 | bytes 17825792 | tf_op jit(solution)/shard_map/dot_general | solution.py:14
  (64 shorter events, 9.8 us)
Async XLA Ops:
  7.2 36.0 %collective-permute-start.2 = (bf16[512,2048]{1,0:T(8,128)(2,1)}, bf16[512,2048]{1,0:T(8,128)(2,1)}, u32[]{:S(2)}, u32[]{:S(2)}) collective-permute-start(bf16[512,2048]{1,0:T(8,128)(2,1)} %param.6), channel_id=1, source_target_pairs={{0,8},{1,9},{2,10},{3,11},{4,12},{5,13},{6,14},{7,15},{8,0},{9,1},... | collective-permute-start | bytes 6291464 | tf_op jit(solution)/shard_map/ppermute | solution.py:36
  8.7 8.3 %copy-start.7 = (bf16[96,8192]{1,0:T(8,128)(2,1)S(1)}, bf16[96,8192]{1,0:T(8,128)(2,1)}, u32[]{:S(2)}) copy-start(bf16[96,8192]{1,0:T(8,128)(2,1)} %param.5) | copy-start | bytes 4718596
  11.5 26.6 %all-to-all-start = ((bf16[96,8,1024]{2,0,1:T(8,128)(2,1)}), bf16[96,8,1024]{2,0,1:T(8,128)(2,1)S(1)}, u32[]{:S(2)}, u32[]{:S(2)}) async-start(bf16[96,8,1024]{2,0,1:T(8,128)(2,1)} %bitcast.83), calls=%async_computation | async-start | bytes 3145728 | tf_op jit(solution)/shard_map/all_to_all | solution.py:47
  16.6 33.1 %collective-permute-start.1 = (bf16[2048,512]{1,0:T(8,128)(2,1)}, bf16[2048,512]{1,0:T(8,128)(2,1)}, u32[]{:S(2)}, u32[]{:S(2)}) collective-permute-start(bf16[2048,512]{1,0:T(8,128)(2,1)} %param.7), channel_id=1, source_target_pairs={{0,8},{1,9},{2,10},{3,11},{4,12},{5,13},{6,14},{7,15},{8,0},{9,1},... | collective-permute-start | bytes 6291464 | tf_op jit(solution)/shard_map/ppermute | solution.py:36
  38.1 37.1 %all-to-all-start.1 = ((bf16[96,8,1024]{2,0,1:T(8,128)(2,1)}), bf16[96,8,1024]{2,0,1:T(8,128)(2,1)S(1)}, u32[]{:S(2)}, u32[]{:S(2)}) async-start(bf16[96,8,1024]{2,0,1:T(8,128)(2,1)} %bitcast.82), calls=%async_computation.1 | async-start | bytes 3145728 | tf_op jit(solution)/shard_map/all_to_all | solution.py:47
  45.6 1.3 copy-start.4
  45.6 2.0 copy-start.5
  52.2 1.3 copy-start.2
  52.3 2.0 copy-start.3
  56.0 4.2 %collective-permute-start.3 = (f32[2]{0:T(128)S(1)}, f32[2]{0:T(128)S(1)}, u32[]{:S(2)}, u32[]{:S(2)}) collective-permute-start(f32[2]{0:T(128)S(1)} %pad_maximum_fusion.6), channel_id=1, source_target_pairs={{0,16},{1,17},{2,18},{3,19},{4,20},{5,21},{6,22},{7,23},{8,24},{9,... | collective-permute-start | bytes 32 | tf_op jit(solution)/shard_map/ppermute | solution.py:36
  60.3 4.2 %collective-permute-start.4 = (f32[2]{0:T(128)S(1)}, f32[2]{0:T(128)S(1)}, u32[]{:S(2)}, u32[]{:S(2)}) collective-permute-start(f32[2]{0:T(128)S(1)} %fusion.11), channel_id=1, source_target_pairs={{0,32},{1,33},{2,34},{3,35},{4,36},{5,37},{6,38},{7,39},{8,40},{9,... | collective-permute-start | bytes 32 | tf_op jit(solution)/shard_map/ppermute | solution.py:36
  64.5 2.4 collective-permute-start.5
  75.2 1.2 copy-start.8
  76.5 4.8 %copy-start.6 = (bf16[96,8192]{1,0:T(8,128)(2,1)S(1)}, bf16[96,8192]{1,0:T(8,128)(2,1)}, u32[]{:S(2)}) copy-start(bf16[96,8192]{1,0:T(8,128)(2,1)} %param.4) | copy-start | bytes 4718596
  76.5 43.1 %all-to-all-start.3 = ((f16[8,96,2048]{2,1,0:T(8,128)(2,1)}), f16[8,96,2048]{2,1,0:T(8,128)(2,1)}, u32[]{:S(2)}, u32[]{:S(2)}) async-start(f16[8,96,2048]{2,1,0:T(8,128)(2,1)} %bitcast.86), calls=%async_computation.3 | async-start | bytes 6291456 | tf_op jit(solution)/shard_map/all_to_all | solution.py:47
  81.2 194.5 %all-gather.3.cloned.1.call-start = ((), (), s32[]{:S(2)}) async-start(), calls=%async_computation.4 | async-start | bytes 3342336 | tf_op jit(solution)/shard_map/all_gather | solution.py:104
  119.6 47.2 %all-to-all-start.2 = ((f16[8,96,2048]{2,1,0:T(8,128)(2,1)}), f16[8,96,2048]{2,1,0:T(8,128)(2,1)}, u32[]{:S(2)}, u32[]{:S(2)}) async-start(f16[8,96,2048]{2,1,0:T(8,128)(2,1)} %bitcast.87), calls=%async_computation.2 | async-start | bytes 6291456 | tf_op jit(solution)/shard_map/all_to_all | solution.py:47
  128.0 157.2 %all-gather.5.cloned.1.call-start = ((), (), s32[]{:S(2)}) async-start(), calls=%async_computation.5 | async-start | bytes 6684672 | tf_op jit(solution)/shard_map/all_gather | solution.py:114
  170.4 1.7 collective-permute-start.6
  172.0 4.4 %collective-permute-start.7 = (bf16[96,2048]{1,0:T(8,128)(2,1)S(1)}, bf16[96,2048]{1,0:T(8,128)(2,1)S(1)}, u32[]{:S(2)}, u32[]{:S(2)}) collective-permute-start(bf16[96,2048]{1,0:T(8,128)(2,1)S(1)} %collective-permute-done.6), channel_id=1, source_target_pairs={{0,0},{1,17},{2,34},{3,51},{4,68},{5,85},{6,102},{7,119},{8,8},{9,... | collective-permute-start | bytes 1179656 | tf_op jit(solution)/shard_map/ppermute | solution.py:36
  173.7 100.3 %collective-permute-start = (bf16[768,512]{1,0:T(8,128)(2,1)}, bf16[768,512]{1,0:T(8,128)(2,1)}, u32[]{:S(2)}, u32[]{:S(2)}) collective-permute-start(bf16[768,512]{1,0:T(8,128)(2,1)} %constant_dynamic-slice_fusion.2), channel_id=1, source_target_pairs={{0,8},{1,9},{2,10},{3,11},{4,12},{5,13},{6,14},{7,15},{8,0},{9,1},... | collective-permute-start | bytes 2359304 | tf_op jit(solution)/shard_map/ppermute | solution.py:36
  176.4 54.0 %collective-permute-start.8 = (bf16[96,2048]{1,0:T(8,128)(2,1)S(1)}, bf16[96,2048]{1,0:T(8,128)(2,1)S(1)}, u32[]{:S(2)}, u32[]{:S(2)}) collective-permute-start(bf16[96,2048]{1,0:T(8,128)(2,1)S(1)} %collective-permute-done.7), channel_id=1, source_target_pairs={{0,1},{1,0},{2,3},{3,2},{4,5},{5,4},{6,7},{7,6},{8,9},{9,8},{10,11... | collective-permute-start | bytes 1179656 | tf_op jit(solution)/shard_map/ppermute | solution.py:36
  214.1 23.7 %collective-permute-start.9 = (bf16[96,2048]{1,0:T(8,128)(2,1)S(1)}, bf16[96,2048]{1,0:T(8,128)(2,1)S(1)}, u32[]{:S(2)}, u32[]{:S(2)}) collective-permute-start(bf16[96,2048]{1,0:T(8,128)(2,1)S(1)} %collective-permute-done.7), channel_id=1, source_target_pairs={{0,2},{1,3},{2,0},{3,1},{4,6},{5,7},{6,4},{7,5},{8,10},{9,11},{10,... | collective-permute-start | bytes 1179656 | tf_op jit(solution)/shard_map/ppermute | solution.py:36
  214.1 25.3 %collective-permute-start.10 = (bf16[96,2048]{1,0:T(8,128)(2,1)S(1)}, bf16[96,2048]{1,0:T(8,128)(2,1)S(1)}, u32[]{:S(2)}, u32[]{:S(2)}) collective-permute-start(bf16[96,2048]{1,0:T(8,128)(2,1)S(1)} %collective-permute-done.7), channel_id=1, source_target_pairs={{0,3},{1,2},{2,1},{3,0},{4,7},{5,6},{6,5},{7,4},{8,11},{9,10},{10,... | collective-permute-start | bytes 1179656 | tf_op jit(solution)/shard_map/ppermute | solution.py:36
  215.3 36.9 %collective-permute-start.11 = (bf16[96,2048]{1,0:T(8,128)(2,1)S(1)}, bf16[96,2048]{1,0:T(8,128)(2,1)S(1)}, u32[]{:S(2)}, u32[]{:S(2)}) collective-permute-start(bf16[96,2048]{1,0:T(8,128)(2,1)S(1)} %collective-permute-done.7), channel_id=1, source_target_pairs={{0,4},{1,5},{2,6},{3,7},{4,0},{5,1},{6,2},{7,3},{8,12},{9,13},{10,... | collective-permute-start | bytes 1179656 | tf_op jit(solution)/shard_map/ppermute | solution.py:36
  230.4 31.2 %collective-permute-start.12 = (bf16[96,2048]{1,0:T(8,128)(2,1)S(1)}, bf16[96,2048]{1,0:T(8,128)(2,1)S(1)}, u32[]{:S(2)}, u32[]{:S(2)}) collective-permute-start(bf16[96,2048]{1,0:T(8,128)(2,1)S(1)} %collective-permute-done.7), channel_id=1, source_target_pairs={{0,5},{1,4},{2,7},{3,6},{4,1},{5,0},{6,3},{7,2},{8,13},{9,12},{10,... | collective-permute-start | bytes 1179656 | tf_op jit(solution)/shard_map/ppermute | solution.py:36
  237.8 23.9 %collective-permute-start.13 = (bf16[96,2048]{1,0:T(8,128)(2,1)S(1)}, bf16[96,2048]{1,0:T(8,128)(2,1)S(1)}, u32[]{:S(2)}, u32[]{:S(2)}) collective-permute-start(bf16[96,2048]{1,0:T(8,128)(2,1)S(1)} %collective-permute-done.7), channel_id=1, source_target_pairs={{0,6},{1,7},{2,4},{3,5},{4,2},{5,3},{6,0},{7,1},{8,14},{9,15},{10,... | collective-permute-start | bytes 1179656 | tf_op jit(solution)/shard_map/ppermute | solution.py:36
  239.4 31.6 %collective-permute-start.14 = (bf16[96,2048]{1,0:T(8,128)(2,1)S(1)}, bf16[96,2048]{1,0:T(8,128)(2,1)S(1)}, u32[]{:S(2)}, u32[]{:S(2)}) collective-permute-start(bf16[96,2048]{1,0:T(8,128)(2,1)S(1)} %collective-permute-done.7), channel_id=1, source_target_pairs={{0,7},{1,6},{2,5},{3,4},{4,3},{5,2},{6,1},{7,0},{8,15},{9,14},{10,... | collective-permute-start | bytes 1179656 | tf_op jit(solution)/shard_map/ppermute | solution.py:36
  271.0 1.7 copy-start
  272.8 8.1 %collective-permute-start.15 = (bf16[8,96,1024]{2,1,0:T(8,128)(2,1)S(1)}, bf16[8,96,1024]{2,1,0:T(8,128)(2,1)}, u32[]{:S(2)}, u32[]{:S(2)}) collective-permute-start(bf16[8,96,1024]{2,1,0:T(8,128)(2,1)S(1)} %constant_dynamic-slice_fusion), channel_id=1, source_target_pairs={{0,8},{1,9},{2,10},{3,11},{4,12},{5,13},{6,14},{7,15},{8,0},{9,1},... | collective-permute-start | bytes 4718600 | tf_op jit(solution)/shard_map/ppermute | solution.py:36
  275.7 5.2 %copy-start.1 = (bf16[8,96,2048]{2,1,0:T(8,128)(2,1)S(1)}, bf16[8,96,2048]{2,1,0:T(8,128)(2,1)}, u32[]{:S(2)}) copy-start(bf16[8,96,2048]{2,1,0:T(8,128)(2,1)} %copy-done) | copy-start | bytes 9437188
Sparse Core Ops, SparseCore 0:
  83.7 59.6 all-gather.2
  170.5 63.6 all-gather.4

commit v2 on v0

v2 whole, which is shorter than its diff:
```python
import functools

import jax
import jax.numpy as jnp
from jax import lax
from jax.experimental import pallas as pl
from jax.experimental.pallas import tpu as pltpu
from jax.sharding import PartitionSpec as P

AXES = ("tok", "tp")
YL, X, CORE, Z, YH = 2, 4, 2, 4, 2
LANES = 128
LN2 = 0.6931471805599453
TINY = 1e-30


def contract_rows(left, right):
    return lax.dot_general(
        left, right, (((0,), (0,)), ((), ())), preferred_element_type=jnp.float32
    )


def contract_cols(left, right):
    return lax.dot_general(
        left, right, (((1,), (1,)), ((), ())), preferred_element_type=jnp.float32
    )


def index_of(yl, x, c, z, yh):
    return ((yl * X + x) * CORE + c) * (Z * YH) + z * YH + yh


def send(value, move):
    pairs = [
        (index_of(yl, x, c, z, yh), index_of(*move(yl, x, c, z, yh)))
        for yl in range(YL)
        for x in range(X)
        for c in range(CORE)
        for z in range(Z)
        for yh in range(YH)
    ]
    return lax.ppermute(value, AXES, pairs)


def over_core(value):
    return send(value, lambda yl, x, c, z, yh: (yl, x, 1 - c, z, yh))


def over_yl(value):
    return send(value, lambda yl, x, c, z, yh: (1 - yl, x, c, z, yh))


def over_other_y(value):
    return send(value, lambda yl, x, c, z, yh: (1 - yl, x, c, z, 1 - yh))


def over_yh(value):
    return send(value, lambda yl, x, c, z, yh: (yl, x, c, z, 1 - yh))


def over_x(value, k):
    return send(value, lambda yl, x, c, z, yh: (yl, x ^ k, c, z, yh))


def over_z(value, k):
    return send(value, lambda yl, x, c, z, yh: (yl, x, c, z ^ k, yh))


def turn_tp(yl, x, c, z, yh):
    p = (z * YH + yh) ^ (c * X + x)
    return yl, x, c, p // YH, p % YH


def turn_tok(yl, x, c, z, yh):
    s = (z * YH + yh) ^ (c * X + x)
    return s // X, s % X, yl, z, yh


def part(value, index, count, axis):
    size = value.shape[axis] // count
    return lax.dynamic_slice_in_dim(value, index * size, size, axis)


def after(value, *others):
    return lax.optimization_barrier((value, *others))[0]


def scaled_kernel(contract, count, *refs):
    fields, weights, out_ref = refs[:count], refs[count:-1], refs[-1]
    size = weights[0].shape[1 if contract else 0]
    units = out_ref.shape[1] - LANES
    tile = 256
    blocks = [(field, i * size) for field in fields for i in range(field.shape[1] // size)]

    def step(n, top):
        columns = pl.ds(pl.multiple_of(n * tile, tile), tile)
        total = None
        for (field, start), weight in zip(blocks, weights):
            block = weight[columns, :] if contract else weight[:, columns]
            term = lax.dot_general(
                field[:, start : start + size],
                block,
                (((1,), (1 if contract else 0,)), ((), ())),
                preferred_element_type=jnp.float32,
            )
            total = term if total is None else total + term
        out_ref[:, columns] = total
        for i in range(tile // LANES):
            top = jnp.maximum(top, jnp.abs(total[:, i * LANES : (i + 1) * LANES]))
        return top

    top = lax.fori_loop(
        0, units // tile, step, jnp.zeros((out_ref.shape[0], LANES), jnp.float32)
    )
    top = jnp.maximum(jnp.max(top, axis=1, keepdims=True), TINY)
    exponent = jnp.floor(14.0 - jnp.log(top) / LN2)
    out_ref[:, :units] *= jnp.exp(exponent * LN2)
    out_ref[:, units:] = jnp.broadcast_to(exponent, (out_ref.shape[0], LANES))


def scaled_product(fields, weights, contract):
    units = weights[0].shape[0 if contract else 1]
    rows = fields[0].shape[0]
    depth = sum(weight.shape[1 if contract else 0] for weight in weights)
    vmem = pl.BlockSpec(memory_space=pltpu.VMEM)
    return pl.pallas_call(
        functools.partial(scaled_kernel, contract, len(fields)),
        out_shape=jax.ShapeDtypeStruct((rows, units + LANES), jnp.float32),
        in_specs=[vmem] * (len(fields) + len(weights)),
        out_specs=vmem,
        compiler_params=pltpu.CompilerParams(vmem_limit_bytes=32 * 2**20),
        cost_estimate=pl.CostEstimate(
            flops=2 * rows * depth * units,
            bytes_accessed=2 * depth * (rows + units) + 4 * rows * units,
            transcendentals=0,
        ),
        name="scaled_product",
    )(*fields, *weights)


def gram_kernel(scale, places, left00, left01, left10, left11, *refs):
    pieces, out_ref, right, sems = refs[:-3], refs[-3], refs[-2], refs[-1]
    b = pl.program_id(0)

    @pl.when((b == 0) & (pl.program_id(1) == 0))
    def _():
        copies = []
        for i, piece in enumerate(pieces):
            for j in range(YH):
                slot = i * YH + j
                copies.append(
                    pltpu.make_async_copy(piece.at[j], right.at[places[slot]], sems.at[slot])
                )
        for copy in copies:
            copy.start()
        for copy in copies:
            copy.wait()

    def tokens(left):
        block = left[...]
        return block.reshape(block.shape[0] * block.shape[2], block.shape[3])

    for which, order in ((0, (left00, left01, left10, left11)), (1, (left10, left11, left00, left01))):

        @pl.when(b == which)
        def _():
            block = jnp.concatenate([tokens(left) for left in order], 0)
            rows = right[...]
            rows = rows.reshape(rows.shape[0] * rows.shape[1], rows.shape[2])
            out_ref[...] = contract_rows(block, rows) * scale


def grad_gram_of(lefts, pieces, places, yl, total):
    _, _, rows, units = lefts[0].shape
    tile = 256
    tiles = units // tile
    block = pl.BlockSpec((X, 1, rows, tile), lambda b, n, *_: (0, b, 0, n))
    slots = YL * CORE * X
    return pl.pallas_call(
        functools.partial(gram_kernel, 1.0 / total),
        out_shape=jax.ShapeDtypeStruct((YL * units, units), jnp.float32),
        grid_spec=pltpu.PrefetchScalarGridSpec(
            num_scalar_prefetch=1,
            grid=(YL, tiles),
            in_specs=[block] * 4 + [pl.BlockSpec(memory_space=pl.ANY)] * len(pieces),
            out_specs=pl.BlockSpec(
                (tile, units), lambda b, n, places: ((places[slots] ^ b) * tiles + n, 0)
            ),
            scratch_shapes=[
                pltpu.VMEM((slots, rows, units), jnp.bfloat16),
                pltpu.SemaphoreType.DMA((slots,)),
            ],
        ),
        compiler_params=pltpu.CompilerParams(vmem_limit_bytes=40 * 2**20),
        cost_estimate=pl.CostEstimate(
            flops=2 * total * YL * units * units,
            bytes_accessed=6 * total * units + 8 * units * units,
            transcendentals=0,
        ),
        name="grad_gram",
    )(places, *lefts, *pieces)


def shards(layer_input, output_grad, gate_weight, down_weight):
    rows, model = layer_input.shape
    total = rows * YL * X * CORE
    place, band = lax.axis_index("tok"), lax.axis_index("tp")
    chip, c = place // CORE, place % CORE
    yl, x = chip // X, chip % X
    width = model // (YL * X)
    half = width // CORE

    def cut(field, *more):
        return [
            jnp.concatenate(
                [
                    part(field, (((yl ^ b) * X + (x ^ k)) * CORE + (c ^ d)), YL * X * CORE, 1)
                    for d in range(CORE)
                    for b in range(YL)
                ]
                + list(more),
                1,
            )
            for k in range(X)
        ]

    def swapped(pieces):
        return [pieces[1], pieces[0], pieces[3], pieces[2]]

    def halved(parts):
        parts = [part.astype(jnp.float16).reshape(X, rows, -1) for part in parts]
        return jnp.concatenate(parts, 2) if len(parts) > 1 else parts[0]

    def exchanged(parts):
        return [parts[0]] + [over_x(parts[k], k) for k in range(1, X)]

    def summed(pieces):
        total_sum = None
        for piece in pieces:
            piece = piece.astype(jnp.float32)
            term = piece[:, :-LANES] * jnp.exp(piece[:, -LANES : 1 - LANES] * -LN2)
            total_sum = term if total_sum is None else total_sum + term
        return total_sum

    def activated(gate, hidden):
        return (hidden * (gate / (1.0 + jnp.exp(-gate)))).astype(jnp.bfloat16)

    def round_x(both):
        return jnp.stack([both if k == 0 else over_x(both, k) for k in range(X)])

    gate_near = part(gate_weight, yl, YL, 1)
    gate_across = over_yl(part(gate_weight, 1 - yl, YL, 1))
    input_cut = cut(layer_input)
    input_first = over_other_y(input_cut[0])
    pieces = [over_x(input_cut[k], k) for k in range(1, X)]
    own_band = part(layer_input, band, YL * X, 1)
    grad_cut = cut(output_grad, own_band)
    gate_across, input_first, pieces, grad_cut = lax.optimization_barrier(
        (gate_across, input_first, pieces, grad_cut)
    )
    gate_other = over_core(jnp.stack([gate_near, gate_across]))
    input_rest = over_other_y(jnp.concatenate(pieces, 0))
    input_own = jnp.concatenate([input_cut[0]] + pieces, 0)
    grad_pieces = [over_x(grad_cut[k], k) for k in range(1, X)]

    gate_pieces = [gate_near, gate_across, gate_other[0], gate_other[1]]
    gate_part = halved([scaled_product([input_own], gate_pieces, False)])
    down_near = part(down_weight, yl, YL, 0)
    down_across = over_yl(after(part(down_weight, 1 - yl, YL, 0), gate_other))
    grad_pieces, input_first, input_rest = after(
        (grad_pieces, input_first, input_rest), gate_part
    )
    gate_sent = exchanged(after(gate_part, *grad_pieces))
    grad_both = jnp.concatenate([grad_cut[0]] + grad_pieces, 0)
    split = 3 * half
    near = over_yl(after(grad_both[:, split:], gate_part))
    far = over_other_y(after(grad_both[:, :split], input_rest))
    input_other = jnp.concatenate([input_first, input_rest], 0)
    gate_part = scaled_product([input_other], swapped(gate_pieces), False)

    down_across = after(down_across, gate_part)
    down_other = over_core(jnp.stack([down_near, down_across]))
    down_pieces = [down_near, down_across, down_other[0], down_other[1]]
    gate = summed(after(gate_sent, gate_part))
    hidden_part = scaled_product([after(grad_both, gate)], down_pieces, True)
    mixed_sent = exchanged(halved([hidden_part, gate_part]))
    near, far = after([near, far], hidden_part)
    hidden_part = halved([scaled_product([far, near], swapped(down_pieces), True)])
    hidden_sent = exchanged(hidden_part)
    mixed_sent = after(mixed_sent, hidden_part)
    cuts = mixed_sent[0].shape[1] // 2
    first = activated(gate, summed([piece[:, :cuts] for piece in mixed_sent]))
    gate = summed([piece[:, cuts:] for piece in mixed_sent])
    moved = send(first, turn_tp)
    both = jnp.stack([first, over_yl(first)])
    moved, both, hidden_sent = lax.optimization_barrier((moved, both, hidden_sent))
    first_round = round_x(both)
    second = activated(gate, summed(hidden_sent))
    moved = send(moved, turn_tok)
    pair = jnp.stack([moved, over_yh(moved)])
    first_turned = [pair] + [over_z(pair, k) for k in range(1, Z)]
    both = jnp.stack([second, over_yl(second)])
    moved = send(send(second, turn_tp), turn_tok)
    pair = jnp.stack([moved, over_yh(moved)])
    second_turned = [pair] + [over_z(pair, k) for k in range(1, Z)]
    second_round = round_x(after(both, *first_turned))
    first_gathered = [first_round, over_core(after(first_round, pair))]
    second_gathered = [second_round, over_core(second_round)]

    bands = jnp.stack([grad_both[:, YL * width :], near[:, half:]])
    mine = jnp.stack([input_own[:, :half], input_other[:, half : 2 * half]])
    theirs = jnp.stack([input_own[:, 2 * half : 3 * half], input_other[:, 3 * half :]])
    across = over_core(after(jnp.concatenate([theirs, bands], 2), first))
    left = jnp.stack([mine, across[:, :, :half]]).reshape(total, half)
    right = jnp.stack([bands, across[:, :, half:]]).reshape(total, width)
    input_gram = contract_rows(left, right) / total

    turn = band ^ chip ^ (c * X + x)
    places = [
        (yl ^ c ^ h) * (CORE * X) + (turn ^ j) for h in range(YL) for j in range(Z * YH)
    ]
    grad_gram = grad_gram_of(
        first_gathered + second_gathered,
        first_turned + after(second_turned, input_gram),
        jnp.stack(places + [yl]).astype(jnp.int32),
        yl,
        total,
    )

    return (input_gram, grad_gram)


def solution(mesh):
    placed = (P("tok", None), P("tok", None), P("tok", "tp"), P("tp", "tok"))
    return jax.shard_map(
        shards,
        mesh=mesh,
        in_specs=placed,
        out_specs=(P("tok", "tp"), P("tp", "tok")),
        check_vma=False,
    )
```

time: 418 us -> 258 us (0.62)
  waiting for transfers between devices: 296 us -> 95.2 us
  starting transfers between devices: 5.58 us -> 94.4 us
  blocking collectives: 59.2 us -> 0 us
  Pallas kernels: 0 us -> 27.6 us
  matrix products: 29.1 us -> 3.13 us
  between operations: 13.8 us -> 1.75 us
  other arithmetic: 2.37 us -> 14.1 us
  local copies, waits for them, and re-layouts: 11.9 us -> 21.2 us
    all_gather x3 -> x0, waiting for transfers between devices: 156 us -> none  [the longest x1 62.3 us: shards(): all_units = lax.all_gather(up_grad, 'tp', axis=1, tiled=True)]
    reduce_scatter x2 -> x0, waiting for transfers between devices: 139 us -> none  [the longest x1 84.9 us: shards(): lax.psum_scatter(contract_cols(rows, down_weight), 'tok', scatter_dimensi...]
    ppermute x0 -> x46, waiting for transfers between devices: none -> 95.2 us  [send(): return lax.ppermute(value, AXES, pairs)]
    ppermute x0 -> x46, starting transfers between devices: none -> 94.4 us  [send(): return lax.ppermute(value, AXES, pairs)]
    all_to_all x2 -> x0, blocking collectives: 59.2 us -> none  [the longest x1 31.5 us: shards(): lax.all_to_all(output_grad, 'tok', split_axis=1, concat_axis=0, tiled=True)]
    pallas_call x0 -> x5, Pallas kernels: none -> 27.6 us  [the longest x1 17.2 us: grad_gram_of(): pl.pallas_call(functools.partial(gram_kernel, 1.0 / total), out_shape=jax...]
    dot_general x2 -> x1, matrix products: 16.1 us -> 3.13 us  [contract_rows(): lax.dot_general(left, right, (((0,), (0,)), ((), ())), preferred_element_...]
    dot_general x2 -> x0, matrix products: 12.9 us -> none  [the longest x1 6.53 us: contract_cols(): lax.dot_general(left, right, (((1,), (1,)), ((), ())), preferred_element_...]
  transfers between devices with their start and end apart: 6 -> 46, of which waited for: 5 -> 19; matrix products, arithmetic and copies ran while one was open for 5% -> 13% of each run, Pallas kernels for 0% -> 4%
where the time goes in v2:
time: 258 us; the launch traced here: 257 us
  waiting for transfers between devices  95.2 us (37%)
  starting transfers between devices  94.4 us (37%)
  Pallas kernels  27.6 us (11%)
  local copies, waits for them, and re-layouts  21.2 us (8%)
  other arithmetic  14.1 us (5%)
  matrix products  3.13 us (1%)
    ppermute x46, waiting for transfers between devices, send(): return lax.ppermute(value, AXES, pairs)  95.2 us
    ppermute x46, starting transfers between devices, send(): return lax.ppermute(value, AXES, pairs)  94.4 us
    pallas_call x1, Pallas kernels, grad_gram_of(): pl.pallas_call(functools.partial(gram_kernel, 1.0 / total), out_shape=jax...  17.2 us
    pallas_call x4, Pallas kernels, scaled_product(): pl.pallas_call(functools.partial(scaled_kernel, contract, len(fields)), o...  10.5 us
    unnamed x68, local copies, waits for them, and re-layouts  9.86 us
  transfers between devices with their start and end apart: 46, of which 19 were waited for; matrix products, arithmetic and copies ran while one was open for 13% of the time, Pallas kernels for 4%

profile of v2, /device:TPU:1, one launch (start us, length us, event | category | flops | bytes accessed | tf_op | source)
XLA Modules:
  0.0 257.5 jit_solution(10132991347911721993)
XLA Ops:
  0.8 2.5 constant_dynamic-slice_fusion.6
  4.2 3.6 %collective-permute-start.1 = (bf16[96,2048]{1,0:T(8,128)(2,1)}, bf16[96,2048]{1,0:T(8,128)(2,1)}, u32[]{:S(2)}, u32[]{:S(2)}) collective-permute-start(bf16[96,2048]{1,0:T(8,128)(2,1)} %pad_maximum_fusion.7), channel_id=1, source_target_pairs={{0,65},{1,64},{2,67},{3,66},{4,69},{5,68},{6,71},{7,70},{8,73},{9,... | collective-permute-start | bytes 1179656 | tf_op jit(solution)/shard_map/ppermute | solution.py:42
  12.0 2.5 collective-permute-start.3
  17.0 1.8 dynamic-slice_dynamic-update-slice_fusion.5
  18.8 1.8 dynamic-slice_dynamic-update-slice_fusion.4
  20.6 1.9 dynamic-slice_dynamic-update-slice_fusion
  22.5 6.7 %collective-permute-done.3 = bf16[96,2048]{1,0:T(8,128)(2,1)S(1)} collective-permute-done((bf16[96,2048]{1,0:T(8,128)(2,1)}, bf16[96,2048]{1,0:T(8,128)(2,1)S(1)}, u32[]{:S(2)}, u32[]{:S(2)}) %collective-permute-start.3) | collective-permute-done | bytes 393248 | tf_op jit(solution)/shard_map/ppermute | solution.py:42
  29.2 5.2 %collective-permute-done.4 = bf16[96,2048]{1,0:T(8,128)(2,1)S(1)} collective-permute-done((bf16[96,2048]{1,0:T(8,128)(2,1)}, bf16[96,2048]{1,0:T(8,128)(2,1)S(1)}, u32[]{:S(2)}, u32[]{:S(2)}) %collective-permute-start.4) | collective-permute-done | bytes 393248 | tf_op jit(solution)/shard_map/ppermute | solution.py:42
  35.0 2.2 collective-permute-start.9
  38.4 2.2 pad_maximum_fusion.2.refs_0_
  41.0 2.7 %collective-permute-start.6 = (bf16[96,3072]{1,0:T(8,128)(2,1)}, bf16[96,3072]{1,0:T(8,128)(2,1)S(1)}, u32[]{:S(2)}, u32[]{:S(2)}) collective-permute-start(bf16[96,3072]{1,0:T(8,128)(2,1)} %get-tuple-element.49), channel_id=1, source_target_pairs={{0,32},{1,33},{2,34},{3,35},{4,36},{5,37},{6,38},{7,39},{8,40},{9,... | collective-permute-start | bytes 1769480 | tf_op jit(solution)/shard_map/ppermute | solution.py:42
  47.7 2.6 %scaled_product.4 = f32[384,1152]{1,0:T(8,128)S(1)} custom-call(bf16[384,2048]{1,0:T(8,128)(2,1)S(1)} %pad_maximum_fusion.2.refs_0_, bf16[512,1024]{1,0:T(8,128)(2,1)S(1)} %get-tuple-element.96.refs_1_.refs_2_, bf16[512,1024]{1,0:T(8,128)(2,1)S(1)} %collective-permute-done.refs_2_.refs_1_, bf16[512,1024]{1,0:T(8,128)(2,1)S(1)} %get-tuple-element.95.refs_3_.refs_4_, ...), custom_call_target="tpu_custom_call" | custom-call | flops 1610612736 | bytes 7340032 | tf_op jit(solution)/shard_map/scaled_product/pallas_call | solution.py:126
  50.4 4.0 %collective-permute-done.5 = bf16[96,3072]{1,0:T(8,128)(2,1)S(1)} collective-permute-done((bf16[96,3072]{1,0:T(8,128)(2,1)}, bf16[96,3072]{1,0:T(8,128)(2,1)S(1)}, u32[]{:S(2)}, u32[]{:S(2)}) %collective-permute-start.5) | collective-permute-done | bytes 589856 | tf_op jit(solution)/shard_map/ppermute | solution.py:42
  54.5 14.2 %collective-permute-done.6 = bf16[96,3072]{1,0:T(8,128)(2,1)S(1)} collective-permute-done((bf16[96,3072]{1,0:T(8,128)(2,1)}, bf16[96,3072]{1,0:T(8,128)(2,1)S(1)}, u32[]{:S(2)}, u32[]{:S(2)}) %collective-permute-start.6) | collective-permute-done | bytes 589856 | tf_op jit(solution)/shard_map/ppermute | solution.py:42
  68.7 2.1 collective-permute-done.7
  71.8 2.4 collective-permute-start.12
  75.4 2.6 %scaled_product.5 = f32[384,1152]{1,0:T(8,128)S(1)} custom-call(bf16[384,2048]{1,0:T(8,128)(2,1)S(1)} %constant_dynamic-update-slice_fusion.refs_0_, bf16[512,1024]{1,0:T(8,128)(2,1)S(1)} %collective-permute-done.refs_2_.refs_1_, bf16[512,1024]{1,0:T(8,128)(2,1)S(1)} %get-tuple-element.96.refs_1_.refs_2_, ...), custom_call_target="tpu_custom_call" | custom-call | flops 1610612736 | bytes 7340032 | tf_op jit(solution)/shard_map/scaled_product/pallas_call | solution.py:126
  78.3 3.7 %collective-permute-start.16 = (bf16[2,1024,512]{2,1,0:T(8,128)(2,1)S(1)}, bf16[2,1024,512]{2,1,0:T(8,128)(2,1)S(1)}, u32[]{:S(2)}, u32[]{:S(2)}) collective-permute-start(bf16[2,1024,512]{2,1,0:T(8,128)(2,1)S(1)} %pad_maximum_fusion.1), channel_id=1, source_target_pairs={{0,8},{1,9},{2,10},{3,11},{4,12},{5,13},{6,14},{7,15},{8,0},{9,1},... | collective-permute-start | bytes 6291464 | tf_op jit(solution)/shard_map/ppermute | solution.py:42
  83.4 2.5 collective-permute-start.11
  86.7 2.6 %scaled_product.6 = f32[384,1152]{1,0:T(8,128)S(1)} custom-call(bf16[384,3072]{1,0:T(8,128)(2,1)S(1)} %constant_dynamic-update-slice_fusion.2.refs_0_, bf16[1024,512]{1,0:T(8,128)(2,1)S(1)} %get-tuple-element.93.refs_1_.refs_3_, bf16[1024,512]{1,0:T(8,128)(2,1)S(1)} %collective-permute-done.15.refs_2_, ...), custom_call_target="tpu_custom_call" | custom-call | flops 1610612736 | bytes 7340032 | tf_op jit(solution)/shard_map/scaled_product/pallas_call | solution.py:126
  91.2 2.6 %collective-permute-start.18 = (f16[96,2304]{1,0:T(8,128)(2,1)S(1)}, f16[96,2304]{1,0:T(8,128)(2,1)S(1)}, u32[]{:S(2)}, u32[]{:S(2)}) collective-permute-start(f16[96,2304]{1,0:T(8,128)(2,1)S(1)} %get-tuple-element.101), channel_id=1, source_target_pairs={{0,32},{1,33},{2,34},{3,35},{4,36},{5,37},{6,38},{7,39},{8,40},{9,... | collective-permute-start | bytes 1327112 | tf_op jit(solution)/shard_map/ppermute | solution.py:42
  93.8 16.2 %collective-permute-done.10.refs_1_ = bf16[384,1536]{1,0:T(8,128)(2,1)S(1)} collective-permute-done((bf16[384,1536]{1,0:T(8,128)(2,1)S(1)}, bf16[384,1536]{1,0:T(8,128)(2,1)S(1)}, u32[]{:S(2)}, u32[]{:S(2)}) %collective-permute-start.10) | collective-permute-done | bytes 1179680 | tf_op jit(solution)/shard_map/ppermute | solution.py:42
  111.3 2.6 %scaled_product.7 = f32[384,1152]{1,0:T(8,128)S(1)} custom-call(bf16[384,1536]{1,0:T(8,128)(2,1)S(1)} %collective-permute-done.11.refs_0_, bf16[384,1536]{1,0:T(8,128)(2,1)S(1)} %collective-permute-done.10.refs_1_, bf16[1024,512]{1,0:T(8,128)(2,1)S(1)} %collective-permute-done.15.refs_2_, bf16[1024,512]{1,0:T(8,128)(2,1)S(1)} %get-tuple-element.93.refs_1_.refs_3_, ...), custom_call_target="tpu_custom_call" | custom-call | flops 1610612736 | bytes 7340032 | tf_op jit(solution)/shard_map/scaled_product/pallas_call | solution.py:126
  114.2 2.5 collective-permute-start.25
  116.9 1.6 maximum_maximum_fusion
  122.0 5.5 %collective-permute-start.21 = (bf16[96,1024]{1,0:T(8,128)(2,1)S(1)}, bf16[96,1024]{1,0:T(8,128)(2,1)S(1)}, u32[]{:S(2)}, u32[]{:S(2)}) collective-permute-start(bf16[96,1024]{1,0:T(8,128)(2,1)S(1)} %fusion.26), channel_id=1, source_target_pairs={{0,0},{1,1},{2,2},{3,3},{4,4},{5,5},{6,6},{7,7},{8,12},{9,13},{10,... | collective-permute-start | bytes 589832 | tf_op jit(solution)/shard_map/ppermute | solution.py:42
  128.7 1.8 collective-permute-done.21
  130.6 1.9 collective-permute-start.34
  132.9 4.7 %collective-permute-done.34 = bf16[96,1024]{1,0:T(8,128)(2,1)S(1)} collective-permute-done((bf16[96,1024]{1,0:T(8,128)(2,1)S(1)}, bf16[96,1024]{1,0:T(8,128)(2,1)S(1)}, u32[]{:S(2)}, u32[]{:S(2)}) %collective-permute-start.34) | collective-permute-done | bytes 196640 | tf_op jit(solution)/shard_map/ppermute | solution.py:42
  137.5 6.2 %collective-permute-start.35 = (bf16[96,1024]{1,0:T(8,128)(2,1)S(1)}, bf16[96,1024]{1,0:T(8,128)(2,1)S(1)}, u32[]{:S(2)}, u32[]{:S(2)}) collective-permute-start(bf16[96,1024]{1,0:T(8,128)(2,1)S(1)} %collective-permute-done.34), channel_id=1, source_target_pairs={{0,1},{1,0},{2,3},{3,2},{4,5},{5,4},{6,7},{7,6},{8,9},{9,8},{10,11... | collective-permute-start | bytes 589832 | tf_op jit(solution)/shard_map/ppermute | solution.py:42
  144.0 5.1 %collective-permute-done.35 = bf16[96,1024]{1,0:T(8,128)(2,1)S(1)} collective-permute-done((bf16[96,1024]{1,0:T(8,128)(2,1)S(1)}, bf16[96,1024]{1,0:T(8,128)(2,1)S(1)}, u32[]{:S(2)}, u32[]{:S(2)}) %collective-permute-start.35) | collective-permute-done | bytes 196640 | tf_op jit(solution)/shard_map/ppermute | solution.py:42
  149.2 3.8 %collective-permute-start.38 = (bf16[2,96,1024]{2,1,0:T(8,128)(2,1)S(1)}, bf16[2,96,1024]{2,1,0:T(8,128)(2,1)S(1)}, u32[]{:S(2)}, u32[]{:S(2)}) collective-permute-start(bf16[2,96,1024]{2,1,0:T(8,128)(2,1)S(1)} %pad_maximum_fusion.14.refs_0_), channel_id=1, source_target_pairs={{0,6},{1,7},{2,4},{3,5},{4,2},{5,3},{6,0},{7,1},{8,14},{9,15},{10,... | collective-permute-start | bytes 1179656 | tf_op jit(solution)/shard_map/ppermute | solution.py:42
  153.4 4.9 %collective-permute-start.29 = (bf16[96,1024]{1,0:T(8,128)(2,1)S(1)}, bf16[96,1024]{1,0:T(8,128)(2,1)S(1)}, u32[]{:S(2)}, u32[]{:S(2)}) collective-permute-start(bf16[96,1024]{1,0:T(8,128)(2,1)S(1)} %fusion.21), channel_id=1, source_target_pairs={{0,0},{1,1},{2,2},{3,3},{4,4},{5,5},{6,6},{7,7},{8,12},{9,13},{10,... | collective-permute-start | bytes 589832 | tf_op jit(solution)/shard_map/ppermute | solution.py:42
  159.0 8.6 %collective-permute-done.29 = bf16[96,1024]{1,0:T(8,128)(2,1)S(1)} collective-permute-done((bf16[96,1024]{1,0:T(8,128)(2,1)S(1)}, bf16[96,1024]{1,0:T(8,128)(2,1)S(1)}, u32[]{:S(2)}, u32[]{:S(2)}) %collective-permute-start.29) | collective-permute-done | bytes 196640 | tf_op jit(solution)/shard_map/ppermute | solution.py:42
  169.1 2.7 %collective-permute-done.38.refs_3_ = bf16[2,96,1024]{2,1,0:T(8,128)(2,1)S(1)} collective-permute-done((bf16[2,96,1024]{2,1,0:T(8,128)(2,1)S(1)}, bf16[2,96,1024]{2,1,0:T(8,128)(2,1)S(1)}, u32[]{:S(2)}, u32[]{:S(2)}) %collective-permute-start.38) | collective-permute-done | bytes 393248 | tf_op jit(solution)/shard_map/ppermute | solution.py:42
  171.9 1.9 collective-permute-start.27
  173.8 2.2 collective-permute-start.26
  176.8 4.0 %collective-permute-start.30 = (bf16[96,1024]{1,0:T(8,128)(2,1)S(1)}, bf16[96,1024]{1,0:T(8,128)(2,1)S(1)}, u32[]{:S(2)}, u32[]{:S(2)}) collective-permute-start(bf16[96,1024]{1,0:T(8,128)(2,1)S(1)} %collective-permute-done.29), channel_id=1, source_target_pairs={{0,0},{1,17},{2,34},{3,51},{4,68},{5,85},{6,102},{7,119},{8,64},{9... | collective-permute-start | bytes 589832 | tf_op jit(solution)/shard_map/ppermute | solution.py:42
  180.8 6.6 %collective-permute-done.28 = bf16[2,96,1024]{2,1,0:T(8,128)(2,1)S(1)} collective-permute-done((bf16[2,96,1024]{2,1,0:T(8,128)(2,1)S(1)}, bf16[2,96,1024]{2,1,0:T(8,128)(2,1)S(1)}, u32[]{:S(2)}, u32[]{:S(2)}) %collective-permute-start.28) | collective-permute-done | bytes 393248 | tf_op jit(solution)/shard_map/ppermute | solution.py:42
  187.4 4.4 %collective-permute-start.40 = (bf16[2,96,1024]{2,1,0:T(8,128)(2,1)S(1)}, bf16[2,96,1024]{2,1,0:T(8,128)(2,1)S(1)}, u32[]{:S(2)}, u32[]{:S(2)}) collective-permute-start(bf16[2,96,1024]{2,1,0:T(8,128)(2,1)S(1)} %pad_maximum_fusion.13), channel_id=1, source_target_pairs={{0,32},{1,33},{2,34},{3,35},{4,36},{5,37},{6,38},{7,39},{8,40},{9,... | collective-permute-start | bytes 1179656 | tf_op jit(solution)/shard_map/ppermute | solution.py:42
  192.7 9.4 %collective-permute-start.31 = (bf16[96,1024]{1,0:T(8,128)(2,1)S(1)}, bf16[96,1024]{1,0:T(8,128)(2,1)S(1)}, u32[]{:S(2)}, u32[]{:S(2)}) collective-permute-start(bf16[96,1024]{1,0:T(8,128)(2,1)S(1)} %collective-permute-done.30), channel_id=1, source_target_pairs={{0,1},{1,0},{2,3},{3,2},{4,5},{5,4},{6,7},{7,6},{8,9},{9,8},{10,11... | collective-permute-start | bytes 589832 | tf_op jit(solution)/shard_map/ppermute | solution.py:42
  202.3 3.3 %collective-permute-done.31 = bf16[96,1024]{1,0:T(8,128)(2,1)S(1)} collective-permute-done((bf16[96,1024]{1,0:T(8,128)(2,1)S(1)}, bf16[96,1024]{1,0:T(8,128)(2,1)S(1)}, u32[]{:S(2)}, u32[]{:S(2)}) %collective-permute-start.31) | collective-permute-done | bytes 196640 | tf_op jit(solution)/shard_map/ppermute | solution.py:42
  206.4 2.4 collective-permute-start.32
  209.1 2.5 collective-permute-start.42
  214.3 7.5 %collective-permute-start.45 = (bf16[2,96,1024]{2,1,0:T(8,128)(2,1)S(1)}, bf16[2,96,1024]{2,1,0:T(8,128)(2,1)S(1)}, u32[]{:S(2)}, u32[]{:S(2)}) collective-permute-start(bf16[2,96,1024]{2,1,0:T(8,128)(2,1)S(1)} %copy-done), channel_id=1, source_target_pairs={{0,6},{1,7},{2,4},{3,5},{4,2},{5,3},{6,0},{7,1},{8,14},{9,15},{10,... | collective-permute-start | bytes 1179656 | tf_op jit(solution)/shard_map/ppermute | solution.py:42
  225.2 3.1 %bitcast_multiply_fusion = f32[512,1024]{1,0:T(8,128)} fusion(bf16[1,2,384,1024]{3,2,1,0:T(8,128)(2,1)S(1)} %slice_bitcast_fusion, bf16[1,2,384,1024]{3,2,1,0:T(8,128)(2,1)S(1)} %maximum_bitcast_fusion, bf16[1,2,384,512]{3,2,1,0:T(8,128)(2,1)S(1)} %slice_bitcast_fusion.5, bf16[1,2,384,512]{3,2,1,0:T(8,128)(2,1)S(1)} %maximum_bitcast_fusion.1), kind=kOutput, calls=%fused_computation.13 | convolution fusion | flops 1613496320 | bytes 6815744 | tf_op jit(solution)/shard_map/dot_general | solution.py:18
  228.3 11.4 %collective-permute-done.45.refs_7_ = bf16[2,96,1024]{2,1,0:T(8,128)(2,1)S(1)} collective-permute-done((bf16[2,96,1024]{2,1,0:T(8,128)(2,1)S(1)}, bf16[2,96,1024]{2,1,0:T(8,128)(2,1)S(1)}, u32[]{:S(2)}, u32[]{:S(2)}) %collective-permute-start.45) | collective-permute-done | bytes 393248 | tf_op jit(solution)/shard_map/ppermute | solution.py:42
  240.2 17.2 %grad_gram.1 = f32[2048,1024]{1,0:T(8,128)} custom-call(s32[17]{0:T(128)S(1)} %stack.221.places, bf16[4,2,96,1024]{3,2,1,0:T(8,128)(2,1)S(1)} %pad_maximum_fusion.3.left00, bf16[4,2,96,1024]{3,2,1,0:T(8,128)(2,1)} %collective-permute-done.32.left01, bf16[4,2,96,1024]{3,2,1,0:T(8,128)(2,1)S(1)} %pad_maximum_fusion.4.left10, ...), custom_call_target="tpu_custom_call" | custom-call | flops 6442450944 | bytes 17825792 | tf_op jit(solution)/shard_map/grad_gram/pallas_call | solution.py:179
  (187 shorter events, 39.2 us)
Async XLA Ops:
  4.2 18.3 %collective-permute-start.1 = (bf16[96,2048]{1,0:T(8,128)(2,1)}, bf16[96,2048]{1,0:T(8,128)(2,1)}, u32[]{:S(2)}, u32[]{:S(2)}) collective-permute-start(bf16[96,2048]{1,0:T(8,128)(2,1)} %pad_maximum_fusion.7), channel_id=1, source_target_pairs={{0,65},{1,64},{2,67},{3,66},{4,69},{5,68},{6,71},{7,70},{8,73},{9,... | collective-permute-start | bytes 1179656 | tf_op jit(solution)/shard_map/ppermute | solution.py:42
  8.6 13.9 %collective-permute-start.2 = (bf16[96,2048]{1,0:T(8,128)(2,1)}, bf16[96,2048]{1,0:T(8,128)(2,1)S(1)}, u32[]{:S(2)}, u32[]{:S(2)}) collective-permute-start(bf16[96,2048]{1,0:T(8,128)(2,1)} %pad_maximum_fusion.8), channel_id=1, source_target_pairs={{0,16},{1,17},{2,18},{3,19},{4,20},{5,21},{6,22},{7,23},{8,24},{9,... | collective-permute-start | bytes 1179656 | tf_op jit(solution)/shard_map/ppermute | solution.py:42
  11.1 23.6 %collective-permute-start = (bf16[512,1024]{1,0:T(8,128)(2,1)}, bf16[512,1024]{1,0:T(8,128)(2,1)S(1)}, u32[]{:S(2)}, u32[]{:S(2)}) collective-permute-start(bf16[512,1024]{1,0:T(8,128)(2,1)} %get-tuple-element.97), channel_id=1, source_target_pairs={{0,64},{1,65},{2,66},{3,67},{4,68},{5,69},{6,70},{7,71},{8,72},{9,... | collective-permute-start | bytes 3145736 | tf_op jit(solution)/shard_map/ppermute | solution.py:42
  12.0 17.2 %collective-permute-start.3 = (bf16[96,2048]{1,0:T(8,128)(2,1)}, bf16[96,2048]{1,0:T(8,128)(2,1)S(1)}, u32[]{:S(2)}, u32[]{:S(2)}) collective-permute-start(bf16[96,2048]{1,0:T(8,128)(2,1)} %pad_maximum_fusion.9), channel_id=1, source_target_pairs={{0,32},{1,33},{2,34},{3,35},{4,36},{5,37},{6,38},{7,39},{8,40},{9,... | collective-permute-start | bytes 1179656 | tf_op jit(solution)/shard_map/ppermute | solution.py:42
  15.2 19.2 %collective-permute-start.4 = (bf16[96,2048]{1,0:T(8,128)(2,1)}, bf16[96,2048]{1,0:T(8,128)(2,1)S(1)}, u32[]{:S(2)}, u32[]{:S(2)}) collective-permute-start(bf16[96,2048]{1,0:T(8,128)(2,1)} %pad_maximum_fusion.10), channel_id=1, source_target_pairs={{0,48},{1,49},{2,50},{3,51},{4,52},{5,53},{6,54},{7,55},{8,56},{9,... | collective-permute-start | bytes 1179656 | tf_op jit(solution)/shard_map/ppermute | solution.py:42
  35.0 11.6 %collective-permute-start.9 = (bf16[2,512,1024]{2,1,0:T(8,128)(2,1)S(1)}, bf16[2,512,1024]{2,1,0:T(8,128)(2,1)S(1)}, u32[]{:S(2)}, u32[]{:S(2)}) collective-permute-start(bf16[2,512,1024]{2,1,0:T(8,128)(2,1)S(1)} %pad_maximum_fusion), channel_id=1, source_target_pairs={{0,8},{1,9},{2,10},{3,11},{4,12},{5,13},{6,14},{7,15},{8,0},{9,1},... | collective-permute-start | bytes 6291464 | tf_op jit(solution)/shard_map/ppermute | solution.py:42
  37.5 33.3 %collective-permute-start.8 = (bf16[288,2048]{1,0:T(8,128)(2,1)S(1)}, bf16[288,2048]{1,0:T(8,128)(2,1)S(1)}, u32[]{:S(2)}, u32[]{:S(2)}) collective-permute-start(bf16[288,2048]{1,0:T(8,128)(2,1)S(1)} %pad_maximum_fusion.5), channel_id=1, source_target_pairs={{0,65},{1,64},{2,67},{3,66},{4,69},{5,68},{6,71},{7,70},{8,73},{9,... | collective-permute-start | bytes 3538952 | tf_op jit(solution)/shard_map/ppermute | solution.py:42
  40.7 13.8 %collective-permute-start.5 = (bf16[96,3072]{1,0:T(8,128)(2,1)}, bf16[96,3072]{1,0:T(8,128)(2,1)S(1)}, u32[]{:S(2)}, u32[]{:S(2)}) collective-permute-start(bf16[96,3072]{1,0:T(8,128)(2,1)} %get-tuple-element.48), channel_id=1, source_target_pairs={{0,16},{1,17},{2,18},{3,19},{4,20},{5,21},{6,22},{7,23},{8,24},{9,... | collective-permute-start | bytes 1769480 | tf_op jit(solution)/shard_map/ppermute | solution.py:42
  41.0 27.7 %collective-permute-start.6 = (bf16[96,3072]{1,0:T(8,128)(2,1)}, bf16[96,3072]{1,0:T(8,128)(2,1)S(1)}, u32[]{:S(2)}, u32[]{:S(2)}) collective-permute-start(bf16[96,3072]{1,0:T(8,128)(2,1)} %get-tuple-element.49), channel_id=1, source_target_pairs={{0,32},{1,33},{2,34},{3,35},{4,36},{5,37},{6,38},{7,39},{8,40},{9,... | collective-permute-start | bytes 1769480 | tf_op jit(solution)/shard_map/ppermute | solution.py:42
  43.7 27.0 %collective-permute-start.7 = (bf16[96,3072]{1,0:T(8,128)(2,1)}, bf16[96,3072]{1,0:T(8,128)(2,1)S(1)}, u32[]{:S(2)}, u32[]{:S(2)}) collective-permute-start(bf16[96,3072]{1,0:T(8,128)(2,1)} %get-tuple-element.50), channel_id=1, source_target_pairs={{0,48},{1,49},{2,50},{3,51},{4,52},{5,53},{6,54},{7,55},{8,56},{9,... | collective-permute-start | bytes 1769480 | tf_op jit(solution)/shard_map/ppermute | solution.py:42
  46.5 31.6 %collective-permute-start.15 = (bf16[1024,512]{1,0:T(8,128)(2,1)S(1)}, bf16[1024,512]{1,0:T(8,128)(2,1)S(1)}, u32[]{:S(2)}, u32[]{:S(2)}) collective-permute-start(bf16[1024,512]{1,0:T(8,128)(2,1)S(1)} %get-tuple-element.67), channel_id=1, source_target_pairs={{0,64},{1,65},{2,66},{3,67},{4,68},{5,69},{6,70},{7,71},{8,72},{9,... | collective-permute-start | bytes 3145736 | tf_op jit(solution)/shard_map/ppermute | solution.py:42
  70.9 12.5 %collective-permute-start.14 = (f16[96,1152]{1,0:T(8,128)(2,1)S(1)}, f16[96,1152]{1,0:T(8,128)(2,1)S(1)}, u32[]{:S(2)}, u32[]{:S(2)}) collective-permute-start(f16[96,1152]{1,0:T(8,128)(2,1)S(1)} %get-tuple-element.146), channel_id=1, source_target_pairs={{0,48},{1,49},{2,50},{3,51},{4,52},{5,53},{6,54},{7,55},{8,56},{9,... | collective-permute-start | bytes 663560 | tf_op jit(solution)/shard_map/ppermute | solution.py:42
  71.8 14.1 %collective-permute-start.13 = (f16[96,1152]{1,0:T(8,128)(2,1)S(1)}, f16[96,1152]{1,0:T(8,128)(2,1)S(1)}, u32[]{:S(2)}, u32[]{:S(2)}) collective-permute-start(f16[96,1152]{1,0:T(8,128)(2,1)S(1)} %get-tuple-element.147), channel_id=1, source_target_pairs={{0,32},{1,33},{2,34},{3,35},{4,36},{5,37},{6,38},{7,39},{8,40},{9,... | collective-permute-start | bytes 663560 | tf_op jit(solution)/shard_map/ppermute | solution.py:42
  71.8 14.1 %collective-permute-start.12 = (f16[96,1152]{1,0:T(8,128)(2,1)S(1)}, f16[96,1152]{1,0:T(8,128)(2,1)S(1)}, u32[]{:S(2)}, u32[]{:S(2)}) collective-permute-start(f16[96,1152]{1,0:T(8,128)(2,1)S(1)} %get-tuple-element.148), channel_id=1, source_target_pairs={{0,16},{1,17},{2,18},{3,19},{4,20},{5,21},{6,22},{7,23},{8,24},{9,... | collective-permute-start | bytes 663560 | tf_op jit(solution)/shard_map/ppermute | solution.py:42
  78.3 8.2 %collective-permute-start.16 = (bf16[2,1024,512]{2,1,0:T(8,128)(2,1)S(1)}, bf16[2,1024,512]{2,1,0:T(8,128)(2,1)S(1)}, u32[]{:S(2)}, u32[]{:S(2)}) collective-permute-start(bf16[2,1024,512]{2,1,0:T(8,128)(2,1)S(1)} %pad_maximum_fusion.1), channel_id=1, source_target_pairs={{0,8},{1,9},{2,10},{3,11},{4,12},{5,13},{6,14},{7,15},{8,0},{9,1},... | collective-permute-start | bytes 6291464 | tf_op jit(solution)/shard_map/ppermute | solution.py:42
  82.3 27.7 %collective-permute-start.10 = (bf16[384,1536]{1,0:T(8,128)(2,1)S(1)}, bf16[384,1536]{1,0:T(8,128)(2,1)S(1)}, u32[]{:S(2)}, u32[]{:S(2)}) collective-permute-start(bf16[384,1536]{1,0:T(8,128)(2,1)S(1)} %get-tuple-element.59), channel_id=1, source_target_pairs={{0,64},{1,65},{2,66},{3,67},{4,68},{5,69},{6,70},{7,71},{8,72},{9,... | collective-permute-start | bytes 3538952 | tf_op jit(solution)/shard_map/ppermute | solution.py:42
  82.5 34.4 %copy-start.7 = (bf16[1,384,1024]{2,1,0:T(8,128)(2,1)}, bf16[1,384,1024]{2,1,0:T(8,128)(2,1)S(1)}, u32[]{:S(2)}) copy-start(bf16[1,384,1024]{2,1,0:T(8,128)(2,1)S(1)} %slice_bitcast_fusion.6) | copy-start | bytes 2359300
  83.4 27.9 %collective-permute-start.11 = (bf16[384,1536]{1,0:T(8,128)(2,1)S(1)}, bf16[384,1536]{1,0:T(8,128)(2,1)S(1)}, u32[]{:S(2)}, u32[]{:S(2)}) collective-permute-start(bf16[384,1536]{1,0:T(8,128)(2,1)S(1)} %get-tuple-element.60), channel_id=1, source_target_pairs={{0,65},{1,64},{2,67},{3,66},{4,69},{5,68},{6,71},{7,70},{8,73},{9,... | collective-permute-start | bytes 3538952 | tf_op jit(solution)/shard_map/ppermute | solution.py:42
  89.9 28.6 %collective-permute-start.19 = (f16[96,2304]{1,0:T(8,128)(2,1)S(1)}, f16[96,2304]{1,0:T(8,128)(2,1)S(1)}, u32[]{:S(2)}, u32[]{:S(2)}) collective-permute-start(f16[96,2304]{1,0:T(8,128)(2,1)S(1)} %get-tuple-element.98), channel_id=1, source_target_pairs={{0,48},{1,49},{2,50},{3,51},{4,52},{5,53},{6,54},{7,55},{8,56},{9,... | collective-permute-start | bytes 1327112 | tf_op jit(solution)/shard_map/ppermute | solution.py:42
  91.2 28.1 %collective-permute-start.17 = (f16[96,2304]{1,0:T(8,128)(2,1)S(1)}, f16[96,2304]{1,0:T(8,128)(2,1)S(1)}, u32[]{:S(2)}, u32[]{:S(2)}) collective-permute-start(f16[96,2304]{1,0:T(8,128)(2,1)S(1)} %get-tuple-element.100), channel_id=1, source_target_pairs={{0,16},{1,17},{2,18},{3,19},{4,20},{5,21},{6,22},{7,23},{8,24},{9,... | collective-permute-start | bytes 1327112 | tf_op jit(solution)/shard_map/ppermute | solution.py:42
  91.2 28.1 %collective-permute-start.18 = (f16[96,2304]{1,0:T(8,128)(2,1)S(1)}, f16[96,2304]{1,0:T(8,128)(2,1)S(1)}, u32[]{:S(2)}, u32[]{:S(2)}) collective-permute-start(f16[96,2304]{1,0:T(8,128)(2,1)S(1)} %get-tuple-element.101), channel_id=1, source_target_pairs={{0,32},{1,33},{2,34},{3,35},{4,36},{5,37},{6,38},{7,39},{8,40},{9,... | collective-permute-start | bytes 1327112 | tf_op jit(solution)/shard_map/ppermute | solution.py:42
  114.2 14.5 %collective-permute-start.25 = (f16[96,1152]{1,0:T(8,128)(2,1)S(1)}, f16[96,1152]{1,0:T(8,128)(2,1)S(1)}, u32[]{:S(2)}, u32[]{:S(2)}) collective-permute-start(f16[96,1152]{1,0:T(8,128)(2,1)S(1)} %get-tuple-element.142), channel_id=1, source_target_pairs={{0,48},{1,49},{2,50},{3,51},{4,52},{5,53},{6,54},{7,55},{8,56},{9,... | collective-permute-start | bytes 663560 | tf_op jit(solution)/shard_map/ppermute | solution.py:42
  116.7 12.0 %collective-permute-start.24 = (f16[96,1152]{1,0:T(8,128)(2,1)S(1)}, f16[96,1152]{1,0:T(8,128)(2,1)S(1)}, u32[]{:S(2)}, u32[]{:S(2)}) collective-permute-start(f16[96,1152]{1,0:T(8,128)(2,1)S(1)} %get-tuple-element.143), channel_id=1, source_target_pairs={{0,32},{1,33},{2,34},{3,35},{4,36},{5,37},{6,38},{7,39},{8,40},{9,... | collective-permute-start | bytes 663560 | tf_op jit(solution)/shard_map/ppermute | solution.py:42
  118.5 10.2 %collective-permute-start.23 = (f16[96,1152]{1,0:T(8,128)(2,1)S(1)}, f16[96,1152]{1,0:T(8,128)(2,1)S(1)}, u32[]{:S(2)}, u32[]{:S(2)}) collective-permute-start(f16[96,1152]{1,0:T(8,128)(2,1)S(1)} %get-tuple-element.144), channel_id=1, source_target_pairs={{0,16},{1,17},{2,18},{3,19},{4,20},{5,21},{6,22},{7,23},{8,24},{9,... | collective-permute-start | bytes 663560 | tf_op jit(solution)/shard_map/ppermute | solution.py:42
  120.4 7.6 %collective-permute-start.22 = (bf16[96,1024]{1,0:T(8,128)(2,1)S(1)}, bf16[96,1024]{1,0:T(8,128)(2,1)S(1)}, u32[]{:S(2)}, u32[]{:S(2)}) collective-permute-start(bf16[96,1024]{1,0:T(8,128)(2,1)S(1)} %fusion.26), channel_id=1, source_target_pairs={{0,64},{1,65},{2,66},{3,67},{4,68},{5,69},{6,70},{7,71},{8,72},{9,... | collective-permute-start | bytes 589832 | tf_op jit(solution)/shard_map/ppermute | solution.py:42
  122.0 8.5 %collective-permute-start.21 = (bf16[96,1024]{1,0:T(8,128)(2,1)S(1)}, bf16[96,1024]{1,0:T(8,128)(2,1)S(1)}, u32[]{:S(2)}, u32[]{:S(2)}) collective-permute-start(bf16[96,1024]{1,0:T(8,128)(2,1)S(1)} %fusion.26), channel_id=1, source_target_pairs={{0,0},{1,1},{2,2},{3,3},{4,4},{5,5},{6,6},{7,7},{8,12},{9,13},{10,... | collective-permute-start | bytes 589832 | tf_op jit(solution)/shard_map/ppermute | solution.py:42
  128.0 93.8 %collective-permute-start.20 = (bf16[2,384,1536]{2,1,0:T(8,128)(2,1)}, bf16[2,384,1536]{2,1,0:T(8,128)(2,1)}, u32[]{:S(2)}, u32[]{:S(2)}) collective-permute-start(bf16[2,384,1536]{2,1,0:T(8,128)(2,1)} %maximum_maximum_fusion), channel_id=1, source_target_pairs={{0,8},{1,9},{2,10},{3,11},{4,12},{5,13},{6,14},{7,15},{8,0},{9,1},... | collective-permute-start | bytes 7077896 | tf_op jit(solution)/shard_map/ppermute | solution.py:42
  130.6 7.0 %collective-permute-start.34 = (bf16[96,1024]{1,0:T(8,128)(2,1)S(1)}, bf16[96,1024]{1,0:T(8,128)(2,1)S(1)}, u32[]{:S(2)}, u32[]{:S(2)}) collective-permute-start(bf16[96,1024]{1,0:T(8,128)(2,1)S(1)} %collective-permute-done.21), channel_id=1, source_target_pairs={{0,0},{1,17},{2,34},{3,51},{4,68},{5,85},{6,102},{7,119},{8,64},{9... | collective-permute-start | bytes 589832 | tf_op jit(solution)/shard_map/ppermute | solution.py:42
  137.5 11.6 %collective-permute-start.35 = (bf16[96,1024]{1,0:T(8,128)(2,1)S(1)}, bf16[96,1024]{1,0:T(8,128)(2,1)S(1)}, u32[]{:S(2)}, u32[]{:S(2)}) collective-permute-start(bf16[96,1024]{1,0:T(8,128)(2,1)S(1)} %collective-permute-done.34), channel_id=1, source_target_pairs={{0,1},{1,0},{2,3},{3,2},{4,5},{5,4},{6,7},{7,6},{8,9},{9,8},{10,11... | collective-permute-start | bytes 589832 | tf_op jit(solution)/shard_map/ppermute | solution.py:42
  149.2 22.7 %collective-permute-start.38 = (bf16[2,96,1024]{2,1,0:T(8,128)(2,1)S(1)}, bf16[2,96,1024]{2,1,0:T(8,128)(2,1)S(1)}, u32[]{:S(2)}, u32[]{:S(2)}) collective-permute-start(bf16[2,96,1024]{2,1,0:T(8,128)(2,1)S(1)} %pad_maximum_fusion.14.refs_0_), channel_id=1, source_target_pairs={{0,6},{1,7},{2,4},{3,5},{4,2},{5,3},{6,0},{7,1},{8,14},{9,15},{10,... | collective-permute-start | bytes 1179656 | tf_op jit(solution)/shard_map/ppermute | solution.py:42
  153.0 20.9 %collective-permute-start.37 = (bf16[2,96,1024]{2,1,0:T(8,128)(2,1)S(1)}, bf16[2,96,1024]{2,1,0:T(8,128)(2,1)S(1)}, u32[]{:S(2)}, u32[]{:S(2)}) collective-permute-start(bf16[2,96,1024]{2,1,0:T(8,128)(2,1)S(1)} %pad_maximum_fusion.14.refs_0_), channel_id=1, source_target_pairs={{0,4},{1,5},{2,6},{3,7},{4,0},{5,1},{6,2},{7,3},{8,12},{9,13},{10,... | collective-permute-start | bytes 1179656 | tf_op jit(solution)/shard_map/ppermute | solution.py:42
  153.3 5.0 %collective-permute-start.33 = (bf16[96,1024]{1,0:T(8,128)(2,1)S(1)}, bf16[96,1024]{1,0:T(8,128)(2,1)S(1)}, u32[]{:S(2)}, u32[]{:S(2)}) collective-permute-start(bf16[96,1024]{1,0:T(8,128)(2,1)S(1)} %fusion.21), channel_id=1, source_target_pairs={{0,64},{1,65},{2,66},{3,67},{4,68},{5,69},{6,70},{7,71},{8,72},{9,... | collective-permute-start | bytes 589832 | tf_op jit(solution)/shard_map/ppermute | solution.py:42
  153.4 14.2 %collective-permute-start.29 = (bf16[96,1024]{1,0:T(8,128)(2,1)S(1)}, bf16[96,1024]{1,0:T(8,128)(2,1)S(1)}, u32[]{:S(2)}, u32[]{:S(2)}) collective-permute-start(bf16[96,1024]{1,0:T(8,128)(2,1)S(1)} %fusion.21), channel_id=1, source_target_pairs={{0,0},{1,1},{2,2},{3,3},{4,4},{5,5},{6,6},{7,7},{8,12},{9,13},{10,... | collective-permute-start | bytes 589832 | tf_op jit(solution)/shard_map/ppermute | solution.py:42
  158.3 17.7 %collective-permute-start.36 = (bf16[2,96,1024]{2,1,0:T(8,128)(2,1)S(1)}, bf16[2,96,1024]{2,1,0:T(8,128)(2,1)S(1)}, u32[]{:S(2)}, u32[]{:S(2)}) collective-permute-start(bf16[2,96,1024]{2,1,0:T(8,128)(2,1)S(1)} %pad_maximum_fusion.14.refs_0_), channel_id=1, source_target_pairs={{0,2},{1,3},{2,0},{3,1},{4,6},{5,7},{6,4},{7,5},{8,10},{9,11},{10,... | collective-permute-start | bytes 1179656 | tf_op jit(solution)/shard_map/ppermute | solution.py:42
  167.6 19.8 %collective-permute-start.28 = (bf16[2,96,1024]{2,1,0:T(8,128)(2,1)S(1)}, bf16[2,96,1024]{2,1,0:T(8,128)(2,1)S(1)}, u32[]{:S(2)}, u32[]{:S(2)}) collective-permute-start(bf16[2,96,1024]{2,1,0:T(8,128)(2,1)S(1)} %pad_maximum_fusion.11), channel_id=1, source_target_pairs={{0,48},{1,49},{2,50},{3,51},{4,52},{5,53},{6,54},{7,55},{8,56},{9,... | collective-permute-start | bytes 1179656 | tf_op jit(solution)/shard_map/ppermute | solution.py:42
  171.9 30.2 %copy-start.1 = (bf16[2,96,1024]{2,1,0:T(8,128)(2,1)}, bf16[2,96,1024]{2,1,0:T(8,128)(2,1)S(1)}, u32[]{:S(2)}) copy-start(bf16[2,96,1024]{2,1,0:T(8,128)(2,1)S(1)} %collective-permute-done.38.refs_3_) | copy-start | bytes 1179652
  171.9 15.5 %collective-permute-start.27 = (bf16[2,96,1024]{2,1,0:T(8,128)(2,1)S(1)}, bf16[2,96,1024]{2,1,0:T(8,128)(2,1)S(1)}, u32[]{:S(2)}, u32[]{:S(2)}) collective-permute-start(bf16[2,96,1024]{2,1,0:T(8,128)(2,1)S(1)} %pad_maximum_fusion.11), channel_id=1, source_target_pairs={{0,32},{1,33},{2,34},{3,35},{4,36},{5,37},{6,38},{7,39},{8,40},{9,... | collective-permute-start | bytes 1179656 | tf_op jit(solution)/shard_map/ppermute | solution.py:42
  173.8 18.2 %collective-permute-start.26 = (bf16[2,96,1024]{2,1,0:T(8,128)(2,1)S(1)}, bf16[2,96,1024]{2,1,0:T(8,128)(2,1)S(1)}, u32[]{:S(2)}, u32[]{:S(2)}) collective-permute-start(bf16[2,96,1024]{2,1,0:T(8,128)(2,1)S(1)} %pad_maximum_fusion.11), channel_id=1, source_target_pairs={{0,16},{1,17},{2,18},{3,19},{4,20},{5,21},{6,22},{7,23},{8,24},{9,... | collective-permute-start | bytes 1179656 | tf_op jit(solution)/shard_map/ppermute | solution.py:42
  176.8 15.9 %collective-permute-start.30 = (bf16[96,1024]{1,0:T(8,128)(2,1)S(1)}, bf16[96,1024]{1,0:T(8,128)(2,1)S(1)}, u32[]{:S(2)}, u32[]{:S(2)}) collective-permute-start(bf16[96,1024]{1,0:T(8,128)(2,1)S(1)} %collective-permute-done.29), channel_id=1, source_target_pairs={{0,0},{1,17},{2,34},{3,51},{4,68},{5,85},{6,102},{7,119},{8,64},{9... | collective-permute-start | bytes 589832 | tf_op jit(solution)/shard_map/ppermute | solution.py:42
  187.4 21.4 %collective-permute-start.41 = (bf16[2,96,1024]{2,1,0:T(8,128)(2,1)S(1)}, bf16[2,96,1024]{2,1,0:T(8,128)(2,1)S(1)}, u32[]{:S(2)}, u32[]{:S(2)}) collective-permute-start(bf16[2,96,1024]{2,1,0:T(8,128)(2,1)S(1)} %pad_maximum_fusion.13), channel_id=1, source_target_pairs={{0,48},{1,49},{2,50},{3,51},{4,52},{5,53},{6,54},{7,55},{8,56},{9,... | collective-permute-start | bytes 1179656 | tf_op jit(solution)/shard_map/ppermute | solution.py:42
  187.4 21.4 %collective-permute-start.40 = (bf16[2,96,1024]{2,1,0:T(8,128)(2,1)S(1)}, bf16[2,96,1024]{2,1,0:T(8,128)(2,1)S(1)}, u32[]{:S(2)}, u32[]{:S(2)}) collective-permute-start(bf16[2,96,1024]{2,1,0:T(8,128)(2,1)S(1)} %pad_maximum_fusion.13), channel_id=1, source_target_pairs={{0,32},{1,33},{2,34},{3,35},{4,36},{5,37},{6,38},{7,39},{8,40},{9,... | collective-permute-start | bytes 1179656 | tf_op jit(solution)/shard_map/ppermute | solution.py:42
  192.0 16.9 %collective-permute-start.39 = (bf16[2,96,1024]{2,1,0:T(8,128)(2,1)S(1)}, bf16[2,96,1024]{2,1,0:T(8,128)(2,1)S(1)}, u32[]{:S(2)}, u32[]{:S(2)}) collective-permute-start(bf16[2,96,1024]{2,1,0:T(8,128)(2,1)S(1)} %pad_maximum_fusion.13), channel_id=1, source_target_pairs={{0,16},{1,17},{2,18},{3,19},{4,20},{5,21},{6,22},{7,23},{8,24},{9,... | collective-permute-start | bytes 1179656 | tf_op jit(solution)/shard_map/ppermute | solution.py:42
  192.7 12.9 %collective-permute-start.31 = (bf16[96,1024]{1,0:T(8,128)(2,1)S(1)}, bf16[96,1024]{1,0:T(8,128)(2,1)S(1)}, u32[]{:S(2)}, u32[]{:S(2)}) collective-permute-start(bf16[96,1024]{1,0:T(8,128)(2,1)S(1)} %collective-permute-done.30), channel_id=1, source_target_pairs={{0,1},{1,0},{2,3},{3,2},{4,5},{5,4},{6,7},{7,6},{8,9},{9,8},{10,11... | collective-permute-start | bytes 589832 | tf_op jit(solution)/shard_map/ppermute | solution.py:42
  206.4 33.7 %collective-permute-start.32 = (bf16[4,2,96,1024]{3,2,1,0:T(8,128)(2,1)S(1)}, bf16[4,2,96,1024]{3,2,1,0:T(8,128)(2,1)}, u32[]{:S(2)}, u32[]{:S(2)}) collective-permute-start(bf16[4,2,96,1024]{3,2,1,0:T(8,128)(2,1)S(1)} %pad_maximum_fusion.3.left00), channel_id=1, source_target_pairs={{0,8},{1,9},{2,10},{3,11},{4,12},{5,13},{6,14},{7,15},{8,0},{9,1},... | collective-permute-start | bytes 4718600 | tf_op jit(solution)/shard_map/ppermute | solution.py:42
  209.1 31.0 %collective-permute-start.42 = (bf16[4,2,96,1024]{3,2,1,0:T(8,128)(2,1)S(1)}, bf16[4,2,96,1024]{3,2,1,0:T(8,128)(2,1)}, u32[]{:S(2)}, u32[]{:S(2)}) collective-permute-start(bf16[4,2,96,1024]{3,2,1,0:T(8,128)(2,1)S(1)} %pad_maximum_fusion.4.left10), channel_id=1, source_target_pairs={{0,8},{1,9},{2,10},{3,11},{4,12},{5,13},{6,14},{7,15},{8,0},{9,1},... | collective-permute-start | bytes 4718600 | tf_op jit(solution)/shard_map/ppermute | solution.py:42
  214.3 25.4 %collective-permute-start.45 = (bf16[2,96,1024]{2,1,0:T(8,128)(2,1)S(1)}, bf16[2,96,1024]{2,1,0:T(8,128)(2,1)S(1)}, u32[]{:S(2)}, u32[]{:S(2)}) collective-permute-start(bf16[2,96,1024]{2,1,0:T(8,128)(2,1)S(1)} %copy-done), channel_id=1, source_target_pairs={{0,6},{1,7},{2,4},{3,5},{4,2},{5,3},{6,0},{7,1},{8,14},{9,15},{10,... | collective-permute-start | bytes 1179656 | tf_op jit(solution)/shard_map/ppermute | solution.py:42
  221.8 17.9 %collective-permute-start.44 = (bf16[2,96,1024]{2,1,0:T(8,128)(2,1)S(1)}, bf16[2,96,1024]{2,1,0:T(8,128)(2,1)S(1)}, u32[]{:S(2)}, u32[]{:S(2)}) collective-permute-start(bf16[2,96,1024]{2,1,0:T(8,128)(2,1)S(1)} %copy-done), channel_id=1, source_target_pairs={{0,4},{1,5},{2,6},{3,7},{4,0},{5,1},{6,2},{7,3},{8,12},{9,13},{10,... | collective-permute-start | bytes 1179656 | tf_op jit(solution)/shard_map/ppermute | solution.py:42
  221.8 18.3 %collective-permute-start.43 = (bf16[2,96,1024]{2,1,0:T(8,128)(2,1)S(1)}, bf16[2,96,1024]{2,1,0:T(8,128)(2,1)S(1)}, u32[]{:S(2)}, u32[]{:S(2)}) collective-permute-start(bf16[2,96,1024]{2,1,0:T(8,128)(2,1)S(1)} %copy-done), channel_id=1, source_target_pairs={{0,2},{1,3},{2,0},{3,1},{4,6},{5,7},{6,4},{7,5},{8,10},{9,11},{10,... | collective-permute-start | bytes 1179656 | tf_op jit(solution)/shard_map/ppermute | solution.py:42
  (28 other events, 142.6 us)

commit v3 on v2

--- a/solution.py
+++ b/solution.py
@@ -74,6 +74,11 @@
 def turn_tok(yl, x, c, z, yh):
     s = (z * YH + yh) ^ (c * X + x)
     return s // X, s % X, yl, z, yh
+
+
+def turn_tok_yh(yl, x, c, z, yh):
+    yl, x, c, z, yh = turn_tok(yl, x, c, z, yh)
+    return yl, x, c, z, 1 - yh
 
 
 def part(value, index, count, axis):
@@ -128,7 +133,7 @@
         out_shape=jax.ShapeDtypeStruct((rows, units + LANES), jnp.float32),
         in_specs=[vmem] * (len(fields) + len(weights)),
         out_specs=vmem,
-        compiler_params=pltpu.CompilerParams(vmem_limit_bytes=32 * 2**20),
+        compiler_params=pltpu.CompilerParams(vmem_limit_bytes=16 * 2**20),
         cost_estimate=pl.CostEstimate(
             flops=2 * rows * depth * units,
             bytes_accessed=2 * depth * (rows + units) + 4 * rows * units,
@@ -138,51 +143,60 @@
     )(*fields, *weights)
 
 
-def gram_kernel(scale, places, left00, left01, left10, left11, *refs):
-    pieces, out_ref, right, sems = refs[:-3], refs[-3], refs[-2], refs[-1]
+def gram_kernel(scale, lefts, places, *refs):
+    lefts, pieces = refs[:lefts], refs[lefts:-3]
+    out_ref, right, sems = refs[-3:]
     b = pl.program_id(0)
 
     @pl.when((b == 0) & (pl.program_id(1) == 0))
     def _():
         copies = []
-        for i, piece in enumerate(pieces):
-            for j in range(YH):
-                slot = i * YH + j
+        tiles = [piece.at[j] for piece in pieces for j in range(piece.shape[0])]
+        for i, tile in enumerate(tiles):
+            for h in range(YL):
+                slot = h * len(tiles) + i
                 copies.append(
-                    pltpu.make_async_copy(piece.at[j], right.at[places[slot]], sems.at[slot])
+                    pltpu.make_async_copy(tile.at[h], right.at[places[slot]], sems.at[slot])
                 )
         for copy in copies:
             copy.start()
         for copy in copies:
             copy.wait()
 
-    def tokens(left):
-        block = left[...]
-        return block.reshape(block.shape[0] * block.shape[2], block.shape[3])
-
-    for which, order in ((0, (left00, left01, left10, left11)), (1, (left10, left11, left00, left01))):
+    def tokens(left, h):
+        block = left[:, 0, h]
+        return block.reshape(block.shape[0] * block.shape[1], block.shape[2])
+
+    for which in range(YL):
 
         @pl.when(b == which)
         def _():
-            block = jnp.concatenate([tokens(left) for left in order], 0)
+            block = jnp.concatenate(
+                [tokens(left, h ^ which) for h in range(YL) for left in lefts], 0
+            )
             rows = right[...]
             rows = rows.reshape(rows.shape[0] * rows.shape[1], rows.shape[2])
             out_ref[...] = contract_rows(block, rows) * scale
 
 
 def grad_gram_of(lefts, pieces, places, yl, total):
-    _, _, rows, units = lefts[0].shape
-    tile = 256
+    rows, units = lefts[0].shape[3:]
+    tile = 512
     tiles = units // tile
-    block = pl.BlockSpec((X, 1, rows, tile), lambda b, n, *_: (0, b, 0, n))
     slots = YL * CORE * X
     return pl.pallas_call(
-        functools.partial(gram_kernel, 1.0 / total),
+        functools.partial(gram_kernel, 1.0 / total, len(lefts)),
         out_shape=jax.ShapeDtypeStruct((YL * units, units), jnp.float32),
         grid_spec=pltpu.PrefetchScalarGridSpec(
             num_scalar_prefetch=1,
             grid=(YL, tiles),
-            in_specs=[block] * 4 + [pl.BlockSpec(memory_space=pl.ANY)] * len(pieces),
+            in_specs=[
+                pl.BlockSpec(
+                    (left.shape[0], 1, YL, rows, tile), lambda b, n, *_: (0, b, 0, 0, n)
+                )
+                for left in lefts
+            ]
+            + [pl.BlockSpec(memory_space=pltpu.HBM)] * len(pieces),
             out_specs=pl.BlockSpec(
                 (tile, units), lambda b, n, places: ((places[slots] ^ b) * tiles + n, 0)
             ),
@@ -191,7 +205,7 @@
                 pltpu.SemaphoreType.DMA((slots,)),
             ],
         ),
-        compiler_params=pltpu.CompilerParams(vmem_limit_bytes=40 * 2**20),
+        compiler_params=pltpu.CompilerParams(vmem_limit_bytes=24 * 2**20),
         cost_estimate=pl.CostEstimate(
             flops=2 * total * YL * units * units,
             bytes_accessed=6 * total * units + 8 * units * units,
@@ -245,83 +259,92 @@
     def activated(gate, hidden):
         return (hidden * (gate / (1.0 + jnp.exp(-gate)))).astype(jnp.bfloat16)
 
-    def round_x(both):
-        return jnp.stack([both if k == 0 else over_x(both, k) for k in range(X)])
-
     gate_near = part(gate_weight, yl, YL, 1)
-    gate_across = over_yl(part(gate_weight, 1 - yl, YL, 1))
-    input_cut = cut(layer_input)
+    gate_far = part(gate_weight, 1 - yl, YL, 1)
+    gate_across = over_yl(gate_far)
+    input_cut = cut(after(layer_input, gate_far))
     input_first = over_other_y(input_cut[0])
     pieces = [over_x(input_cut[k], k) for k in range(1, X)]
     own_band = part(layer_input, band, YL * X, 1)
     grad_cut = cut(output_grad, own_band)
-    gate_across, input_first, pieces, grad_cut = lax.optimization_barrier(
-        (gate_across, input_first, pieces, grad_cut)
+    down_near, down_far = part(down_weight, yl, YL, 0), part(down_weight, 1 - yl, YL, 0)
+    gate_across, input_first, pieces, grad_cut, down_far = lax.optimization_barrier(
+        (gate_across, input_first, pieces, grad_cut, down_far)
     )
     gate_other = over_core(jnp.stack([gate_near, gate_across]))
     input_rest = over_other_y(jnp.concatenate(pieces, 0))
+    down_across = over_yl(down_far)
     input_own = jnp.concatenate([input_cut[0]] + pieces, 0)
     grad_pieces = [over_x(grad_cut[k], k) for k in range(1, X)]
 
     gate_pieces = [gate_near, gate_across, gate_other[0], gate_other[1]]
-    gate_part = halved([scaled_product([input_own], gate_pieces, False)])
-    down_near = part(down_weight, yl, YL, 0)
-    down_across = over_yl(after(part(down_weight, 1 - yl, YL, 0), gate_other))
-    grad_pieces, input_first, input_rest = after(
-        (grad_pieces, input_first, input_rest), gate_part
-    )
-    gate_sent = exchanged(after(gate_part, *grad_pieces))
-    grad_both = jnp.concatenate([grad_cut[0]] + grad_pieces, 0)
-    split = 3 * half
-    near = over_yl(after(grad_both[:, split:], gate_part))
-    far = over_other_y(after(grad_both[:, :split], input_rest))
-    input_other = jnp.concatenate([input_first, input_rest], 0)
-    gate_part = scaled_product([input_other], swapped(gate_pieces), False)
-
-    down_across = after(down_across, gate_part)
+    gate_part = scaled_product([input_own], gate_pieces, False)
+    grad_pieces, down_across, input_rest, gate_part = lax.optimization_barrier(
+        (grad_pieces, down_across, input_rest, gate_part)
+    )
     down_other = over_core(jnp.stack([down_near, down_across]))
     down_pieces = [down_near, down_across, down_other[0], down_other[1]]
-    gate = summed(after(gate_sent, gate_part))
-    hidden_part = scaled_product([after(grad_both, gate)], down_pieces, True)
-    mixed_sent = exchanged(halved([hidden_part, gate_part]))
-    near, far = after([near, far], hidden_part)
-    hidden_part = halved([scaled_product([far, near], swapped(down_pieces), True)])
-    hidden_sent = exchanged(hidden_part)
-    mixed_sent = after(mixed_sent, hidden_part)
-    cuts = mixed_sent[0].shape[1] // 2
-    first = activated(gate, summed([piece[:, :cuts] for piece in mixed_sent]))
-    gate = summed([piece[:, cuts:] for piece in mixed_sent])
-    moved = send(first, turn_tp)
-    both = jnp.stack([first, over_yl(first)])
-    moved, both, hidden_sent = lax.optimization_barrier((moved, both, hidden_sent))
-    first_round = round_x(both)
-    second = activated(gate, summed(hidden_sent))
-    moved = send(moved, turn_tok)
-    pair = jnp.stack([moved, over_yh(moved)])
-    first_turned = [pair] + [over_z(pair, k) for k in range(1, Z)]
-    both = jnp.stack([second, over_yl(second)])
-    moved = send(send(second, turn_tp), turn_tok)
-    pair = jnp.stack([moved, over_yh(moved)])
-    second_turned = [pair] + [over_z(pair, k) for k in range(1, Z)]
-    second_round = round_x(after(both, *first_turned))
-    first_gathered = [first_round, over_core(after(first_round, pair))]
-    second_gathered = [second_round, over_core(second_round)]
-
-    bands = jnp.stack([grad_both[:, YL * width :], near[:, half:]])
+    grad_both = jnp.concatenate([grad_cut[0]] + grad_pieces, 0)
+    far, near, band_own = jnp.split(grad_both, [width, 2 * width], 1)
+    near, far, band_own, grad_both = lax.optimization_barrier((near, far, band_own, grad_both))
+    near = over_yl(near)
+    far = over_other_y(far)
+    hidden_part = scaled_product([grad_both], down_pieces, True)
+    first_sent = exchanged(halved([gate_part, hidden_part]))
+    input_other = jnp.concatenate([input_first, input_rest], 0)
+    gate_part = scaled_product(
+        [after(input_other, hidden_part)], swapped(gate_pieces), False
+    )
+    near, far = after([near, far], gate_part, first_sent[1], first_sent[3])
+    hidden_part = scaled_product([far, near], swapped(down_pieces), True)
+    second_sent = exchanged(halved([gate_part, hidden_part]))
+    band_other = over_yl(after(band_own, near))
+    second_sent, band_other = lax.optimization_barrier((second_sent, band_other))
+
+    def up_grads(sent):
+        cuts = sent[0].shape[1] // 2
+        gate = summed([piece[:, :cuts] for piece in sent])
+        return activated(gate, summed([piece[:, cuts:] for piece in sent]))
+
+    first = up_grads(after(first_sent, hidden_part))
+    up_grad = jnp.stack([first, up_grads(after(second_sent, first))])
+    moved = send(up_grad, turn_tp)
+    both = jnp.stack([up_grad, over_yl(up_grad)])
+    pair = jnp.stack([send(moved, turn_tok), send(moved, turn_tok_yh)])
+    pair, both = lax.optimization_barrier((pair, both))
+    ring = [over_x(both, 1), over_x(both, 3), over_z(pair, 1), over_z(pair, 3)]
+    ring, both, pair = lax.optimization_barrier((ring, both, pair))
+    near_most = jnp.stack([both] + ring[:2])
+    far_most = over_core(near_most)
+    opposite = [
+        over_x(ring[0][0], 3),
+        over_x(ring[1][1], 1),
+        over_z(ring[2][0], 3),
+        over_z(ring[3][1], 1),
+    ]
+    bands = jnp.stack([band_own, band_other])
     mine = jnp.stack([input_own[:, :half], input_other[:, half : 2 * half]])
     theirs = jnp.stack([input_own[:, 2 * half : 3 * half], input_other[:, 3 * half :]])
-    across = over_core(after(jnp.concatenate([theirs, bands], 2), first))
+    across = over_core(after(jnp.concatenate([theirs, bands], 2), pair))
     left = jnp.stack([mine, across[:, :, :half]]).reshape(total, half)
     right = jnp.stack([bands, across[:, :, half:]]).reshape(total, width)
     input_gram = contract_rows(left, right) / total
 
+    opposite, input_gram = lax.optimization_barrier((opposite, input_gram))
+    near_last = jnp.stack(opposite[:2])[None]
+    turned = [pair, ring[2], opposite[2][None], opposite[3][None], ring[3]]
+    rows_of = [near_most, near_last, far_most, over_core(near_last)]
+
     turn = band ^ chip ^ (c * X + x)
-    places = [
-        (yl ^ c ^ h) * (CORE * X) + (turn ^ j) for h in range(YL) for j in range(Z * YH)
-    ]
+    places = []
+    for h in range(YL):
+        for j in range(Z * YH):
+            tile = turn ^ j
+            tile = tile ^ ((tile & (X - 1)) >> 1)
+            places.append((yl ^ c ^ h) * (CORE * X) + tile)
     grad_gram = grad_gram_of(
-        first_gathered + second_gathered,
-        first_turned + after(second_turned, input_gram),
+        rows_of,
+        turned,
         jnp.stack(places + [yl]).astype(jnp.int32),
         yl,
         total,

time: 258 us -> 231 us (0.90)
  starting transfers between devices: 94.4 us -> 61.9 us
  waiting for transfers between devices: 95.2 us -> 109 us
  local copies, waits for them, and re-layouts: 21.2 us -> 16.3 us
    ppermute x46 -> x36, starting transfers between devices: 94.4 us -> 61.9 us  [send(): return lax.ppermute(value, AXES, pairs)]
    ppermute x46 -> x36, waiting for transfers between devices: 95.2 us -> 109 us  [send(): return lax.ppermute(value, AXES, pairs)]
    unnamed x68 -> x30, local copies, waits for them, and re-layouts: 9.86 us -> 9.66 us
  transfers between devices with their start and end apart: 46 -> 36, of which waited for: 19 -> 25; matrix products, arithmetic and copies ran while one was open for 13% -> 10% of each run, Pallas kernels for 4% -> 5%
where the time goes in v3:
time: 231 us; the launch traced here: 230 us
  waiting for transfers between devices  109 us (47%)
  starting transfers between devices  61.9 us (27%)
  Pallas kernels  26.2 us (11%)
  local copies, waits for them, and re-layouts  16.3 us (7%)
  other arithmetic  12 us (5%)
  matrix products  3.16 us (1%)
    ppermute x36, waiting for transfers between devices, send(): return lax.ppermute(value, AXES, pairs)  109 us
    ppermute x36, starting transfers between devices, send(): return lax.ppermute(value, AXES, pairs)  61.9 us
    pallas_call x1, Pallas kernels, grad_gram_of(): pl.pallas_call(functools.partial(gram_kernel, 1.0 / total, len(lefts)), o...  15.7 us
    pallas_call x4, Pallas kernels, scaled_product(): pl.pallas_call(functools.partial(scaled_kernel, contract, len(fields)), o...  10.5 us
    unnamed x30, local copies, waits for them, and re-layouts  9.66 us
  transfers between devices with their start and end apart: 36, of which 25 were waited for; matrix products, arithmetic and copies ran while one was open for 10% of the time, Pallas kernels for 5%

profile of v3, /device:TPU:1, one launch (start us, length us, event | category | flops | bytes accessed | tf_op | source)
XLA Modules:
  0.0 230.4 jit_solution(16649815460545934918)
XLA Ops:
  0.7 2.7 %constant_dynamic-slice_fusion.1 = (bf16[512,1024]{1,0:T(8,128)(2,1)S(1)}, bf16[512,1024]{1,0:T(8,128)(2,1)}) fusion(bf16[512,2048]{1,0:T(8,128)(2,1)} %param.6, s32[]{:T(128)S(6)} %select_n.115, s32[]{:T(128)S(6)} %select_n.95), kind=kLoop, calls=%fused_computation.190 | loop fusion | bytes 4194312 | tf_op jit(solution)/shard_map/dynamic_slice | solution.py:86
  3.4 2.1 collective-permute-start
  5.5 1.6 constant_dynamic-slice_fusion.6
  7.9 1.9 collective-permute-start.1
  12.6 2.5 %collective-permute-start.3 = (bf16[96,2048]{1,0:T(8,128)(2,1)}, bf16[96,2048]{1,0:T(8,128)(2,1)S(1)}, u32[]{:S(2)}, u32[]{:S(2)}) collective-permute-start(bf16[96,2048]{1,0:T(8,128)(2,1)} %pad_maximum_fusion.11), channel_id=1, source_target_pairs={{0,32},{1,33},{2,34},{3,35},{4,36},{5,37},{6,38},{7,39},{8,40},{9,... | collective-permute-start | bytes 1179656 | tf_op jit(solution)/shard_map/ppermute | solution.py:42
  21.8 9.1 %collective-permute-done.3 = bf16[96,2048]{1,0:T(8,128)(2,1)S(1)} collective-permute-done((bf16[96,2048]{1,0:T(8,128)(2,1)}, bf16[96,2048]{1,0:T(8,128)(2,1)S(1)}, u32[]{:S(2)}, u32[]{:S(2)}) %collective-permute-start.3) | collective-permute-done | bytes 393248 | tf_op jit(solution)/shard_map/ppermute | solution.py:42
  30.8 3.6 %collective-permute-done.4 = bf16[96,2048]{1,0:T(8,128)(2,1)S(1)} collective-permute-done((bf16[96,2048]{1,0:T(8,128)(2,1)}, bf16[96,2048]{1,0:T(8,128)(2,1)S(1)}, u32[]{:S(2)}, u32[]{:S(2)}) %collective-permute-start.4) | collective-permute-done | bytes 393248 | tf_op jit(solution)/shard_map/ppermute | solution.py:42
  34.7 2.8 %collective-permute-start.10 = (bf16[2,512,1024]{2,1,0:T(8,128)(2,1)S(1)}, bf16[2,512,1024]{2,1,0:T(8,128)(2,1)S(1)}, u32[]{:S(2)}, u32[]{:S(2)}) collective-permute-start(bf16[2,512,1024]{2,1,0:T(8,128)(2,1)S(1)} %pad_maximum_fusion.1), channel_id=1, source_target_pairs={{0,8},{1,9},{2,10},{3,11},{4,12},{5,13},{6,14},{7,15},{8,0},{9,1},... | collective-permute-start | bytes 6291464 | tf_op jit(solution)/shard_map/ppermute | solution.py:42
  38.5 1.4 collective-permute-start.6
  39.8 1.5 collective-permute-done.10
  42.3 2.3 %pad_maximum_fusion.3.refs_0_ = bf16[384,2048]{1,0:T(8,128)(2,1)S(1)} fusion(bf16[96,2048]{1,0:T(8,128)(2,1)S(1)} %collective-permute-done.4, bf16[96,2048]{1,0:T(8,128)(2,1)S(1)} %collective-permute-done.3, bf16[96,2048]{1,0:T(8,128)(2,1)S(1)} %collective-permute-done.2, bf16[96,512]{1,0:T(8,128)(2,1)S(1)} %get-tuple-element.161, ...), kind=kLoop, calls=%fused_computation.22 | loop fusion | flops 11010048 | bytes 3145728 | tf_op jit(solution)/shard_map/concatenate | solution.py:277
  44.8 2.6 %scaled_product.4 = f32[384,1152]{1,0:T(8,128)S(1)} custom-call(bf16[384,2048]{1,0:T(8,128)(2,1)S(1)} %pad_maximum_fusion.3.refs_0_, bf16[512,1024]{1,0:T(8,128)(2,1)S(1)} %get-tuple-element.115.refs_1_.refs_2_, bf16[512,1024]{1,0:T(8,128)(2,1)S(1)} %collective-permute-done.refs_2_.refs_1_, bf16[512,1024]{1,0:T(8,128)(2,1)S(1)} %get-tuple-element.114.refs_3_.refs_4_, ...), custom_call_target="tpu_custom_call" | custom-call | flops 1610612736 | bytes 7340032 | tf_op jit(solution)/shard_map/scaled_product/pallas_call | solution.py:131
  47.4 5.6 %collective-permute-done.5 = bf16[96,3072]{1,0:T(8,128)(2,1)S(1)} collective-permute-done((bf16[96,3072]{1,0:T(8,128)(2,1)S(1)}, bf16[96,3072]{1,0:T(8,128)(2,1)S(1)}, u32[]{:S(2)}, u32[]{:S(2)}) %collective-permute-start.5) | collective-permute-done | bytes 589856 | tf_op jit(solution)/shard_map/ppermute | solution.py:42
  53.1 12.6 %collective-permute-done.6 = bf16[96,3072]{1,0:T(8,128)(2,1)S(1)} collective-permute-done((bf16[96,3072]{1,0:T(8,128)(2,1)S(1)}, bf16[96,3072]{1,0:T(8,128)(2,1)S(1)}, u32[]{:S(2)}, u32[]{:S(2)}) %collective-permute-start.6) | collective-permute-done | bytes 589856 | tf_op jit(solution)/shard_map/ppermute | solution.py:42
  65.7 4.0 %collective-permute-done.7 = bf16[96,3072]{1,0:T(8,128)(2,1)S(1)} collective-permute-done((bf16[96,3072]{1,0:T(8,128)(2,1)S(1)}, bf16[96,3072]{1,0:T(8,128)(2,1)S(1)}, u32[]{:S(2)}, u32[]{:S(2)}) %collective-permute-start.7) | collective-permute-done | bytes 589856 | tf_op jit(solution)/shard_map/ppermute | solution.py:42
  69.9 1.3 collective-permute-start.11
  72.2 1.5 collective-permute-start.16
  73.7 1.3 collective-permute-done.11
  75.1 2.6 %scaled_product.5 = f32[384,1152]{1,0:T(8,128)S(1)} custom-call(bf16[384,3072]{1,0:T(8,128)(2,1)S(1)} %constant_dynamic-update-slice_fusion.refs_0_, bf16[1024,512]{1,0:T(8,128)(2,1)S(1)} %get-tuple-element.111.refs_1_.refs_3_, bf16[1024,512]{1,0:T(8,128)(2,1)S(1)} %collective-permute-done.8.refs_2_, ...), custom_call_target="tpu_custom_call" | custom-call | flops 1610612736 | bytes 7340032 | tf_op jit(solution)/shard_map/scaled_product/pallas_call | solution.py:131
  80.7 2.1 collective-permute-start.13
  82.8 2.6 %scaled_product.6 = f32[384,1152]{1,0:T(8,128)S(1)} custom-call(bf16[384,2048]{1,0:T(8,128)(2,1)S(1)} %constant_dynamic-update-slice_fusion.4.refs_0_, bf16[512,1024]{1,0:T(8,128)(2,1)S(1)} %collective-permute-done.refs_2_.refs_1_, bf16[512,1024]{1,0:T(8,128)(2,1)S(1)} %get-tuple-element.115.refs_1_.refs_2_, ...), custom_call_target="tpu_custom_call" | custom-call | flops 1610612736 | bytes 7340032 | tf_op jit(solution)/shard_map/scaled_product/pallas_call | solution.py:131
  85.5 5.4 %collective-permute-done.15.refs_1_ = bf16[384,1024]{1,0:T(8,128)(2,1)S(1)} collective-permute-done((bf16[384,1024]{1,0:T(8,128)(2,1)S(1)}, bf16[384,1024]{1,0:T(8,128)(2,1)S(1)}, u32[]{:S(2)}, u32[]{:S(2)}) %collective-permute-start.15) | collective-permute-done | bytes 786464 | tf_op jit(solution)/shard_map/ppermute | solution.py:42
  90.9 1.3 collective-permute-done.16.refs_0_
  92.2 2.6 %scaled_product.7 = f32[384,1152]{1,0:T(8,128)S(1)} custom-call(bf16[384,1024]{1,0:T(8,128)(2,1)S(1)} %collective-permute-done.16.refs_0_, bf16[384,1024]{1,0:T(8,128)(2,1)S(1)} %collective-permute-done.15.refs_1_, bf16[1024,512]{1,0:T(8,128)(2,1)S(1)} %collective-permute-done.8.refs_2_, bf16[1024,512]{1,0:T(8,128)(2,1)S(1)} %get-tuple-element.111.refs_1_.refs_3_, ...), custom_call_target="tpu_custom_call" | custom-call | flops 1610612736 | bytes 7340032 | tf_op jit(solution)/shard_map/scaled_product/pallas_call | solution.py:131
  95.0 5.0 %collective-permute-done.13 = f16[96,2304]{1,0:T(8,128)(2,1)S(1)} collective-permute-done((f16[96,2304]{1,0:T(8,128)(2,1)S(1)}, f16[96,2304]{1,0:T(8,128)(2,1)S(1)}, u32[]{:S(2)}, u32[]{:S(2)}) %collective-permute-start.13) | collective-permute-done | bytes 442400 | tf_op jit(solution)/shard_map/ppermute | solution.py:42
  99.9 1.5 collective-permute-start.20
  101.8 4.7 %collective-permute-start.19 = (f16[96,2304]{1,0:T(8,128)(2,1)S(1)}, f16[96,2304]{1,0:T(8,128)(2,1)S(1)}, u32[]{:S(2)}, u32[]{:S(2)}) collective-permute-start(f16[96,2304]{1,0:T(8,128)(2,1)S(1)} %get-tuple-element.121), channel_id=1, source_target_pairs={{0,48},{1,49},{2,50},{3,51},{4,52},{5,53},{6,54},{7,55},{8,56},{9,... | collective-permute-start | bytes 1327112 | tf_op jit(solution)/shard_map/ppermute | solution.py:42
  106.5 1.3 collective-permute-start.18
  109.4 5.9 %collective-permute-done.19 = f16[96,2304]{1,0:T(8,128)(2,1)S(1)} collective-permute-done((f16[96,2304]{1,0:T(8,128)(2,1)S(1)}, f16[96,2304]{1,0:T(8,128)(2,1)S(1)}, u32[]{:S(2)}, u32[]{:S(2)}) %collective-permute-start.19) | collective-permute-done | bytes 442400 | tf_op jit(solution)/shard_map/ppermute | solution.py:42
  116.4 9.4 %collective-permute-done.18 = f16[96,2304]{1,0:T(8,128)(2,1)S(1)} collective-permute-done((f16[96,2304]{1,0:T(8,128)(2,1)S(1)}, f16[96,2304]{1,0:T(8,128)(2,1)S(1)}, u32[]{:S(2)}, u32[]{:S(2)}) %collective-permute-start.18) | collective-permute-done | bytes 442400 | tf_op jit(solution)/shard_map/ppermute | solution.py:42
  127.5 5.5 %collective-permute-start.21 = (bf16[2,96,1024]{2,1,0:T(8,128)(2,1)S(1)}, bf16[2,96,1024]{2,1,0:T(8,128)(2,1)S(1)}, u32[]{:S(2)}, u32[]{:S(2)}) collective-permute-start(bf16[2,96,1024]{2,1,0:T(8,128)(2,1)S(1)} %get-tuple-element.182), channel_id=1, source_target_pairs={{0,0},{1,1},{2,2},{3,3},{4,4},{5,5},{6,6},{7,7},{8,12},{9,13},{10,... | collective-permute-start | bytes 1179656 | tf_op jit(solution)/shard_map/ppermute | solution.py:42
  133.2 5.1 %collective-permute-done.21 = bf16[2,96,1024]{2,1,0:T(8,128)(2,1)S(1)} collective-permute-done((bf16[2,96,1024]{2,1,0:T(8,128)(2,1)S(1)}, bf16[2,96,1024]{2,1,0:T(8,128)(2,1)S(1)}, u32[]{:S(2)}, u32[]{:S(2)}) %collective-permute-start.21) | collective-permute-done | bytes 393248 | tf_op jit(solution)/shard_map/ppermute | solution.py:42
  138.2 3.6 %collective-permute-start.22 = (bf16[2,96,1024]{2,1,0:T(8,128)(2,1)S(1)}, bf16[2,96,1024]{2,1,0:T(8,128)(2,1)S(1)}, u32[]{:S(2)}, u32[]{:S(2)}) collective-permute-start(bf16[2,96,1024]{2,1,0:T(8,128)(2,1)S(1)} %collective-permute-done.21), channel_id=1, source_target_pairs={{0,0},{1,17},{2,34},{3,51},{4,68},{5,85},{6,102},{7,119},{8,64},{9... | collective-permute-start | bytes 1179656 | tf_op jit(solution)/shard_map/ppermute | solution.py:42
  142.2 14.1 %collective-permute-done.23 = bf16[2,96,1024]{2,1,0:T(8,128)(2,1)S(1)} collective-permute-done((bf16[2,96,1024]{2,1,0:T(8,128)(2,1)S(1)}, bf16[2,96,1024]{2,1,0:T(8,128)(2,1)S(1)}, u32[]{:S(2)}, u32[]{:S(2)}) %collective-permute-start.23) | collective-permute-done | bytes 393248 | tf_op jit(solution)/shard_map/ppermute | solution.py:42
  156.4 7.8 %collective-permute-start.26 = (bf16[2,2,96,1024]{3,2,1,0:T(8,128)(2,1)S(1)}, bf16[2,2,96,1024]{3,2,1,0:T(8,128)(2,1)S(1)}, u32[]{:S(2)}, u32[]{:S(2)}) collective-permute-start(bf16[2,2,96,1024]{3,2,1,0:T(8,128)(2,1)S(1)} %pad_maximum_fusion.6), channel_id=1, source_target_pairs={{0,48},{1,49},{2,50},{3,51},{4,52},{5,53},{6,54},{7,55},{8,56},{9,... | collective-permute-start | bytes 2359304 | tf_op jit(solution)/shard_map/ppermute | solution.py:42
  164.2 6.9 %collective-permute-start.28 = (bf16[2,2,96,1024]{3,2,1,0:T(8,128)(2,1)S(1)}, bf16[2,2,96,1024]{3,2,1,0:T(8,128)(2,1)S(1)}, u32[]{:S(2)}, u32[]{:S(2)}) collective-permute-start(bf16[2,2,96,1024]{3,2,1,0:T(8,128)(2,1)S(1)} %pad_maximum_fusion.5.refs_4_), channel_id=1, source_target_pairs={{0,6},{1,7},{2,4},{3,5},{4,2},{5,3},{6,0},{7,1},{8,14},{9,15},{10,... | collective-permute-start | bytes 2359304 | tf_op jit(solution)/shard_map/ppermute | solution.py:42
  171.5 10.4 %collective-permute-done.26 = bf16[2,2,96,1024]{3,2,1,0:T(8,128)(2,1)S(1)} collective-permute-done((bf16[2,2,96,1024]{3,2,1,0:T(8,128)(2,1)S(1)}, bf16[2,2,96,1024]{3,2,1,0:T(8,128)(2,1)S(1)}, u32[]{:S(2)}, u32[]{:S(2)}) %collective-permute-start.26) | collective-permute-done | bytes 786464 | tf_op jit(solution)/shard_map/ppermute | solution.py:42
  181.9 1.7 collective-permute-done.25
  183.6 1.6 collective-permute-done.28.refs_8_
  186.1 5.0 %collective-permute-start.33 = (bf16[2,384,1536]{2,1,0:T(8,128)(2,1)S(1)}, bf16[2,384,1536]{2,1,0:T(8,128)(2,1)S(1)}, u32[]{:S(2)}, u32[]{:S(2)}) collective-permute-start(bf16[2,384,1536]{2,1,0:T(8,128)(2,1)S(1)} %maximum_maximum_fusion), channel_id=1, source_target_pairs={{0,8},{1,9},{2,10},{3,11},{4,12},{5,13},{6,14},{7,15},{8,0},{9,1},... | collective-permute-start | bytes 7077896 | tf_op jit(solution)/shard_map/ppermute | solution.py:42
  191.9 1.4 collective-permute-start.31
  193.5 1.8 collective-permute-done.33
  195.3 2.0 collective-permute-start.29
  197.5 3.2 %bitcast_multiply_fusion = f32[512,1024]{1,0:T(8,128)} fusion(bf16[1,2,384,1024]{3,2,1,0:T(8,128)(2,1)S(1)} %slice_bitcast_fusion, bf16[1,2,384,1024]{3,2,1,0:T(8,128)(2,1)S(1)} %maximum_bitcast_fusion, bf16[1,2,384,512]{3,2,1,0:T(8,128)(2,1)S(1)} %slice_bitcast_fusion.5, bf16[1,2,384,512]{3,2,1,0:T(8,128)(2,1)S(1)} %maximum_bitcast_fusion.1), kind=kOutput, calls=%fused_computation.20 | convolution fusion | flops 1613496320 | bytes 6815744 | tf_op jit(solution)/shard_map/dot_general | solution.py:18
  200.7 1.4 collective-permute-done.32
  203.9 2.9 %collective-permute-done.29 = bf16[2,96,1024]{2,1,0:T(8,128)(2,1)S(1)} collective-permute-done((bf16[2,96,1024]{2,1,0:T(8,128)(2,1)S(1)}, bf16[2,96,1024]{2,1,0:T(8,128)(2,1)S(1)}, u32[]{:S(2)}, u32[]{:S(2)}) %collective-permute-start.29) | collective-permute-done | bytes 393248 | tf_op jit(solution)/shard_map/ppermute | solution.py:42
  209.1 2.1 collective-permute-done.35.refs_3_
  214.5 15.7 %grad_gram.1 = f32[2048,1024]{1,0:T(8,128)} custom-call(s32[17]{0:T(128)S(1)} %stack.212.places, bf16[3,2,2,96,1024]{4,3,2,1,0:T(8,128)(2,1)S(1)} %pad_maximum_fusion.refs_0_, bf16[1,2,2,96,1024]{4,3,2,1,0:T(8,128)(2,1)} %maximum_bitcast_fusion.2.refs_1_, bf16[3,2,2,96,1024]{4,3,2,1,0:T(8,128)(2,1)} %collective-permute-done.34.refs_2_, ...), custom_call_target="tpu_custom_call" | custom-call | flops 6442450944 | bytes 17825792 | tf_op jit(solution)/shard_map/grad_gram/pallas_call | solution.py:187
  (124 shorter events, 31.9 us)
Async XLA Ops:
  3.4 31.1 %collective-permute-start = (bf16[512,1024]{1,0:T(8,128)(2,1)}, bf16[512,1024]{1,0:T(8,128)(2,1)S(1)}, u32[]{:S(2)}, u32[]{:S(2)}) collective-permute-start(bf16[512,1024]{1,0:T(8,128)(2,1)} %get-tuple-element.116), channel_id=1, source_target_pairs={{0,64},{1,65},{2,66},{3,67},{4,68},{5,69},{6,70},{7,71},{8,72},{9,... | collective-permute-start | bytes 3145736 | tf_op jit(solution)/shard_map/ppermute | solution.py:42
  7.1 2.7 %copy-start.7 = (bf16[96,512]{1,0:T(8,128)(2,1)}, bf16[96,512]{1,0:T(8,128)(2,1)S(1)}, u32[]{:S(2)}) copy-start(bf16[96,512]{1,0:T(8,128)(2,1)S(1)} %get-tuple-element.163) | copy-start | bytes 294916
  7.1 2.7 %copy-start.9 = (bf16[96,512]{1,0:T(8,128)(2,1)}, bf16[96,512]{1,0:T(8,128)(2,1)S(1)}, u32[]{:S(2)}) copy-start(bf16[96,512]{1,0:T(8,128)(2,1)S(1)} %get-tuple-element.164) | copy-start | bytes 294916
  7.9 13.8 %collective-permute-start.1 = (bf16[96,2048]{1,0:T(8,128)(2,1)}, bf16[96,2048]{1,0:T(8,128)(2,1)}, u32[]{:S(2)}, u32[]{:S(2)}) collective-permute-start(bf16[96,2048]{1,0:T(8,128)(2,1)} %pad_maximum_fusion.9), channel_id=1, source_target_pairs={{0,65},{1,64},{2,67},{3,66},{4,69},{5,68},{6,71},{7,70},{8,73},{9,... | collective-permute-start | bytes 1179656 | tf_op jit(solution)/shard_map/ppermute | solution.py:42
  10.6 11.2 %collective-permute-start.2 = (bf16[96,2048]{1,0:T(8,128)(2,1)}, bf16[96,2048]{1,0:T(8,128)(2,1)S(1)}, u32[]{:S(2)}, u32[]{:S(2)}) collective-permute-start(bf16[96,2048]{1,0:T(8,128)(2,1)} %pad_maximum_fusion.10), channel_id=1, source_target_pairs={{0,16},{1,17},{2,18},{3,19},{4,20},{5,21},{6,22},{7,23},{8,24},{9,... | collective-permute-start | bytes 1179656 | tf_op jit(solution)/shard_map/ppermute | solution.py:42
  12.6 18.2 %collective-permute-start.3 = (bf16[96,2048]{1,0:T(8,128)(2,1)}, bf16[96,2048]{1,0:T(8,128)(2,1)S(1)}, u32[]{:S(2)}, u32[]{:S(2)}) collective-permute-start(bf16[96,2048]{1,0:T(8,128)(2,1)} %pad_maximum_fusion.11), channel_id=1, source_target_pairs={{0,32},{1,33},{2,34},{3,35},{4,36},{5,37},{6,38},{7,39},{8,40},{9,... | collective-permute-start | bytes 1179656 | tf_op jit(solution)/shard_map/ppermute | solution.py:42
  15.8 18.7 %collective-permute-start.4 = (bf16[96,2048]{1,0:T(8,128)(2,1)}, bf16[96,2048]{1,0:T(8,128)(2,1)S(1)}, u32[]{:S(2)}, u32[]{:S(2)}) collective-permute-start(bf16[96,2048]{1,0:T(8,128)(2,1)} %pad_maximum_fusion.12), channel_id=1, source_target_pairs={{0,48},{1,49},{2,50},{3,51},{4,52},{5,53},{6,54},{7,55},{8,56},{9,... | collective-permute-start | bytes 1179656 | tf_op jit(solution)/shard_map/ppermute | solution.py:42
  16.0 5.5 %copy-start.6 = (bf16[2048,512]{1,0:T(8,128)(2,1)S(1)}, bf16[2048,512]{1,0:T(8,128)(2,1)}, u32[]{:S(2)}) copy-start(bf16[2048,512]{1,0:T(8,128)(2,1)} %param.7) | copy-start | bytes 6291460
  34.7 7.6 %copy-start.8 = (bf16[96,512]{1,0:T(8,128)(2,1)S(1)}, bf16[96,512]{1,0:T(8,128)(2,1)}, u32[]{:S(2)}) copy-start(bf16[96,512]{1,0:T(8,128)(2,1)} %copy-done.7) | copy-start | bytes 294916
  34.7 7.6 %copy-start.10 = (bf16[96,512]{1,0:T(8,128)(2,1)S(1)}, bf16[96,512]{1,0:T(8,128)(2,1)}, u32[]{:S(2)}) copy-start(bf16[96,512]{1,0:T(8,128)(2,1)} %copy-done.9) | copy-start | bytes 294916
  34.7 6.6 %collective-permute-start.10 = (bf16[2,512,1024]{2,1,0:T(8,128)(2,1)S(1)}, bf16[2,512,1024]{2,1,0:T(8,128)(2,1)S(1)}, u32[]{:S(2)}, u32[]{:S(2)}) collective-permute-start(bf16[2,512,1024]{2,1,0:T(8,128)(2,1)S(1)} %pad_maximum_fusion.1), channel_id=1, source_target_pairs={{0,8},{1,9},{2,10},{3,11},{4,12},{5,13},{6,14},{7,15},{8,0},{9,1},... | collective-permute-start | bytes 6291464 | tf_op jit(solution)/shard_map/ppermute | solution.py:42
  37.6 32.1 %collective-permute-start.9 = (bf16[288,2048]{1,0:T(8,128)(2,1)S(1)}, bf16[288,2048]{1,0:T(8,128)(2,1)S(1)}, u32[]{:S(2)}, u32[]{:S(2)}) collective-permute-start(bf16[288,2048]{1,0:T(8,128)(2,1)S(1)} %pad_maximum_fusion.4), channel_id=1, source_target_pairs={{0,65},{1,64},{2,67},{3,66},{4,69},{5,68},{6,71},{7,70},{8,73},{9,... | collective-permute-start | bytes 3538952 | tf_op jit(solution)/shard_map/ppermute | solution.py:42
  38.4 31.2 %collective-permute-start.8 = (bf16[1024,512]{1,0:T(8,128)(2,1)S(1)}, bf16[1024,512]{1,0:T(8,128)(2,1)S(1)}, u32[]{:S(2)}, u32[]{:S(2)}) collective-permute-start(bf16[1024,512]{1,0:T(8,128)(2,1)S(1)} %get-tuple-element.58), channel_id=1, source_target_pairs={{0,64},{1,65},{2,66},{3,67},{4,68},{5,69},{6,70},{7,71},{8,72},{9,... | collective-permute-start | bytes 3145736 | tf_op jit(solution)/shard_map/ppermute | solution.py:42
  38.5 14.6 %collective-permute-start.5 = (bf16[96,3072]{1,0:T(8,128)(2,1)S(1)}, bf16[96,3072]{1,0:T(8,128)(2,1)S(1)}, u32[]{:S(2)}, u32[]{:S(2)}) collective-permute-start(bf16[96,3072]{1,0:T(8,128)(2,1)S(1)} %get-tuple-element.55), channel_id=1, source_target_pairs={{0,16},{1,17},{2,18},{3,19},{4,20},{5,21},{6,22},{7,23},{8,24},{9,... | collective-permute-start | bytes 1769480 | tf_op jit(solution)/shard_map/ppermute | solution.py:42
  38.5 27.2 %collective-permute-start.6 = (bf16[96,3072]{1,0:T(8,128)(2,1)S(1)}, bf16[96,3072]{1,0:T(8,128)(2,1)S(1)}, u32[]{:S(2)}, u32[]{:S(2)}) collective-permute-start(bf16[96,3072]{1,0:T(8,128)(2,1)S(1)} %get-tuple-element.56), channel_id=1, source_target_pairs={{0,32},{1,33},{2,34},{3,35},{4,36},{5,37},{6,38},{7,39},{8,40},{9,... | collective-permute-start | bytes 1769480 | tf_op jit(solution)/shard_map/ppermute | solution.py:42
  41.3 28.4 %collective-permute-start.7 = (bf16[96,3072]{1,0:T(8,128)(2,1)S(1)}, bf16[96,3072]{1,0:T(8,128)(2,1)S(1)}, u32[]{:S(2)}, u32[]{:S(2)}) collective-permute-start(bf16[96,3072]{1,0:T(8,128)(2,1)S(1)} %get-tuple-element.57), channel_id=1, source_target_pairs={{0,48},{1,49},{2,50},{3,51},{4,52},{5,53},{6,54},{7,55},{8,56},{9,... | collective-permute-start | bytes 1769480 | tf_op jit(solution)/shard_map/ppermute | solution.py:42
  69.9 5.1 %collective-permute-start.11 = (bf16[2,1024,512]{2,1,0:T(8,128)(2,1)S(1)}, bf16[2,1024,512]{2,1,0:T(8,128)(2,1)S(1)}, u32[]{:S(2)}, u32[]{:S(2)}) collective-permute-start(bf16[2,1024,512]{2,1,0:T(8,128)(2,1)S(1)} %pad_maximum_fusion.2), channel_id=1, source_target_pairs={{0,8},{1,9},{2,10},{3,11},{4,12},{5,13},{6,14},{7,15},{8,0},{9,1},... | collective-permute-start | bytes 6291464 | tf_op jit(solution)/shard_map/ppermute | solution.py:42
  71.7 19.2 %collective-permute-start.15 = (bf16[384,1024]{1,0:T(8,128)(2,1)S(1)}, bf16[384,1024]{1,0:T(8,128)(2,1)S(1)}, u32[]{:S(2)}, u32[]{:S(2)}) collective-permute-start(bf16[384,1024]{1,0:T(8,128)(2,1)S(1)} %get-tuple-element.70), channel_id=1, source_target_pairs={{0,64},{1,65},{2,66},{3,67},{4,68},{5,69},{6,70},{7,71},{8,72},{9,... | collective-permute-start | bytes 2359304 | tf_op jit(solution)/shard_map/ppermute | solution.py:42
  72.2 20.0 %collective-permute-start.16 = (bf16[384,1024]{1,0:T(8,128)(2,1)S(1)}, bf16[384,1024]{1,0:T(8,128)(2,1)S(1)}, u32[]{:S(2)}, u32[]{:S(2)}) collective-permute-start(bf16[384,1024]{1,0:T(8,128)(2,1)S(1)} %get-tuple-element.71), channel_id=1, source_target_pairs={{0,65},{1,64},{2,67},{3,66},{4,69},{5,68},{6,71},{7,70},{8,73},{9,... | collective-permute-start | bytes 2359304 | tf_op jit(solution)/shard_map/ppermute | solution.py:42
  78.3 13.9 %collective-permute-start.12 = (f16[96,2304]{1,0:T(8,128)(2,1)S(1)}, f16[96,2304]{1,0:T(8,128)(2,1)S(1)}, u32[]{:S(2)}, u32[]{:S(2)}) collective-permute-start(f16[96,2304]{1,0:T(8,128)(2,1)S(1)} %get-tuple-element.119), channel_id=1, source_target_pairs={{0,16},{1,17},{2,18},{3,19},{4,20},{5,21},{6,22},{7,23},{8,24},{9,... | collective-permute-start | bytes 1327112 | tf_op jit(solution)/shard_map/ppermute | solution.py:42
  78.4 13.8 %collective-permute-start.14 = (f16[96,2304]{1,0:T(8,128)(2,1)S(1)}, f16[96,2304]{1,0:T(8,128)(2,1)S(1)}, u32[]{:S(2)}, u32[]{:S(2)}) collective-permute-start(f16[96,2304]{1,0:T(8,128)(2,1)S(1)} %get-tuple-element.120), channel_id=1, source_target_pairs={{0,48},{1,49},{2,50},{3,51},{4,52},{5,53},{6,54},{7,55},{8,56},{9,... | collective-permute-start | bytes 1327112 | tf_op jit(solution)/shard_map/ppermute | solution.py:42
  80.7 19.3 %collective-permute-start.13 = (f16[96,2304]{1,0:T(8,128)(2,1)S(1)}, f16[96,2304]{1,0:T(8,128)(2,1)S(1)}, u32[]{:S(2)}, u32[]{:S(2)}) collective-permute-start(f16[96,2304]{1,0:T(8,128)(2,1)S(1)} %get-tuple-element.117), channel_id=1, source_target_pairs={{0,32},{1,33},{2,34},{3,35},{4,36},{5,37},{6,38},{7,39},{8,40},{9,... | collective-permute-start | bytes 1327112 | tf_op jit(solution)/shard_map/ppermute | solution.py:42
  99.9 25.9 %collective-permute-start.20 = (bf16[384,1024]{1,0:T(8,128)(2,1)S(1)}, bf16[384,1024]{1,0:T(8,128)(2,1)S(1)}, u32[]{:S(2)}, u32[]{:S(2)}) collective-permute-start(bf16[384,1024]{1,0:T(8,128)(2,1)S(1)} %get-tuple-element.82), channel_id=1, source_target_pairs={{0,64},{1,65},{2,66},{3,67},{4,68},{5,69},{6,70},{7,71},{8,72},{9,... | collective-permute-start | bytes 2359304 | tf_op jit(solution)/shard_map/ppermute | solution.py:42
  101.8 13.5 %collective-permute-start.19 = (f16[96,2304]{1,0:T(8,128)(2,1)S(1)}, f16[96,2304]{1,0:T(8,128)(2,1)S(1)}, u32[]{:S(2)}, u32[]{:S(2)}) collective-permute-start(f16[96,2304]{1,0:T(8,128)(2,1)S(1)} %get-tuple-element.121), channel_id=1, source_target_pairs={{0,48},{1,49},{2,50},{3,51},{4,52},{5,53},{6,54},{7,55},{8,56},{9,... | collective-permute-start | bytes 1327112 | tf_op jit(solution)/shard_map/ppermute | solution.py:42
  106.5 9.9 %collective-permute-start.17 = (f16[96,2304]{1,0:T(8,128)(2,1)S(1)}, f16[96,2304]{1,0:T(8,128)(2,1)S(1)}, u32[]{:S(2)}, u32[]{:S(2)}) collective-permute-start(f16[96,2304]{1,0:T(8,128)(2,1)S(1)} %get-tuple-element.123), channel_id=1, source_target_pairs={{0,16},{1,17},{2,18},{3,19},{4,20},{5,21},{6,22},{7,23},{8,24},{9,... | collective-permute-start | bytes 1327112 | tf_op jit(solution)/shard_map/ppermute | solution.py:42
  106.5 19.3 %collective-permute-start.18 = (f16[96,2304]{1,0:T(8,128)(2,1)S(1)}, f16[96,2304]{1,0:T(8,128)(2,1)S(1)}, u32[]{:S(2)}, u32[]{:S(2)}) collective-permute-start(f16[96,2304]{1,0:T(8,128)(2,1)S(1)} %get-tuple-element.124), channel_id=1, source_target_pairs={{0,32},{1,33},{2,34},{3,35},{4,36},{5,37},{6,38},{7,39},{8,40},{9,... | collective-permute-start | bytes 1327112 | tf_op jit(solution)/shard_map/ppermute | solution.py:42
  127.5 10.7 %collective-permute-start.21 = (bf16[2,96,1024]{2,1,0:T(8,128)(2,1)S(1)}, bf16[2,96,1024]{2,1,0:T(8,128)(2,1)S(1)}, u32[]{:S(2)}, u32[]{:S(2)}) collective-permute-start(bf16[2,96,1024]{2,1,0:T(8,128)(2,1)S(1)} %get-tuple-element.182), channel_id=1, source_target_pairs={{0,0},{1,1},{2,2},{3,3},{4,4},{5,5},{6,6},{7,7},{8,12},{9,13},{10,... | collective-permute-start | bytes 1179656 | tf_op jit(solution)/shard_map/ppermute | solution.py:42
  133.1 9.1 %collective-permute-start.24 = (bf16[2,96,1024]{2,1,0:T(8,128)(2,1)S(1)}, bf16[2,96,1024]{2,1,0:T(8,128)(2,1)S(1)}, u32[]{:S(2)}, u32[]{:S(2)}) collective-permute-start(bf16[2,96,1024]{2,1,0:T(8,128)(2,1)S(1)} %get-tuple-element.182), channel_id=1, source_target_pairs={{0,64},{1,65},{2,66},{3,67},{4,68},{5,69},{6,70},{7,71},{8,72},{9,... | collective-permute-start | bytes 1179656 | tf_op jit(solution)/shard_map/ppermute | solution.py:42
  138.2 18.1 %collective-permute-start.23 = (bf16[2,96,1024]{2,1,0:T(8,128)(2,1)S(1)}, bf16[2,96,1024]{2,1,0:T(8,128)(2,1)S(1)}, u32[]{:S(2)}, u32[]{:S(2)}) collective-permute-start(bf16[2,96,1024]{2,1,0:T(8,128)(2,1)S(1)} %collective-permute-done.21), channel_id=1, source_target_pairs={{0,1},{1,16},{2,35},{3,50},{4,69},{5,84},{6,103},{7,118},{8,65},{9... | collective-permute-start | bytes 1179656 | tf_op jit(solution)/shard_map/ppermute | solution.py:42
  138.2 18.1 %collective-permute-start.22 = (bf16[2,96,1024]{2,1,0:T(8,128)(2,1)S(1)}, bf16[2,96,1024]{2,1,0:T(8,128)(2,1)S(1)}, u32[]{:S(2)}, u32[]{:S(2)}) collective-permute-start(bf16[2,96,1024]{2,1,0:T(8,128)(2,1)S(1)} %collective-permute-done.21), channel_id=1, source_target_pairs={{0,0},{1,17},{2,34},{3,51},{4,68},{5,85},{6,102},{7,119},{8,64},{9... | collective-permute-start | bytes 1179656 | tf_op jit(solution)/shard_map/ppermute | solution.py:42
  156.4 25.5 %collective-permute-start.26 = (bf16[2,2,96,1024]{3,2,1,0:T(8,128)(2,1)S(1)}, bf16[2,2,96,1024]{3,2,1,0:T(8,128)(2,1)S(1)}, u32[]{:S(2)}, u32[]{:S(2)}) collective-permute-start(bf16[2,2,96,1024]{3,2,1,0:T(8,128)(2,1)S(1)} %pad_maximum_fusion.6), channel_id=1, source_target_pairs={{0,48},{1,49},{2,50},{3,51},{4,52},{5,53},{6,54},{7,55},{8,56},{9,... | collective-permute-start | bytes 2359304 | tf_op jit(solution)/shard_map/ppermute | solution.py:42
  164.2 19.4 %collective-permute-start.25 = (bf16[2,2,96,1024]{3,2,1,0:T(8,128)(2,1)S(1)}, bf16[2,2,96,1024]{3,2,1,0:T(8,128)(2,1)S(1)}, u32[]{:S(2)}, u32[]{:S(2)}) collective-permute-start(bf16[2,2,96,1024]{3,2,1,0:T(8,128)(2,1)S(1)} %pad_maximum_fusion.6), channel_id=1, source_target_pairs={{0,16},{1,17},{2,18},{3,19},{4,20},{5,21},{6,22},{7,23},{8,24},{9,... | collective-permute-start | bytes 2359304 | tf_op jit(solution)/shard_map/ppermute | solution.py:42
  164.2 21.0 %collective-permute-start.28 = (bf16[2,2,96,1024]{3,2,1,0:T(8,128)(2,1)S(1)}, bf16[2,2,96,1024]{3,2,1,0:T(8,128)(2,1)S(1)}, u32[]{:S(2)}, u32[]{:S(2)}) collective-permute-start(bf16[2,2,96,1024]{3,2,1,0:T(8,128)(2,1)S(1)} %pad_maximum_fusion.5.refs_4_), channel_id=1, source_target_pairs={{0,6},{1,7},{2,4},{3,5},{4,2},{5,3},{6,0},{7,1},{8,14},{9,15},{10,... | collective-permute-start | bytes 2359304 | tf_op jit(solution)/shard_map/ppermute | solution.py:42
  171.1 14.9 %collective-permute-start.27 = (bf16[2,2,96,1024]{3,2,1,0:T(8,128)(2,1)S(1)}, bf16[2,2,96,1024]{3,2,1,0:T(8,128)(2,1)S(1)}, u32[]{:S(2)}, u32[]{:S(2)}) collective-permute-start(bf16[2,2,96,1024]{3,2,1,0:T(8,128)(2,1)S(1)} %pad_maximum_fusion.5.refs_4_), channel_id=1, source_target_pairs={{0,2},{1,3},{2,0},{3,1},{4,6},{5,7},{6,4},{7,5},{8,10},{9,11},{10,... | collective-permute-start | bytes 2359304 | tf_op jit(solution)/shard_map/ppermute | solution.py:42
  185.2 6.6 %copy-start = (bf16[2,2,96,1024]{3,2,1,0:T(8,128)(2,1)}, bf16[2,2,96,1024]{3,2,1,0:T(8,128)(2,1)S(1)}, u32[]{:S(2)}) copy-start(bf16[2,2,96,1024]{3,2,1,0:T(8,128)(2,1)S(1)} %collective-permute-done.28.refs_8_) | copy-start | bytes 2359300
  186.1 5.6 %copy-start.2 = (bf16[2,2,96,1024]{3,2,1,0:T(8,128)(2,1)}, bf16[2,2,96,1024]{3,2,1,0:T(8,128)(2,1)S(1)}, u32[]{:S(2)}) copy-start(bf16[2,2,96,1024]{3,2,1,0:T(8,128)(2,1)S(1)} %collective-permute-done.27.refs_5_) | copy-start | bytes 2359300
  186.1 9.2 %collective-permute-start.33 = (bf16[2,384,1536]{2,1,0:T(8,128)(2,1)S(1)}, bf16[2,384,1536]{2,1,0:T(8,128)(2,1)S(1)}, u32[]{:S(2)}, u32[]{:S(2)}) collective-permute-start(bf16[2,384,1536]{2,1,0:T(8,128)(2,1)S(1)} %maximum_maximum_fusion), channel_id=1, source_target_pairs={{0,8},{1,9},{2,10},{3,11},{4,12},{5,13},{6,14},{7,15},{8,0},{9,1},... | collective-permute-start | bytes 7077896 | tf_op jit(solution)/shard_map/ppermute | solution.py:42
  191.6 17.5 %collective-permute-start.34 = (bf16[3,2,2,96,1024]{4,3,2,1,0:T(8,128)(2,1)S(1)}, bf16[3,2,2,96,1024]{4,3,2,1,0:T(8,128)(2,1)}, u32[]{:S(2)}, u32[]{:S(2)}) collective-permute-start(bf16[3,2,2,96,1024]{4,3,2,1,0:T(8,128)(2,1)S(1)} %pad_maximum_fusion.refs_0_), channel_id=1, source_target_pairs={{0,8},{1,9},{2,10},{3,11},{4,12},{5,13},{6,14},{7,15},{8,0},{9,1},... | collective-permute-start | bytes 7077896 | tf_op jit(solution)/shard_map/ppermute | solution.py:42
  191.8 10.3 %collective-permute-start.32 = (bf16[2,96,1024]{2,1,0:T(8,128)(2,1)S(1)}, bf16[2,96,1024]{2,1,0:T(8,128)(2,1)S(1)}, u32[]{:S(2)}, u32[]{:S(2)}) collective-permute-start(bf16[2,96,1024]{2,1,0:T(8,128)(2,1)S(1)} %slice_bitcast_fusion.10), channel_id=1, source_target_pairs={{0,2},{1,3},{2,0},{3,1},{4,6},{5,7},{6,4},{7,5},{8,10},{9,11},{10,... | collective-permute-start | bytes 1179656 | tf_op jit(solution)/shard_map/ppermute | solution.py:42
  191.9 11.3 %collective-permute-start.31 = (bf16[2,96,1024]{2,1,0:T(8,128)(2,1)S(1)}, bf16[2,96,1024]{2,1,0:T(8,128)(2,1)S(1)}, u32[]{:S(2)}, u32[]{:S(2)}) collective-permute-start(bf16[2,96,1024]{2,1,0:T(8,128)(2,1)S(1)} %slice_bitcast_fusion.11), channel_id=1, source_target_pairs={{0,6},{1,7},{2,4},{3,5},{4,2},{5,3},{6,0},{7,1},{8,14},{9,15},{10,... | collective-permute-start | bytes 1179656 | tf_op jit(solution)/shard_map/ppermute | solution.py:42
  193.3 10.6 %collective-permute-start.30 = (bf16[2,96,1024]{2,1,0:T(8,128)(2,1)S(1)}, bf16[2,96,1024]{2,1,0:T(8,128)(2,1)S(1)}, u32[]{:S(2)}, u32[]{:S(2)}) collective-permute-start(bf16[2,96,1024]{2,1,0:T(8,128)(2,1)S(1)} %slice_bitcast_fusion.12), channel_id=1, source_target_pairs={{0,16},{1,17},{2,18},{3,19},{4,20},{5,21},{6,22},{7,23},{8,24},{9,... | collective-permute-start | bytes 1179656 | tf_op jit(solution)/shard_map/ppermute | solution.py:42
  195.3 11.5 %collective-permute-start.29 = (bf16[2,96,1024]{2,1,0:T(8,128)(2,1)S(1)}, bf16[2,96,1024]{2,1,0:T(8,128)(2,1)S(1)}, u32[]{:S(2)}, u32[]{:S(2)}) collective-permute-start(bf16[2,96,1024]{2,1,0:T(8,128)(2,1)S(1)} %slice_bitcast_fusion.13), channel_id=1, source_target_pairs={{0,48},{1,49},{2,50},{3,51},{4,52},{5,53},{6,54},{7,55},{8,56},{9,... | collective-permute-start | bytes 1179656 | tf_op jit(solution)/shard_map/ppermute | solution.py:42
  203.1 0.7 copy-start.4
  207.8 3.5 %collective-permute-start.35 = (bf16[1,2,2,96,1024]{4,3,2,1,0:T(8,128)(2,1)}, bf16[1,2,2,96,1024]{4,3,2,1,0:T(8,128)(2,1)}, u32[]{:S(2)}, u32[]{:S(2)}) collective-permute-start(bf16[1,2,2,96,1024]{4,3,2,1,0:T(8,128)(2,1)} %maximum_bitcast_fusion.2.refs_1_), channel_id=1, source_target_pairs={{0,8},{1,9},{2,10},{3,11},{4,12},{5,13},{6,14},{7,15},{8,0},{9,1},... | collective-permute-start | bytes 2359304 | tf_op jit(solution)/shard_map/ppermute | solution.py:42
  211.2 1.1 copy-start.1
  212.3 1.1 copy-start.3
  213.5 1.0 copy-start.5

commit v4 on v3

--- a/solution.py
+++ b/solution.py
@@ -141,6 +141,33 @@
         ),
         name="scaled_product",
     )(*fields, *weights)
+
+
+def product_kernel(scale, left_ref, right_ref, out_ref):
+    out_ref[...] = contract_rows(left_ref[...], right_ref[...]) * scale
+
+
+def input_gram_of(left, right):
+    total, rows = left.shape
+    width = right.shape[1]
+    tile = 256
+    return pl.pallas_call(
+        functools.partial(product_kernel, 1.0 / total),
+        out_shape=jax.ShapeDtypeStruct((rows, width), jnp.float32),
+        grid=(rows // tile,),
+        in_specs=[
+            pl.BlockSpec((total, tile), lambda n: (0, n)),
+            pl.BlockSpec((total, width), lambda n: (0, 0)),
+        ],
+        out_specs=pl.BlockSpec((tile, width), lambda n: (n, 0)),
+        compiler_params=pltpu.CompilerParams(vmem_limit_bytes=20 * 2**20),
+        cost_estimate=pl.CostEstimate(
+            flops=2 * total * rows * width,
+            bytes_accessed=2 * total * (rows + width) + 4 * rows * width,
+            transcendentals=0,
+        ),
+        name="input_gram",
+    )(left, right)
 
 
 def gram_kernel(scale, lefts, places, *refs):
@@ -205,7 +232,7 @@
                 pltpu.SemaphoreType.DMA((slots,)),
             ],
         ),
-        compiler_params=pltpu.CompilerParams(vmem_limit_bytes=24 * 2**20),
+        compiler_params=pltpu.CompilerParams(vmem_limit_bytes=58 * 2**20),
         cost_estimate=pl.CostEstimate(
             flops=2 * total * YL * units * units,
             bytes_accessed=6 * total * units + 8 * units * units,
@@ -259,10 +286,11 @@
     def activated(gate, hidden):
         return (hidden * (gate / (1.0 + jnp.exp(-gate)))).astype(jnp.bfloat16)
 
+    input_cut = cut(layer_input)
+    gate_weight = after(gate_weight, *input_cut)
     gate_near = part(gate_weight, yl, YL, 1)
     gate_far = part(gate_weight, 1 - yl, YL, 1)
     gate_across = over_yl(gate_far)
-    input_cut = cut(after(layer_input, gate_far))
     input_first = over_other_y(input_cut[0])
     pieces = [over_x(input_cut[k], k) for k in range(1, X)]
     own_band = part(layer_input, band, YL * X, 1)
@@ -311,9 +339,17 @@
     moved = send(up_grad, turn_tp)
     both = jnp.stack([up_grad, over_yl(up_grad)])
     pair = jnp.stack([send(moved, turn_tok), send(moved, turn_tok_yh)])
-    pair, both = lax.optimization_barrier((pair, both))
+    bands = jnp.stack([band_own, band_other])
+    mine = jnp.stack([input_own[:, :half], input_other[:, half : 2 * half]])
+    theirs = jnp.stack([input_own[:, 2 * half : 3 * half], input_other[:, 3 * half :]])
+    across = over_core(after(jnp.concatenate([theirs, bands], 2), moved))
+    pair, both, across = lax.optimization_barrier((pair, both, across))
+    left = jnp.stack([mine, across[:, :, :half]]).reshape(total, half)
+    right = jnp.stack([bands, across[:, :, half:]]).reshape(total, width)
+    input_gram = input_gram_of(left, right)
+
     ring = [over_x(both, 1), over_x(both, 3), over_z(pair, 1), over_z(pair, 3)]
-    ring, both, pair = lax.optimization_barrier((ring, both, pair))
+    ring, both, pair, input_gram = lax.optimization_barrier((ring, both, pair, input_gram))
     near_most = jnp.stack([both] + ring[:2])
     far_most = over_core(near_most)
     opposite = [
@@ -322,15 +358,7 @@
         over_z(ring[2][0], 3),
         over_z(ring[3][1], 1),
     ]
-    bands = jnp.stack([band_own, band_other])
-    mine = jnp.stack([input_own[:, :half], input_other[:, half : 2 * half]])
-    theirs = jnp.stack([input_own[:, 2 * half : 3 * half], input_other[:, 3 * half :]])
-    across = over_core(after(jnp.concatenate([theirs, bands], 2), pair))
-    left = jnp.stack([mine, across[:, :, :half]]).reshape(total, half)
-    right = jnp.stack([bands, across[:, :, half:]]).reshape(total, width)
-    input_gram = contract_rows(left, right) / total
-
-    opposite, input_gram = lax.optimization_barrier((opposite, input_gram))
+    opposite = lax.optimization_barrier(opposite)
     near_last = jnp.stack(opposite[:2])[None]
     turned = [pair, ring[2], opposite[2][None], opposite[3][None], ring[3]]
     rows_of = [near_most, near_last, far_most, over_core(near_last)]

time: 231 us -> 222 us (0.961)
  starting transfers between devices: 61.9 us -> 56 us
  matrix products: 3.16 us -> 0 us
  waiting for transfers between devices: 109 us -> 112 us
    ppermute x36, starting transfers between devices: 61.9 us -> 56 us  [send(): return lax.ppermute(value, AXES, pairs)]
    dot_general x1 -> x0, matrix products: 3.16 us -> none  [contract_rows(): lax.dot_general(left, right, (((0,), (0,)), ((), ())), preferred_element_...]
    dynamic_slice x3 -> x2, local copies, waits for them, and re-layouts: 4.44 us -> 1.31 us  [part(): return lax.dynamic_slice_in_dim(value, index * size, size, axis)]
    pallas_call x0 -> x1, Pallas kernels: none -> 3.13 us  [input_gram_of(): pl.pallas_call(functools.partial(product_kernel, 1.0 / total), out_shape=...]
    pallas_call x1, Pallas kernels: 15.7 us -> 13.2 us  [grad_gram_of(): pl.pallas_call(functools.partial(gram_kernel, 1.0 / total, len(lefts)), o...]
    unnamed x30 -> x42, local copies, waits for them, and re-layouts: 9.66 us -> 9.31 us
  transfers between devices with their start and end apart: 36 -> 36, of which waited for: 25 -> 24; matrix products, arithmetic and copies ran while one was open for 10% -> 7% of each run, Pallas kernels for 5% -> 6%
where the time goes in v4:
time: 222 us
  waiting for transfers between devices  112 us (50%)
  starting transfers between devices  56 us (25%)
  Pallas kernels  26.8 us (12%)
  local copies, waits for them, and re-layouts  14.3 us (6%)
  other arithmetic  11.6 us (5%)
    ppermute x36, waiting for transfers between devices, send(): return lax.ppermute(value, AXES, pairs)  112 us
    ppermute x36, starting transfers between devices, send(): return lax.ppermute(value, AXES, pairs)  56 us
    pallas_call x1, Pallas kernels, grad_gram_of(): pl.pallas_call(functools.partial(gram_kernel, 1.0 / total, len(lefts)), o...  13.2 us
    pallas_call x4, Pallas kernels, scaled_product(): pl.pallas_call(functools.partial(scaled_kernel, contract, len(fields)), o...  10.5 us
    unnamed x42, local copies, waits for them, and re-layouts  9.31 us
  transfers between devices with their start and end apart: 36, of which 24 were waited for; matrix products, arithmetic and copies ran while one was open for 7% of the time, Pallas kernels for 6%

profile of v4, /device:TPU:1, one launch (start us, length us, event | category | flops | bytes accessed | tf_op | source)
XLA Modules:
  0.0 221.9 jit_solution(17111602309805771827)
XLA Ops:
  0.8 2.5 %dynamic-slice_dynamic-update-slice_fusion.7 = (bf16[96,3072]{1,0:T(8,128)(2,1)}, bf16[96,3072]{1,0:T(8,128)(2,1)}, bf16[96,3072]{1,0:T(8,128)(2,1)}, bf16[96,30...) fusion(bf16[96,8192]{1,0:T(8,128)(2,1)} %param.5, ...), kind=kLoop, calls=%fused_computation.116 | loop fusion | bytes 3932224
  7.7 2.1 collective-permute-start
  9.9 1.9 collective-permute-start.1
  11.8 2.7 %collective-permute-start.3 = (bf16[96,2048]{1,0:T(8,128)(2,1)}, bf16[96,2048]{1,0:T(8,128)(2,1)S(1)}, u32[]{:S(2)}, u32[]{:S(2)}) collective-permute-start(bf16[96,2048]{1,0:T(8,128)(2,1)} %pad_maximum_fusion.13), channel_id=1, source_target_pairs={{0,32},{1,33},{2,34},{3,35},{4,36},{5,37},{6,38},{7,39},{8,40},{9,... | collective-permute-start | bytes 1179656 | tf_op jit(solution)/shard_map/ppermute | solution.py:42
  15.4 1.9 dynamic-slice_dynamic-update-slice_fusion.6
  17.3 1.8 dynamic-slice_dynamic-update-slice_fusion.5
  19.1 1.8 dynamic-slice_dynamic-update-slice_fusion.4
  20.9 1.9 dynamic-slice_dynamic-update-slice_fusion
  23.0 8.4 %collective-permute-done.2 = bf16[96,2048]{1,0:T(8,128)(2,1)S(1)} collective-permute-done((bf16[96,2048]{1,0:T(8,128)(2,1)}, bf16[96,2048]{1,0:T(8,128)(2,1)S(1)}, u32[]{:S(2)}, u32[]{:S(2)}) %collective-permute-start.2) | collective-permute-done | bytes 393248 | tf_op jit(solution)/shard_map/ppermute | solution.py:42
  31.4 1.5 collective-permute-done.4
  34.6 3.0 %collective-permute-start.9 = (bf16[288,2048]{1,0:T(8,128)(2,1)S(1)}, bf16[288,2048]{1,0:T(8,128)(2,1)S(1)}, u32[]{:S(2)}, u32[]{:S(2)}) collective-permute-start(bf16[288,2048]{1,0:T(8,128)(2,1)S(1)} %pad_maximum_fusion.6), channel_id=1, source_target_pairs={{0,65},{1,64},{2,67},{3,66},{4,69},{5,68},{6,71},{7,70},{8,73},{9,... | collective-permute-start | bytes 3538952 | tf_op jit(solution)/shard_map/ppermute | solution.py:42
  38.8 2.5 %collective-permute-start.6 = (bf16[96,3072]{1,0:T(8,128)(2,1)S(1)}, bf16[96,3072]{1,0:T(8,128)(2,1)S(1)}, u32[]{:S(2)}, u32[]{:S(2)}) collective-permute-start(bf16[96,3072]{1,0:T(8,128)(2,1)S(1)} %copy-done.13), channel_id=1, source_target_pairs={{0,32},{1,33},{2,34},{3,35},{4,36},{5,37},{6,38},{7,39},{8,40},{9,... | collective-permute-start | bytes 1769480 | tf_op jit(solution)/shard_map/ppermute | solution.py:42
  41.5 2.3 %pad_maximum_fusion.4.refs_0_ = bf16[384,2048]{1,0:T(8,128)(2,1)S(1)} fusion(bf16[96,2048]{1,0:T(8,128)(2,1)S(1)} %collective-permute-done.4, bf16[96,2048]{1,0:T(8,128)(2,1)S(1)} %collective-permute-done.3, bf16[96,2048]{1,0:T(8,128)(2,1)S(1)} %collective-permute-done.2, bf16[96,512]{1,0:T(8,128)(2,1)S(1)} %copy-done.6, bf16[96,512]{1,0:T(8,128)(2,1)S(1)} %copy-done.4, ...), kind=kLoop, calls=%fused_computation.17 | loop fusion | flops 11010048 | bytes 3145728 | tf_op jit(solution)/shard_map/concatenate | solution.py:305
  44.0 2.6 %scaled_product.4 = f32[384,1152]{1,0:T(8,128)S(1)} custom-call(bf16[384,2048]{1,0:T(8,128)(2,1)S(1)} %pad_maximum_fusion.4.refs_0_, bf16[512,1024]{1,0:T(8,128)(2,1)S(1)} %get-tuple-element.117.refs_1_.refs_2_, bf16[512,1024]{1,0:T(8,128)(2,1)S(1)} %collective-permute-done.refs_2_.refs_1_, bf16[512,1024]{1,0:T(8,128)(2,1)S(1)} %get-tuple-element.116.refs_3_.refs_4_, ...), custom_call_target="tpu_custom_call" | custom-call | flops 1610612736 | bytes 7340032 | tf_op jit(solution)/shard_map/scaled_product/pallas_call | solution.py:131
  46.6 5.5 %collective-permute-done.5 = bf16[96,3072]{1,0:T(8,128)(2,1)S(1)} collective-permute-done((bf16[96,3072]{1,0:T(8,128)(2,1)S(1)}, bf16[96,3072]{1,0:T(8,128)(2,1)S(1)}, u32[]{:S(2)}, u32[]{:S(2)}) %collective-permute-start.5) | collective-permute-done | bytes 589856 | tf_op jit(solution)/shard_map/ppermute | solution.py:42
  52.1 14.9 %collective-permute-done.6 = bf16[96,3072]{1,0:T(8,128)(2,1)S(1)} collective-permute-done((bf16[96,3072]{1,0:T(8,128)(2,1)S(1)}, bf16[96,3072]{1,0:T(8,128)(2,1)S(1)}, u32[]{:S(2)}, u32[]{:S(2)}) %collective-permute-start.6) | collective-permute-done | bytes 589856 | tf_op jit(solution)/shard_map/ppermute | solution.py:42
  66.9 2.0 collective-permute-done.7
  69.2 2.0 collective-permute-start.11
  71.7 1.5 collective-permute-start.15
  73.4 1.6 collective-permute-done.11
  75.1 2.6 %scaled_product.5 = f32[384,1152]{1,0:T(8,128)S(1)} custom-call(bf16[384,3072]{1,0:T(8,128)(2,1)S(1)} %constant_dynamic-update-slice_fusion.refs_0_, bf16[1024,512]{1,0:T(8,128)(2,1)S(1)} %get-tuple-element.113.refs_1_.refs_3_, bf16[1024,512]{1,0:T(8,128)(2,1)S(1)} %collective-permute-done.8.refs_2_, ...), custom_call_target="tpu_custom_call" | custom-call | flops 1610612736 | bytes 7340032 | tf_op jit(solution)/shard_map/scaled_product/pallas_call | solution.py:131
  79.6 3.2 %collective-permute-start.13 = (f16[96,2304]{1,0:T(8,128)(2,1)S(1)}, f16[96,2304]{1,0:T(8,128)(2,1)S(1)}, u32[]{:S(2)}, u32[]{:S(2)}) collective-permute-start(f16[96,2304]{1,0:T(8,128)(2,1)S(1)} %get-tuple-element.119), channel_id=1, source_target_pairs={{0,32},{1,33},{2,34},{3,35},{4,36},{5,37},{6,38},{7,39},{8,40},{9,... | collective-permute-start | bytes 1327112 | tf_op jit(solution)/shard_map/ppermute | solution.py:42
  82.9 2.6 %scaled_product.6 = f32[384,1152]{1,0:T(8,128)S(1)} custom-call(bf16[384,2048]{1,0:T(8,128)(2,1)S(1)} %constant_dynamic-update-slice_fusion.4.refs_0_, bf16[512,1024]{1,0:T(8,128)(2,1)S(1)} %collective-permute-done.refs_2_.refs_1_, bf16[512,1024]{1,0:T(8,128)(2,1)S(1)} %get-tuple-element.117.refs_1_.refs_2_, ...), custom_call_target="tpu_custom_call" | custom-call | flops 1610612736 | bytes 7340032 | tf_op jit(solution)/shard_map/scaled_product/pallas_call | solution.py:131
  85.6 4.6 %collective-permute-done.15.refs_1_ = bf16[384,1024]{1,0:T(8,128)(2,1)S(1)} collective-permute-done((bf16[384,1024]{1,0:T(8,128)(2,1)S(1)}, bf16[384,1024]{1,0:T(8,128)(2,1)S(1)}, u32[]{:S(2)}, u32[]{:S(2)}) %collective-permute-start.15) | collective-permute-done | bytes 786464 | tf_op jit(solution)/shard_map/ppermute | solution.py:42
  90.2 2.3 %collective-permute-done.16.refs_0_ = bf16[384,1024]{1,0:T(8,128)(2,1)S(1)} collective-permute-done((bf16[384,1024]{1,0:T(8,128)(2,1)S(1)}, bf16[384,1024]{1,0:T(8,128)(2,1)S(1)}, u32[]{:S(2)}, u32[]{:S(2)}) %collective-permute-start.16) | collective-permute-done | bytes 786464 | tf_op jit(solution)/shard_map/ppermute | solution.py:42
  92.6 7.9 %collective-permute-done.14 = f16[96,2304]{1,0:T(8,128)(2,1)S(1)} collective-permute-done((f16[96,2304]{1,0:T(8,128)(2,1)S(1)}, f16[96,2304]{1,0:T(8,128)(2,1)S(1)}, u32[]{:S(2)}, u32[]{:S(2)}) %collective-permute-start.14) | collective-permute-done | bytes 442400 | tf_op jit(solution)/shard_map/ppermute | solution.py:42
  100.5 2.7 %scaled_product.7 = f32[384,1152]{1,0:T(8,128)S(1)} custom-call(bf16[384,1024]{1,0:T(8,128)(2,1)S(1)} %collective-permute-done.16.refs_0_, bf16[384,1024]{1,0:T(8,128)(2,1)S(1)} %collective-permute-done.15.refs_1_, bf16[1024,512]{1,0:T(8,128)(2,1)S(1)} %collective-permute-done.8.refs_2_, bf16[1024,512]{1,0:T(8,128)(2,1)S(1)} %get-tuple-element.113.refs_1_.refs_3_, ...), custom_call_target="tpu_custom_call" | custom-call | flops 1610612736 | bytes 7340032 | tf_op jit(solution)/shard_map/scaled_product/pallas_call | solution.py:131
  105.7 3.8 %collective-permute-start.18 = (f16[96,2304]{1,0:T(8,128)(2,1)S(1)}, f16[96,2304]{1,0:T(8,128)(2,1)S(1)}, u32[]{:S(2)}, u32[]{:S(2)}) collective-permute-start(f16[96,2304]{1,0:T(8,128)(2,1)S(1)} %get-tuple-element.126), channel_id=1, source_target_pairs={{0,32},{1,33},{2,34},{3,35},{4,36},{5,37},{6,38},{7,39},{8,40},{9,... | collective-permute-start | bytes 1327112 | tf_op jit(solution)/shard_map/ppermute | solution.py:42
  110.8 6.2 %collective-permute-done.19 = f16[96,2304]{1,0:T(8,128)(2,1)S(1)} collective-permute-done((f16[96,2304]{1,0:T(8,128)(2,1)S(1)}, f16[96,2304]{1,0:T(8,128)(2,1)S(1)}, u32[]{:S(2)}, u32[]{:S(2)}) %collective-permute-start.19) | collective-permute-done | bytes 442400 | tf_op jit(solution)/shard_map/ppermute | solution.py:42
  117.0 10.4 %collective-permute-done.18 = f16[96,2304]{1,0:T(8,128)(2,1)S(1)} collective-permute-done((f16[96,2304]{1,0:T(8,128)(2,1)S(1)}, f16[96,2304]{1,0:T(8,128)(2,1)S(1)}, u32[]{:S(2)}, u32[]{:S(2)}) %collective-permute-start.18) | collective-permute-done | bytes 442400 | tf_op jit(solution)/shard_map/ppermute | solution.py:42
  129.1 5.5 %collective-permute-start.21 = (bf16[2,96,1024]{2,1,0:T(8,128)(2,1)S(1)}, bf16[2,96,1024]{2,1,0:T(8,128)(2,1)S(1)}, u32[]{:S(2)}, u32[]{:S(2)}) collective-permute-start(bf16[2,96,1024]{2,1,0:T(8,128)(2,1)S(1)} %get-tuple-element.184), channel_id=1, source_target_pairs={{0,0},{1,1},{2,2},{3,3},{4,4},{5,5},{6,6},{7,7},{8,12},{9,13},{10,... | collective-permute-start | bytes 1179656 | tf_op jit(solution)/shard_map/ppermute | solution.py:42
  134.8 4.9 %collective-permute-done.21 = bf16[2,96,1024]{2,1,0:T(8,128)(2,1)S(1)} collective-permute-done((bf16[2,96,1024]{2,1,0:T(8,128)(2,1)S(1)}, bf16[2,96,1024]{2,1,0:T(8,128)(2,1)S(1)}, u32[]{:S(2)}, u32[]{:S(2)}) %collective-permute-start.21) | collective-permute-done | bytes 393248 | tf_op jit(solution)/shard_map/ppermute | solution.py:42
  139.8 4.0 %collective-permute-start.22 = (bf16[2,96,1024]{2,1,0:T(8,128)(2,1)S(1)}, bf16[2,96,1024]{2,1,0:T(8,128)(2,1)S(1)}, u32[]{:S(2)}, u32[]{:S(2)}) collective-permute-start(bf16[2,96,1024]{2,1,0:T(8,128)(2,1)S(1)} %collective-permute-done.21), channel_id=1, source_target_pairs={{0,0},{1,17},{2,34},{3,51},{4,68},{5,85},{6,102},{7,119},{8,64},{9... | collective-permute-start | bytes 1179656 | tf_op jit(solution)/shard_map/ppermute | solution.py:42
  144.0 5.9 %collective-permute-done.24 = bf16[2,96,1024]{2,1,0:T(8,128)(2,1)S(1)} collective-permute-done((bf16[2,96,1024]{2,1,0:T(8,128)(2,1)S(1)}, bf16[2,96,1024]{2,1,0:T(8,128)(2,1)S(1)}, u32[]{:S(2)}, u32[]{:S(2)}) %collective-permute-start.24) | collective-permute-done | bytes 393248 | tf_op jit(solution)/shard_map/ppermute | solution.py:42
  150.0 6.1 %collective-permute-done.23 = bf16[2,96,1024]{2,1,0:T(8,128)(2,1)S(1)} collective-permute-done((bf16[2,96,1024]{2,1,0:T(8,128)(2,1)S(1)}, bf16[2,96,1024]{2,1,0:T(8,128)(2,1)S(1)}, u32[]{:S(2)}, u32[]{:S(2)}) %collective-permute-start.23) | collective-permute-done | bytes 393248 | tf_op jit(solution)/shard_map/ppermute | solution.py:42
  156.0 3.0 %collective-permute-done.22 = bf16[2,96,1024]{2,1,0:T(8,128)(2,1)S(1)} collective-permute-done((bf16[2,96,1024]{2,1,0:T(8,128)(2,1)S(1)}, bf16[2,96,1024]{2,1,0:T(8,128)(2,1)S(1)}, u32[]{:S(2)}, u32[]{:S(2)}) %collective-permute-start.22) | collective-permute-done | bytes 393248 | tf_op jit(solution)/shard_map/ppermute | solution.py:42
  159.1 7.4 %collective-permute-start.27 = (bf16[2,2,96,1024]{3,2,1,0:T(8,128)(2,1)S(1)}, bf16[2,2,96,1024]{3,2,1,0:T(8,128)(2,1)S(1)}, u32[]{:S(2)}, u32[]{:S(2)}) collective-permute-start(bf16[2,2,96,1024]{3,2,1,0:T(8,128)(2,1)S(1)} %pad_maximum_fusion.8), channel_id=1, source_target_pairs={{0,48},{1,49},{2,50},{3,51},{4,52},{5,53},{6,54},{7,55},{8,56},{9,... | collective-permute-start | bytes 2359304 | tf_op jit(solution)/shard_map/ppermute | solution.py:42
  166.5 2.9 %collective-permute-start.29 = (bf16[2,2,96,1024]{3,2,1,0:T(8,128)(2,1)S(1)}, bf16[2,2,96,1024]{3,2,1,0:T(8,128)(2,1)S(1)}, u32[]{:S(2)}, u32[]{:S(2)}) collective-permute-start(bf16[2,2,96,1024]{3,2,1,0:T(8,128)(2,1)S(1)} %pad_maximum_fusion.7.refs_4_), channel_id=1, source_target_pairs={{0,6},{1,7},{2,4},{3,5},{4,2},{5,3},{6,0},{7,1},{8,14},{9,15},{10,... | collective-permute-start | bytes 2359304 | tf_op jit(solution)/shard_map/ppermute | solution.py:42
  170.1 3.1 %input_gram.1 = f32[512,1024]{1,0:T(8,128)} custom-call(bf16[1536,512]{1,0:T(8,128)(2,1)S(1)} %bitcast.99, bf16[1536,1024]{1,0:T(8,128)(2,1)S(1)} %bitcast.96), custom_call_target="tpu_custom_call" | custom-call | flops 1610612736 | bytes 6815744 | tf_op jit(solution)/shard_map/input_gram/pallas_call | solution.py:154
  173.2 10.1 %collective-permute-done.27 = bf16[2,2,96,1024]{3,2,1,0:T(8,128)(2,1)S(1)} collective-permute-done((bf16[2,2,96,1024]{3,2,1,0:T(8,128)(2,1)S(1)}, bf16[2,2,96,1024]{3,2,1,0:T(8,128)(2,1)S(1)}, u32[]{:S(2)}, u32[]{:S(2)}) %collective-permute-start.27) | collective-permute-done | bytes 786464 | tf_op jit(solution)/shard_map/ppermute | solution.py:42
  183.3 2.0 collective-permute-done.26
  185.3 1.7 collective-permute-done.29.refs_8_
  188.1 1.6 collective-permute-start.34
  189.9 1.9 collective-permute-start.32
  193.4 6.7 %collective-permute-done.33 = bf16[2,96,1024]{2,1,0:T(8,128)(2,1)S(1)} collective-permute-done((bf16[2,96,1024]{2,1,0:T(8,128)(2,1)S(1)}, bf16[2,96,1024]{2,1,0:T(8,128)(2,1)S(1)}, u32[]{:S(2)}, u32[]{:S(2)}) %collective-permute-start.33) | collective-permute-done | bytes 393248 | tf_op jit(solution)/shard_map/ppermute | solution.py:42
  201.5 2.4 %collective-permute-done.30 = bf16[2,96,1024]{2,1,0:T(8,128)(2,1)S(1)} collective-permute-done((bf16[2,96,1024]{2,1,0:T(8,128)(2,1)S(1)}, bf16[2,96,1024]{2,1,0:T(8,128)(2,1)S(1)}, u32[]{:S(2)}, u32[]{:S(2)}) %collective-permute-start.30) | collective-permute-done | bytes 393248 | tf_op jit(solution)/shard_map/ppermute | solution.py:42
  204.0 2.5 %collective-permute-start.35 = (bf16[1,2,2,96,1024]{4,3,2,1,0:T(8,128)(2,1)S(1)}, bf16[1,2,2,96,1024]{4,3,2,1,0:T(8,128)(2,1)}, u32[]{:S(2)}, u32[]{:S(2)}) collective-permute-start(bf16[1,2,2,96,1024]{4,3,2,1,0:T(8,128)(2,1)S(1)} %maximum_bitcast_fusion.2.refs_1_), channel_id=1, source_target_pairs={{0,8},{1,9},{2,10},{3,11},{4,12},{5,13},{6,14},{7,15},{8,0},{9,1},... | collective-permute-start | bytes 2359304 | tf_op jit(solution)/shard_map/ppermute | solution.py:42
  208.6 13.2 %grad_gram.1 = f32[2048,1024]{1,0:T(8,128)} custom-call(s32[17]{0:T(128)} %stack.212.places, bf16[3,2,2,96,1024]{4,3,2,1,0:T(8,128)(2,1)} %copy-done, bf16[1,2,2,96,1024]{4,3,2,1,0:T(8,128)(2,1)} %copy-done.9, bf16[3,2,2,96,1024]{4,3,2,1,0:T(8,128)(2,1)} %collective-permute-done.34.refs_2_, bf16[1,2,2,96,1024]{4,3,2,1,0:T(8,128)(2,1)} %collective-permute-done.35.refs_3_, ...), custom_call_target="tpu_custom_call" | custom-call | flops 6442450944 | bytes 17825792 | tf_op jit(solution)/shard_map/grad_gram/pallas_call | solution.py:214
  (139 shorter events, 24.6 us)
Async XLA Ops:
  3.3 4.4 %copy-start.3 = (bf16[96,512]{1,0:T(8,128)(2,1)}, bf16[96,512]{1,0:T(8,128)(2,1)S(1)}, u32[]{:S(2)}) copy-start(bf16[96,512]{1,0:T(8,128)(2,1)S(1)} %get-tuple-element.188) | copy-start | bytes 294916
  3.4 3.2 %copy-start.1 = (bf16[512,2048]{1,0:T(8,128)(2,1)S(1)}, bf16[512,2048]{1,0:T(8,128)(2,1)}, u32[]{:S(2)}) copy-start(bf16[512,2048]{1,0:T(8,128)(2,1)} %param.6) | copy-start | bytes 6291460
  7.7 25.2 %collective-permute-start = (bf16[512,1024]{1,0:T(8,128)(2,1)}, bf16[512,1024]{1,0:T(8,128)(2,1)S(1)}, u32[]{:S(2)}, u32[]{:S(2)}) collective-permute-start(bf16[512,1024]{1,0:T(8,128)(2,1)} %get-tuple-element.118), channel_id=1, source_target_pairs={{0,64},{1,65},{2,66},{3,67},{4,68},{5,69},{6,70},{7,71},{8,72},{9,... | collective-permute-start | bytes 3145736 | tf_op jit(solution)/shard_map/ppermute | solution.py:42
  9.9 13.1 %collective-permute-start.1 = (bf16[96,2048]{1,0:T(8,128)(2,1)}, bf16[96,2048]{1,0:T(8,128)(2,1)}, u32[]{:S(2)}, u32[]{:S(2)}) collective-permute-start(bf16[96,2048]{1,0:T(8,128)(2,1)} %pad_maximum_fusion.11), channel_id=1, source_target_pairs={{0,65},{1,64},{2,67},{3,66},{4,69},{5,68},{6,71},{7,70},{8,73},{9,... | collective-permute-start | bytes 1179656 | tf_op jit(solution)/shard_map/ppermute | solution.py:42
  11.8 11.2 %collective-permute-start.3 = (bf16[96,2048]{1,0:T(8,128)(2,1)}, bf16[96,2048]{1,0:T(8,128)(2,1)S(1)}, u32[]{:S(2)}, u32[]{:S(2)}) collective-permute-start(bf16[96,2048]{1,0:T(8,128)(2,1)} %pad_maximum_fusion.13), channel_id=1, source_target_pairs={{0,32},{1,33},{2,34},{3,35},{4,36},{5,37},{6,38},{7,39},{8,40},{9,... | collective-permute-start | bytes 1179656 | tf_op jit(solution)/shard_map/ppermute | solution.py:42
  14.5 16.9 %collective-permute-start.2 = (bf16[96,2048]{1,0:T(8,128)(2,1)}, bf16[96,2048]{1,0:T(8,128)(2,1)S(1)}, u32[]{:S(2)}, u32[]{:S(2)}) collective-permute-start(bf16[96,2048]{1,0:T(8,128)(2,1)} %pad_maximum_fusion.12), channel_id=1, source_target_pairs={{0,16},{1,17},{2,18},{3,19},{4,20},{5,21},{6,22},{7,23},{8,24},{9,... | collective-permute-start | bytes 1179656 | tf_op jit(solution)/shard_map/ppermute | solution.py:42
  14.8 18.1 %collective-permute-start.4 = (bf16[96,2048]{1,0:T(8,128)(2,1)}, bf16[96,2048]{1,0:T(8,128)(2,1)S(1)}, u32[]{:S(2)}, u32[]{:S(2)}) collective-permute-start(bf16[96,2048]{1,0:T(8,128)(2,1)} %pad_maximum_fusion.14), channel_id=1, source_target_pairs={{0,48},{1,49},{2,50},{3,51},{4,52},{5,53},{6,54},{7,55},{8,56},{9,... | collective-permute-start | bytes 1179656 | tf_op jit(solution)/shard_map/ppermute | solution.py:42
  15.4 7.5 %copy-start.2 = (bf16[2048,512]{1,0:T(8,128)(2,1)S(1)}, bf16[2048,512]{1,0:T(8,128)(2,1)}, u32[]{:S(2)}) copy-start(bf16[2048,512]{1,0:T(8,128)(2,1)} %param.7) | copy-start | bytes 6291460
  33.2 4.4 %copy-start.14 = (bf16[96,3072]{1,0:T(8,128)(2,1)S(1)}, bf16[96,3072]{1,0:T(8,128)(2,1)}, u32[]{:S(2)}) copy-start(bf16[96,3072]{1,0:T(8,128)(2,1)} %get-tuple-element.56) | copy-start | bytes 1769476
  33.2 5.6 %copy-start.13 = (bf16[96,3072]{1,0:T(8,128)(2,1)S(1)}, bf16[96,3072]{1,0:T(8,128)(2,1)}, u32[]{:S(2)}) copy-start(bf16[96,3072]{1,0:T(8,128)(2,1)} %get-tuple-element.57) | copy-start | bytes 1769476
  33.2 8.1 %copy-start.12 = (bf16[96,3072]{1,0:T(8,128)(2,1)S(1)}, bf16[96,3072]{1,0:T(8,128)(2,1)}, u32[]{:S(2)}) copy-start(bf16[96,3072]{1,0:T(8,128)(2,1)} %get-tuple-element.58) | copy-start | bytes 1769476
  33.2 8.3 %copy-start.4 = (bf16[96,512]{1,0:T(8,128)(2,1)S(1)}, bf16[96,512]{1,0:T(8,128)(2,1)}, u32[]{:S(2)}) copy-start(bf16[96,512]{1,0:T(8,128)(2,1)} %copy-done.3) | copy-start | bytes 294916
  33.2 8.3 %copy-start.6 = (bf16[96,512]{1,0:T(8,128)(2,1)S(1)}, bf16[96,512]{1,0:T(8,128)(2,1)}, u32[]{:S(2)}) copy-start(bf16[96,512]{1,0:T(8,128)(2,1)} %copy-done.5) | copy-start | bytes 294916
  33.2 8.1 %collective-permute-start.10 = (bf16[2,512,1024]{2,1,0:T(8,128)(2,1)S(1)}, bf16[2,512,1024]{2,1,0:T(8,128)(2,1)S(1)}, u32[]{:S(2)}, u32[]{:S(2)}) collective-permute-start(bf16[2,512,1024]{2,1,0:T(8,128)(2,1)S(1)} %pad_maximum_fusion.2), channel_id=1, source_target_pairs={{0,8},{1,9},{2,10},{3,11},{4,12},{5,13},{6,14},{7,15},{8,0},{9,1},... | collective-permute-start | bytes 6291464 | tf_op jit(solution)/shard_map/ppermute | solution.py:42
  34.6 34.3 %collective-permute-start.9 = (bf16[288,2048]{1,0:T(8,128)(2,1)S(1)}, bf16[288,2048]{1,0:T(8,128)(2,1)S(1)}, u32[]{:S(2)}, u32[]{:S(2)}) collective-permute-start(bf16[288,2048]{1,0:T(8,128)(2,1)S(1)} %pad_maximum_fusion.6), channel_id=1, source_target_pairs={{0,65},{1,64},{2,67},{3,66},{4,69},{5,68},{6,71},{7,70},{8,73},{9,... | collective-permute-start | bytes 3538952 | tf_op jit(solution)/shard_map/ppermute | solution.py:42
  37.6 31.4 %collective-permute-start.8 = (bf16[1024,512]{1,0:T(8,128)(2,1)S(1)}, bf16[1024,512]{1,0:T(8,128)(2,1)S(1)}, u32[]{:S(2)}, u32[]{:S(2)}) collective-permute-start(bf16[1024,512]{1,0:T(8,128)(2,1)S(1)} %get-tuple-element.59), channel_id=1, source_target_pairs={{0,64},{1,65},{2,66},{3,67},{4,68},{5,69},{6,70},{7,71},{8,72},{9,... | collective-permute-start | bytes 3145736 | tf_op jit(solution)/shard_map/ppermute | solution.py:42
  37.6 14.5 %collective-permute-start.5 = (bf16[96,3072]{1,0:T(8,128)(2,1)S(1)}, bf16[96,3072]{1,0:T(8,128)(2,1)S(1)}, u32[]{:S(2)}, u32[]{:S(2)}) collective-permute-start(bf16[96,3072]{1,0:T(8,128)(2,1)S(1)} %copy-done.14), channel_id=1, source_target_pairs={{0,16},{1,17},{2,18},{3,19},{4,20},{5,21},{6,22},{7,23},{8,24},{9,... | collective-permute-start | bytes 1769480 | tf_op jit(solution)/shard_map/ppermute | solution.py:42
  38.8 28.1 %collective-permute-start.6 = (bf16[96,3072]{1,0:T(8,128)(2,1)S(1)}, bf16[96,3072]{1,0:T(8,128)(2,1)S(1)}, u32[]{:S(2)}, u32[]{:S(2)}) collective-permute-start(bf16[96,3072]{1,0:T(8,128)(2,1)S(1)} %copy-done.13), channel_id=1, source_target_pairs={{0,32},{1,33},{2,34},{3,35},{4,36},{5,37},{6,38},{7,39},{8,40},{9,... | collective-permute-start | bytes 1769480 | tf_op jit(solution)/shard_map/ppermute | solution.py:42
  41.3 27.7 %collective-permute-start.7 = (bf16[96,3072]{1,0:T(8,128)(2,1)S(1)}, bf16[96,3072]{1,0:T(8,128)(2,1)S(1)}, u32[]{:S(2)}, u32[]{:S(2)}) collective-permute-start(bf16[96,3072]{1,0:T(8,128)(2,1)S(1)} %copy-done.12), channel_id=1, source_target_pairs={{0,48},{1,49},{2,50},{3,51},{4,52},{5,53},{6,54},{7,55},{8,56},{9,... | collective-permute-start | bytes 1769480 | tf_op jit(solution)/shard_map/ppermute | solution.py:42
  69.2 5.8 %collective-permute-start.11 = (bf16[2,1024,512]{2,1,0:T(8,128)(2,1)S(1)}, bf16[2,1024,512]{2,1,0:T(8,128)(2,1)S(1)}, u32[]{:S(2)}, u32[]{:S(2)}) collective-permute-start(bf16[2,1024,512]{2,1,0:T(8,128)(2,1)S(1)} %pad_maximum_fusion.3), channel_id=1, source_target_pairs={{0,8},{1,9},{2,10},{3,11},{4,12},{5,13},{6,14},{7,15},{8,0},{9,1},... | collective-permute-start | bytes 6291464 | tf_op jit(solution)/shard_map/ppermute | solution.py:42
  71.7 18.5 %collective-permute-start.15 = (bf16[384,1024]{1,0:T(8,128)(2,1)S(1)}, bf16[384,1024]{1,0:T(8,128)(2,1)S(1)}, u32[]{:S(2)}, u32[]{:S(2)}) collective-permute-start(bf16[384,1024]{1,0:T(8,128)(2,1)S(1)} %get-tuple-element.71), channel_id=1, source_target_pairs={{0,64},{1,65},{2,66},{3,67},{4,68},{5,69},{6,70},{7,71},{8,72},{9,... | collective-permute-start | bytes 2359304 | tf_op jit(solution)/shard_map/ppermute | solution.py:42
  73.3 19.3 %collective-permute-start.16 = (bf16[384,1024]{1,0:T(8,128)(2,1)S(1)}, bf16[384,1024]{1,0:T(8,128)(2,1)S(1)}, u32[]{:S(2)}, u32[]{:S(2)}) collective-permute-start(bf16[384,1024]{1,0:T(8,128)(2,1)S(1)} %get-tuple-element.72), channel_id=1, source_target_pairs={{0,65},{1,64},{2,67},{3,66},{4,69},{5,68},{6,71},{7,70},{8,73},{9,... | collective-permute-start | bytes 2359304 | tf_op jit(solution)/shard_map/ppermute | solution.py:42
  78.2 14.3 %collective-permute-start.12 = (f16[96,2304]{1,0:T(8,128)(2,1)S(1)}, f16[96,2304]{1,0:T(8,128)(2,1)S(1)}, u32[]{:S(2)}, u32[]{:S(2)}) collective-permute-start(f16[96,2304]{1,0:T(8,128)(2,1)S(1)} %get-tuple-element.121), channel_id=1, source_target_pairs={{0,16},{1,17},{2,18},{3,19},{4,20},{5,21},{6,22},{7,23},{8,24},{9,... | collective-permute-start | bytes 1327112 | tf_op jit(solution)/shard_map/ppermute | solution.py:42
  78.3 22.2 %collective-permute-start.14 = (f16[96,2304]{1,0:T(8,128)(2,1)S(1)}, f16[96,2304]{1,0:T(8,128)(2,1)S(1)}, u32[]{:S(2)}, u32[]{:S(2)}) collective-permute-start(f16[96,2304]{1,0:T(8,128)(2,1)S(1)} %get-tuple-element.122), channel_id=1, source_target_pairs={{0,48},{1,49},{2,50},{3,51},{4,52},{5,53},{6,54},{7,55},{8,56},{9,... | collective-permute-start | bytes 1327112 | tf_op jit(solution)/shard_map/ppermute | solution.py:42
  79.6 23.6 %collective-permute-start.13 = (f16[96,2304]{1,0:T(8,128)(2,1)S(1)}, f16[96,2304]{1,0:T(8,128)(2,1)S(1)}, u32[]{:S(2)}, u32[]{:S(2)}) collective-permute-start(f16[96,2304]{1,0:T(8,128)(2,1)S(1)} %get-tuple-element.119), channel_id=1, source_target_pairs={{0,32},{1,33},{2,34},{3,35},{4,36},{5,37},{6,38},{7,39},{8,40},{9,... | collective-permute-start | bytes 1327112 | tf_op jit(solution)/shard_map/ppermute | solution.py:42
  103.6 23.8 %collective-permute-start.20 = (bf16[384,1024]{1,0:T(8,128)(2,1)S(1)}, bf16[384,1024]{1,0:T(8,128)(2,1)S(1)}, u32[]{:S(2)}, u32[]{:S(2)}) collective-permute-start(bf16[384,1024]{1,0:T(8,128)(2,1)S(1)} %get-tuple-element.83), channel_id=1, source_target_pairs={{0,64},{1,65},{2,66},{3,67},{4,68},{5,69},{6,70},{7,71},{8,72},{9,... | collective-permute-start | bytes 2359304 | tf_op jit(solution)/shard_map/ppermute | solution.py:42
  105.5 11.5 %collective-permute-start.19 = (f16[96,2304]{1,0:T(8,128)(2,1)S(1)}, f16[96,2304]{1,0:T(8,128)(2,1)S(1)}, u32[]{:S(2)}, u32[]{:S(2)}) collective-permute-start(f16[96,2304]{1,0:T(8,128)(2,1)S(1)} %get-tuple-element.123), channel_id=1, source_target_pairs={{0,48},{1,49},{2,50},{3,51},{4,52},{5,53},{6,54},{7,55},{8,56},{9,... | collective-permute-start | bytes 1327112 | tf_op jit(solution)/shard_map/ppermute | solution.py:42
  105.6 11.4 %collective-permute-start.17 = (f16[96,2304]{1,0:T(8,128)(2,1)S(1)}, f16[96,2304]{1,0:T(8,128)(2,1)S(1)}, u32[]{:S(2)}, u32[]{:S(2)}) collective-permute-start(f16[96,2304]{1,0:T(8,128)(2,1)S(1)} %get-tuple-element.125), channel_id=1, source_target_pairs={{0,16},{1,17},{2,18},{3,19},{4,20},{5,21},{6,22},{7,23},{8,24},{9,... | collective-permute-start | bytes 1327112 | tf_op jit(solution)/shard_map/ppermute | solution.py:42
  105.7 21.7 %collective-permute-start.18 = (f16[96,2304]{1,0:T(8,128)(2,1)S(1)}, f16[96,2304]{1,0:T(8,128)(2,1)S(1)}, u32[]{:S(2)}, u32[]{:S(2)}) collective-permute-start(f16[96,2304]{1,0:T(8,128)(2,1)S(1)} %get-tuple-element.126), channel_id=1, source_target_pairs={{0,32},{1,33},{2,34},{3,35},{4,36},{5,37},{6,38},{7,39},{8,40},{9,... | collective-permute-start | bytes 1327112 | tf_op jit(solution)/shard_map/ppermute | solution.py:42
  129.1 10.7 %collective-permute-start.21 = (bf16[2,96,1024]{2,1,0:T(8,128)(2,1)S(1)}, bf16[2,96,1024]{2,1,0:T(8,128)(2,1)S(1)}, u32[]{:S(2)}, u32[]{:S(2)}) collective-permute-start(bf16[2,96,1024]{2,1,0:T(8,128)(2,1)S(1)} %get-tuple-element.184), channel_id=1, source_target_pairs={{0,0},{1,1},{2,2},{3,3},{4,4},{5,5},{6,6},{7,7},{8,12},{9,13},{10,... | collective-permute-start | bytes 1179656 | tf_op jit(solution)/shard_map/ppermute | solution.py:42
  139.7 19.4 %collective-permute-start.25 = (bf16[2,384,1536]{2,1,0:T(8,128)(2,1)S(1)}, bf16[2,384,1536]{2,1,0:T(8,128)(2,1)S(1)}, u32[]{:S(2)}, u32[]{:S(2)}) collective-permute-start(bf16[2,384,1536]{2,1,0:T(8,128)(2,1)S(1)} %maximum_maximum_fusion), channel_id=1, source_target_pairs={{0,8},{1,9},{2,10},{3,11},{4,12},{5,13},{6,14},{7,15},{8,0},{9,1},... | collective-permute-start | bytes 7077896 | tf_op jit(solution)/shard_map/ppermute | solution.py:42
  139.7 10.2 %collective-permute-start.24 = (bf16[2,96,1024]{2,1,0:T(8,128)(2,1)S(1)}, bf16[2,96,1024]{2,1,0:T(8,128)(2,1)S(1)}, u32[]{:S(2)}, u32[]{:S(2)}) collective-permute-start(bf16[2,96,1024]{2,1,0:T(8,128)(2,1)S(1)} %get-tuple-element.184), channel_id=1, source_target_pairs={{0,64},{1,65},{2,66},{3,67},{4,68},{5,69},{6,70},{7,71},{8,72},{9,... | collective-permute-start | bytes 1179656 | tf_op jit(solution)/shard_map/ppermute | solution.py:42
  139.8 16.3 %collective-permute-start.23 = (bf16[2,96,1024]{2,1,0:T(8,128)(2,1)S(1)}, bf16[2,96,1024]{2,1,0:T(8,128)(2,1)S(1)}, u32[]{:S(2)}, u32[]{:S(2)}) collective-permute-start(bf16[2,96,1024]{2,1,0:T(8,128)(2,1)S(1)} %collective-permute-done.21), channel_id=1, source_target_pairs={{0,1},{1,16},{2,35},{3,50},{4,69},{5,84},{6,103},{7,118},{8,65},{9... | collective-permute-start | bytes 1179656 | tf_op jit(solution)/shard_map/ppermute | solution.py:42
  139.8 19.2 %collective-permute-start.22 = (bf16[2,96,1024]{2,1,0:T(8,128)(2,1)S(1)}, bf16[2,96,1024]{2,1,0:T(8,128)(2,1)S(1)}, u32[]{:S(2)}, u32[]{:S(2)}) collective-permute-start(bf16[2,96,1024]{2,1,0:T(8,128)(2,1)S(1)} %collective-permute-done.21), channel_id=1, source_target_pairs={{0,0},{1,17},{2,34},{3,51},{4,68},{5,85},{6,102},{7,119},{8,64},{9... | collective-permute-start | bytes 1179656 | tf_op jit(solution)/shard_map/ppermute | solution.py:42
  159.1 10.5 %copy-start.8 = (bf16[2,2,96,1024]{3,2,1,0:T(8,128)(2,1)}, bf16[2,2,96,1024]{3,2,1,0:T(8,128)(2,1)S(1)}, u32[]{:S(2)}) copy-start(bf16[2,2,96,1024]{3,2,1,0:T(8,128)(2,1)S(1)} %pad_maximum_fusion.7.refs_4_) | copy-start | bytes 2359300
  159.1 24.2 %collective-permute-start.27 = (bf16[2,2,96,1024]{3,2,1,0:T(8,128)(2,1)S(1)}, bf16[2,2,96,1024]{3,2,1,0:T(8,128)(2,1)S(1)}, u32[]{:S(2)}, u32[]{:S(2)}) collective-permute-start(bf16[2,2,96,1024]{3,2,1,0:T(8,128)(2,1)S(1)} %pad_maximum_fusion.8), channel_id=1, source_target_pairs={{0,48},{1,49},{2,50},{3,51},{4,52},{5,53},{6,54},{7,55},{8,56},{9,... | collective-permute-start | bytes 2359304 | tf_op jit(solution)/shard_map/ppermute | solution.py:42
  166.5 18.8 %collective-permute-start.26 = (bf16[2,2,96,1024]{3,2,1,0:T(8,128)(2,1)S(1)}, bf16[2,2,96,1024]{3,2,1,0:T(8,128)(2,1)S(1)}, u32[]{:S(2)}, u32[]{:S(2)}) collective-permute-start(bf16[2,2,96,1024]{3,2,1,0:T(8,128)(2,1)S(1)} %pad_maximum_fusion.8), channel_id=1, source_target_pairs={{0,16},{1,17},{2,18},{3,19},{4,20},{5,21},{6,22},{7,23},{8,24},{9,... | collective-permute-start | bytes 2359304 | tf_op jit(solution)/shard_map/ppermute | solution.py:42
  166.5 20.5 %collective-permute-start.29 = (bf16[2,2,96,1024]{3,2,1,0:T(8,128)(2,1)S(1)}, bf16[2,2,96,1024]{3,2,1,0:T(8,128)(2,1)S(1)}, u32[]{:S(2)}, u32[]{:S(2)}) collective-permute-start(bf16[2,2,96,1024]{3,2,1,0:T(8,128)(2,1)S(1)} %pad_maximum_fusion.7.refs_4_), channel_id=1, source_target_pairs={{0,6},{1,7},{2,4},{3,5},{4,2},{5,3},{6,0},{7,1},{8,14},{9,15},{10,... | collective-permute-start | bytes 2359304 | tf_op jit(solution)/shard_map/ppermute | solution.py:42
  169.4 18.4 %collective-permute-start.28 = (bf16[2,2,96,1024]{3,2,1,0:T(8,128)(2,1)S(1)}, bf16[2,2,96,1024]{3,2,1,0:T(8,128)(2,1)S(1)}, u32[]{:S(2)}, u32[]{:S(2)}) collective-permute-start(bf16[2,2,96,1024]{3,2,1,0:T(8,128)(2,1)S(1)} %pad_maximum_fusion.7.refs_4_), channel_id=1, source_target_pairs={{0,2},{1,3},{2,0},{3,1},{4,6},{5,7},{6,4},{7,5},{8,10},{9,11},{10,... | collective-permute-start | bytes 2359304 | tf_op jit(solution)/shard_map/ppermute | solution.py:42
  188.1 15.9 %copy-start = (bf16[3,2,2,96,1024]{4,3,2,1,0:T(8,128)(2,1)}, bf16[3,2,2,96,1024]{4,3,2,1,0:T(8,128)(2,1)S(1)}, u32[]{:S(2)}) copy-start(bf16[3,2,2,96,1024]{4,3,2,1,0:T(8,128)(2,1)S(1)} %pad_maximum_fusion.1.refs_0_) | copy-start | bytes 7077892
  188.1 20.4 %collective-permute-start.34 = (bf16[3,2,2,96,1024]{4,3,2,1,0:T(8,128)(2,1)S(1)}, bf16[3,2,2,96,1024]{4,3,2,1,0:T(8,128)(2,1)}, u32[]{:S(2)}, u32[]{:S(2)}) collective-permute-start(bf16[3,2,2,96,1024]{4,3,2,1,0:T(8,128)(2,1)S(1)} %pad_maximum_fusion.1.refs_0_), channel_id=1, source_target_pairs={{0,8},{1,9},{2,10},{3,11},{4,12},{5,13},{6,14},{7,15},{8,0},{9,1},... | collective-permute-start | bytes 7077896 | tf_op jit(solution)/shard_map/ppermute | solution.py:42
  189.9 10.3 %collective-permute-start.33 = (bf16[2,96,1024]{2,1,0:T(8,128)(2,1)S(1)}, bf16[2,96,1024]{2,1,0:T(8,128)(2,1)S(1)}, u32[]{:S(2)}, u32[]{:S(2)}) collective-permute-start(bf16[2,96,1024]{2,1,0:T(8,128)(2,1)S(1)} %slice_bitcast_fusion.10), channel_id=1, source_target_pairs={{0,2},{1,3},{2,0},{3,1},{4,6},{5,7},{6,4},{7,5},{8,10},{9,11},{10,... | collective-permute-start | bytes 1179656 | tf_op jit(solution)/shard_map/ppermute | solution.py:42
  189.9 11.1 %collective-permute-start.32 = (bf16[2,96,1024]{2,1,0:T(8,128)(2,1)S(1)}, bf16[2,96,1024]{2,1,0:T(8,128)(2,1)S(1)}, u32[]{:S(2)}, u32[]{:S(2)}) collective-permute-start(bf16[2,96,1024]{2,1,0:T(8,128)(2,1)S(1)} %slice_bitcast_fusion.11), channel_id=1, source_target_pairs={{0,6},{1,7},{2,4},{3,5},{4,2},{5,3},{6,0},{7,1},{8,14},{9,15},{10,... | collective-permute-start | bytes 1179656 | tf_op jit(solution)/shard_map/ppermute | solution.py:42
  191.9 9.6 %collective-permute-start.31 = (bf16[2,96,1024]{2,1,0:T(8,128)(2,1)S(1)}, bf16[2,96,1024]{2,1,0:T(8,128)(2,1)S(1)}, u32[]{:S(2)}, u32[]{:S(2)}) collective-permute-start(bf16[2,96,1024]{2,1,0:T(8,128)(2,1)S(1)} %slice_bitcast_fusion.12), channel_id=1, source_target_pairs={{0,16},{1,17},{2,18},{3,19},{4,20},{5,21},{6,22},{7,23},{8,24},{9,... | collective-permute-start | bytes 1179656 | tf_op jit(solution)/shard_map/ppermute | solution.py:42
  193.4 10.5 %collective-permute-start.30 = (bf16[2,96,1024]{2,1,0:T(8,128)(2,1)S(1)}, bf16[2,96,1024]{2,1,0:T(8,128)(2,1)S(1)}, u32[]{:S(2)}, u32[]{:S(2)}) collective-permute-start(bf16[2,96,1024]{2,1,0:T(8,128)(2,1)S(1)} %slice_bitcast_fusion.13), channel_id=1, source_target_pairs={{0,48},{1,49},{2,50},{3,51},{4,52},{5,53},{6,54},{7,55},{8,56},{9,... | collective-permute-start | bytes 1179656 | tf_op jit(solution)/shard_map/ppermute | solution.py:42
  200.2 8.4 %copy-start.15 = (bf16[2,96,1024]{2,1,0:T(8,128)(2,1)}, bf16[2,96,1024]{2,1,0:T(8,128)(2,1)S(1)}, u32[]{:S(2)}) copy-start(bf16[2,96,1024]{2,1,0:T(8,128)(2,1)S(1)} %collective-permute-done.33) | copy-start | bytes 1179652
  204.0 4.6 %copy-start.9 = (bf16[1,2,2,96,1024]{4,3,2,1,0:T(8,128)(2,1)}, bf16[1,2,2,96,1024]{4,3,2,1,0:T(8,128)(2,1)S(1)}, u32[]{:S(2)}) copy-start(bf16[1,2,2,96,1024]{4,3,2,1,0:T(8,128)(2,1)S(1)} %maximum_bitcast_fusion.2.refs_1_) | copy-start | bytes 2359300
  204.0 4.6 %collective-permute-start.35 = (bf16[1,2,2,96,1024]{4,3,2,1,0:T(8,128)(2,1)S(1)}, bf16[1,2,2,96,1024]{4,3,2,1,0:T(8,128)(2,1)}, u32[]{:S(2)}, u32[]{:S(2)}) collective-permute-start(bf16[1,2,2,96,1024]{4,3,2,1,0:T(8,128)(2,1)S(1)} %maximum_bitcast_fusion.2.refs_1_), channel_id=1, source_target_pairs={{0,8},{1,9},{2,10},{3,11},{4,12},{5,13},{6,14},{7,15},{8,0},{9,1},... | collective-permute-start | bytes 2359304 | tf_op jit(solution)/shard_map/ppermute | solution.py:42
  (5 other events, 12.2 us)

commit v5 on v4

--- a/solution.py
+++ b/solution.py
@@ -268,18 +268,27 @@
     def swapped(pieces):
         return [pieces[1], pieces[0], pieces[3], pieces[2]]
 
-    def halved(parts):
-        parts = [part.astype(jnp.float16).reshape(X, rows, -1) for part in parts]
-        return jnp.concatenate(parts, 2) if len(parts) > 1 else parts[0]
+    def halved(gate_part, hidden_part):
+        lane = lax.broadcasted_iota(jnp.int32, (gate_part.shape[0], LANES), 1)
+        exponents = jnp.where(
+            lane < LANES // 2, gate_part[:, -LANES:], hidden_part[:, -LANES:]
+        )
+        parts = [gate_part[:, :-LANES], hidden_part[:, :-LANES], exponents]
+        return jnp.concatenate(
+            [part.astype(jnp.float16).reshape(X, rows, -1) for part in parts], 2
+        )
 
     def exchanged(parts):
         return [parts[0]] + [over_x(parts[k], k) for k in range(1, X)]
 
-    def summed(pieces):
+    def summed(pieces, which):
+        units = (pieces[0].shape[1] - LANES) // 2
+        place = 2 * units + which * (LANES // 2)
         total_sum = None
         for piece in pieces:
-            piece = piece.astype(jnp.float32)
-            term = piece[:, :-LANES] * jnp.exp(piece[:, -LANES : 1 - LANES] * -LN2)
+            values = piece[:, which * units : (which + 1) * units].astype(jnp.float32)
+            exponent = piece[:, place : place + 1].astype(jnp.float32)
+            term = values * jnp.exp(exponent * -LN2)
             total_sum = term if total_sum is None else total_sum + term
         return total_sum
 
@@ -318,21 +327,19 @@
     near = over_yl(near)
     far = over_other_y(far)
     hidden_part = scaled_product([grad_both], down_pieces, True)
-    first_sent = exchanged(halved([gate_part, hidden_part]))
+    first_sent = exchanged(halved(gate_part, hidden_part))
     input_other = jnp.concatenate([input_first, input_rest], 0)
     gate_part = scaled_product(
         [after(input_other, hidden_part)], swapped(gate_pieces), False
     )
     near, far = after([near, far], gate_part, first_sent[1], first_sent[3])
     hidden_part = scaled_product([far, near], swapped(down_pieces), True)
-    second_sent = exchanged(halved([gate_part, hidden_part]))
+    second_sent = exchanged(halved(gate_part, hidden_part))
     band_other = over_yl(after(band_own, near))
     second_sent, band_other = lax.optimization_barrier((second_sent, band_other))
 
     def up_grads(sent):
-        cuts = sent[0].shape[1] // 2
-        gate = summed([piece[:, :cuts] for piece in sent])
-        return activated(gate, summed([piece[:, cuts:] for piece in sent]))
+        return activated(summed(sent, 0), summed(sent, 1))
 
     first = up_grads(after(first_sent, hidden_part))
     up_grad = jnp.stack([first, up_grads(after(second_sent, first))])

time: 222 us -> 226 us (1.018)
  starting transfers between devices: 56 us -> 67.9 us
  waiting for transfers between devices: 112 us -> 101 us
    ppermute x36, starting transfers between devices: 56 us -> 67.9 us  [send(): return lax.ppermute(value, AXES, pairs)]
    ppermute x36, waiting for transfers between devices: 112 us -> 101 us  [send(): return lax.ppermute(value, AXES, pairs)]
  transfers between devices with their start and end apart: 36 -> 36, of which waited for: 24 -> 19; matrix products, arithmetic and copies ran while one was open for 7% -> 8% of each run, Pallas kernels for 6% -> 6%
where the time goes in v5:
time: 226 us; the launch traced here: 225 us
  waiting for transfers between devices  101 us (45%)
  starting transfers between devices  67.9 us (30%)
  Pallas kernels  26.8 us (12%)
  local copies, waits for them, and re-layouts  16.3 us (7%)
  other arithmetic  11.4 us (5%)
    ppermute x36, waiting for transfers between devices, send(): return lax.ppermute(value, AXES, pairs)  101 us
    ppermute x36, starting transfers between devices, send(): return lax.ppermute(value, AXES, pairs)  67.9 us
    pallas_call x1, Pallas kernels, grad_gram_of(): pl.pallas_call(functools.partial(gram_kernel, 1.0 / total, len(lefts)), o...  13.2 us
    unnamed x42, local copies, waits for them, and re-layouts  10.7 us
    pallas_call x4, Pallas kernels, scaled_product(): pl.pallas_call(functools.partial(scaled_kernel, contract, len(fields)), o...  10.5 us
  transfers between devices with their start and end apart: 36, of which 19 were waited for; matrix products, arithmetic and copies ran while one was open for 8% of the time, Pallas kernels for 6%

profile of v5, /device:TPU:1, one launch (start us, length us, event | category | flops | bytes accessed | tf_op | source)
XLA Modules:
  0.0 225.3 jit_solution(8152960612214720156)
XLA Ops:
  0.8 2.5 %dynamic-slice_dynamic-update-slice_fusion.7 = (bf16[96,3072]{1,0:T(8,128)(2,1)}, bf16[96,3072]{1,0:T(8,128)(2,1)}, bf16[96,3072]{1,0:T(8,128)(2,1)}, bf16[96,30...) fusion(bf16[96,8192]{1,0:T(8,128)(2,1)} %param.5, ...), kind=kLoop, calls=%fused_computation.60 | loop fusion | bytes 3932224
  8.4 2.1 collective-permute-start
  10.5 1.9 collective-permute-start.1
  12.4 1.2 collective-permute-start.2
  13.6 2.5 %collective-permute-start.3 = (bf16[96,2048]{1,0:T(8,128)(2,1)}, bf16[96,2048]{1,0:T(8,128)(2,1)S(1)}, u32[]{:S(2)}, u32[]{:S(2)}) collective-permute-start(bf16[96,2048]{1,0:T(8,128)(2,1)} %pad_maximum_fusion.13), channel_id=1, source_target_pairs={{0,32},{1,33},{2,34},{3,35},{4,36},{5,37},{6,38},{7,39},{8,40},{9,... | collective-permute-start | bytes 1179656 | tf_op jit(solution)/shard_map/ppermute | solution.py:42
  16.3 1.9 dynamic-slice_dynamic-update-slice_fusion.6
  18.2 1.8 dynamic-slice_dynamic-update-slice_fusion.5
  20.0 1.8 dynamic-slice_dynamic-update-slice_fusion.4
  21.8 1.9 dynamic-slice_dynamic-update-slice_fusion
  23.9 8.8 %collective-permute-done.3 = bf16[96,2048]{1,0:T(8,128)(2,1)S(1)} collective-permute-done((bf16[96,2048]{1,0:T(8,128)(2,1)}, bf16[96,2048]{1,0:T(8,128)(2,1)S(1)}, u32[]{:S(2)}, u32[]{:S(2)}) %collective-permute-start.3) | collective-permute-done | bytes 393248 | tf_op jit(solution)/shard_map/ppermute | solution.py:42
  32.6 2.1 collective-permute-done.4
  34.9 2.8 %collective-permute-start.10 = (bf16[2,512,1024]{2,1,0:T(8,128)(2,1)S(1)}, bf16[2,512,1024]{2,1,0:T(8,128)(2,1)S(1)}, u32[]{:S(2)}, u32[]{:S(2)}) collective-permute-start(bf16[2,512,1024]{2,1,0:T(8,128)(2,1)S(1)} %pad_maximum_fusion.2), channel_id=1, source_target_pairs={{0,8},{1,9},{2,10},{3,11},{4,12},{5,13},{6,14},{7,15},{8,0},{9,1},... | collective-permute-start | bytes 6291464 | tf_op jit(solution)/shard_map/ppermute | solution.py:42
  38.7 2.3 %pad_maximum_fusion.6.refs_0_ = bf16[384,2048]{1,0:T(8,128)(2,1)S(1)} fusion(bf16[96,2048]{1,0:T(8,128)(2,1)S(1)} %collective-permute-done.4, bf16[96,2048]{1,0:T(8,128)(2,1)S(1)} %collective-permute-done.3, bf16[96,2048]{1,0:T(8,128)(2,1)S(1)} %collective-permute-done.2, bf16[96,512]{1,0:T(8,128)(2,1)S(1)} %copy-done.6, bf16[96,512]{1,0:T(8,128)(2,1)S(1)} %copy-done.4, ...), kind=kLoop, calls=%fused_computation.11 | loop fusion | flops 11010048 | bytes 3145728 | tf_op jit(solution)/shard_map/concatenate | solution.py:314
  41.9 2.5 %collective-permute-start.6 = (bf16[96,3072]{1,0:T(8,128)(2,1)S(1)}, bf16[96,3072]{1,0:T(8,128)(2,1)S(1)}, u32[]{:S(2)}, u32[]{:S(2)}) collective-permute-start(bf16[96,3072]{1,0:T(8,128)(2,1)S(1)} %copy-done.13), channel_id=1, source_target_pairs={{0,32},{1,33},{2,34},{3,35},{4,36},{5,37},{6,38},{7,39},{8,40},{9,... | collective-permute-start | bytes 1769480 | tf_op jit(solution)/shard_map/ppermute | solution.py:42
  45.4 2.6 %scaled_product.4 = f32[384,1152]{1,0:T(8,128)S(1)} custom-call(bf16[384,2048]{1,0:T(8,128)(2,1)S(1)} %pad_maximum_fusion.6.refs_0_, bf16[512,1024]{1,0:T(8,128)(2,1)S(1)} %get-tuple-element.133.refs_1_.refs_2_, bf16[512,1024]{1,0:T(8,128)(2,1)S(1)} %collective-permute-done.refs_2_.refs_1_, bf16[512,1024]{1,0:T(8,128)(2,1)S(1)} %get-tuple-element.132.refs_3_.refs_4_, ...), custom_call_target="tpu_custom_call" | custom-call | flops 1610612736 | bytes 7340032 | tf_op jit(solution)/shard_map/scaled_product/pallas_call | solution.py:131
  48.0 7.7 %collective-permute-done.5 = bf16[96,3072]{1,0:T(8,128)(2,1)S(1)} collective-permute-done((bf16[96,3072]{1,0:T(8,128)(2,1)S(1)}, bf16[96,3072]{1,0:T(8,128)(2,1)S(1)}, u32[]{:S(2)}, u32[]{:S(2)}) %collective-permute-start.5) | collective-permute-done | bytes 589856 | tf_op jit(solution)/shard_map/ppermute | solution.py:42
  55.8 14.4 %collective-permute-done.6 = bf16[96,3072]{1,0:T(8,128)(2,1)S(1)} collective-permute-done((bf16[96,3072]{1,0:T(8,128)(2,1)S(1)}, bf16[96,3072]{1,0:T(8,128)(2,1)S(1)}, u32[]{:S(2)}, u32[]{:S(2)}) %collective-permute-start.6) | collective-permute-done | bytes 589856 | tf_op jit(solution)/shard_map/ppermute | solution.py:42
  70.2 2.0 collective-permute-done.7
  72.3 2.0 collective-permute-start.11
  75.7 1.5 collective-permute-start.15
  78.3 2.6 %scaled_product.5 = f32[384,1152]{1,0:T(8,128)S(1)} custom-call(bf16[384,3072]{1,0:T(8,128)(2,1)S(1)} %constant_dynamic-update-slice_fusion.refs_0_, bf16[1024,512]{1,0:T(8,128)(2,1)S(1)} %get-tuple-element.129.refs_1_.refs_3_, bf16[1024,512]{1,0:T(8,128)(2,1)S(1)} %collective-permute-done.8.refs_2_, ...), custom_call_target="tpu_custom_call" | custom-call | flops 1610612736 | bytes 7340032 | tf_op jit(solution)/shard_map/scaled_product/pallas_call | solution.py:131
  82.0 2.1 collective-permute-start.14
  85.2 2.6 %scaled_product.6 = f32[384,1152]{1,0:T(8,128)S(1)} custom-call(bf16[384,2048]{1,0:T(8,128)(2,1)S(1)} %constant_dynamic-update-slice_fusion.4.refs_0_, bf16[512,1024]{1,0:T(8,128)(2,1)S(1)} %collective-permute-done.refs_2_.refs_1_, bf16[512,1024]{1,0:T(8,128)(2,1)S(1)} %get-tuple-element.133.refs_1_.refs_2_, ...), custom_call_target="tpu_custom_call" | custom-call | flops 1610612736 | bytes 7340032 | tf_op jit(solution)/shard_map/scaled_product/pallas_call | solution.py:131
  87.9 7.0 %collective-permute-done.15.refs_1_ = bf16[384,1024]{1,0:T(8,128)(2,1)S(1)} collective-permute-done((bf16[384,1024]{1,0:T(8,128)(2,1)S(1)}, bf16[384,1024]{1,0:T(8,128)(2,1)S(1)}, u32[]{:S(2)}, u32[]{:S(2)}) %collective-permute-start.15) | collective-permute-done | bytes 786464 | tf_op jit(solution)/shard_map/ppermute | solution.py:42
  95.0 2.4 %collective-permute-done.16.refs_0_ = bf16[384,1024]{1,0:T(8,128)(2,1)S(1)} collective-permute-done((bf16[384,1024]{1,0:T(8,128)(2,1)S(1)}, bf16[384,1024]{1,0:T(8,128)(2,1)S(1)}, u32[]{:S(2)}, u32[]{:S(2)}) %collective-permute-start.16) | collective-permute-done | bytes 786464 | tf_op jit(solution)/shard_map/ppermute | solution.py:42
  97.3 2.7 %scaled_product.7 = f32[384,1152]{1,0:T(8,128)S(1)} custom-call(bf16[384,1024]{1,0:T(8,128)(2,1)S(1)} %collective-permute-done.16.refs_0_, bf16[384,1024]{1,0:T(8,128)(2,1)S(1)} %collective-permute-done.15.refs_1_, bf16[1024,512]{1,0:T(8,128)(2,1)S(1)} %collective-permute-done.8.refs_2_, bf16[1024,512]{1,0:T(8,128)(2,1)S(1)} %get-tuple-element.129.refs_1_.refs_3_, ...), custom_call_target="tpu_custom_call" | custom-call | flops 1610612736 | bytes 7340032 | tf_op jit(solution)/shard_map/scaled_product/pallas_call | solution.py:131
  101.0 7.1 %collective-permute-start.17 = (f16[96,2176]{1,0:T(8,128)(2,1)S(1)}, f16[96,2176]{1,0:T(8,128)(2,1)S(1)}, u32[]{:S(2)}, u32[]{:S(2)}) collective-permute-start(f16[96,2176]{1,0:T(8,128)(2,1)S(1)} %get-tuple-element.141), channel_id=1, source_target_pairs={{0,16},{1,17},{2,18},{3,19},{4,20},{5,21},{6,22},{7,23},{8,24},{9,... | collective-permute-start | bytes 1253384 | tf_op jit(solution)/shard_map/ppermute | solution.py:42
  108.3 2.4 %collective-permute-start.19 = (f16[96,2176]{1,0:T(8,128)(2,1)S(1)}, f16[96,2176]{1,0:T(8,128)(2,1)S(1)}, u32[]{:S(2)}, u32[]{:S(2)}) collective-permute-start(f16[96,2176]{1,0:T(8,128)(2,1)S(1)} %get-tuple-element.139), channel_id=1, source_target_pairs={{0,48},{1,49},{2,50},{3,51},{4,52},{5,53},{6,54},{7,55},{8,56},{9,... | collective-permute-start | bytes 1253384 | tf_op jit(solution)/shard_map/ppermute | solution.py:42
  111.9 3.4 %collective-permute-done.17 = f16[96,2176]{1,0:T(8,128)(2,1)S(1)} collective-permute-done((f16[96,2176]{1,0:T(8,128)(2,1)S(1)}, f16[96,2176]{1,0:T(8,128)(2,1)S(1)}, u32[]{:S(2)}, u32[]{:S(2)}) %collective-permute-start.17) | collective-permute-done | bytes 417824 | tf_op jit(solution)/shard_map/ppermute | solution.py:42
  115.3 9.0 %collective-permute-done.18 = f16[96,2176]{1,0:T(8,128)(2,1)S(1)} collective-permute-done((f16[96,2176]{1,0:T(8,128)(2,1)S(1)}, f16[96,2176]{1,0:T(8,128)(2,1)S(1)}, u32[]{:S(2)}, u32[]{:S(2)}) %collective-permute-start.18) | collective-permute-done | bytes 417824 | tf_op jit(solution)/shard_map/ppermute | solution.py:42
  125.6 5.5 %collective-permute-start.21 = (bf16[2,96,1024]{2,1,0:T(8,128)(2,1)S(1)}, bf16[2,96,1024]{2,1,0:T(8,128)(2,1)S(1)}, u32[]{:S(2)}, u32[]{:S(2)}) collective-permute-start(bf16[2,96,1024]{2,1,0:T(8,128)(2,1)S(1)} %get-tuple-element.184), channel_id=1, source_target_pairs={{0,0},{1,1},{2,2},{3,3},{4,4},{5,5},{6,6},{7,7},{8,12},{9,13},{10,... | collective-permute-start | bytes 1179656 | tf_op jit(solution)/shard_map/ppermute | solution.py:42
  131.4 4.9 %collective-permute-done.21 = bf16[2,96,1024]{2,1,0:T(8,128)(2,1)S(1)} collective-permute-done((bf16[2,96,1024]{2,1,0:T(8,128)(2,1)S(1)}, bf16[2,96,1024]{2,1,0:T(8,128)(2,1)S(1)}, u32[]{:S(2)}, u32[]{:S(2)}) %collective-permute-start.21) | collective-permute-done | bytes 393248 | tf_op jit(solution)/shard_map/ppermute | solution.py:42
  137.0 7.4 %collective-permute-start.23 = (bf16[2,96,1024]{2,1,0:T(8,128)(2,1)S(1)}, bf16[2,96,1024]{2,1,0:T(8,128)(2,1)S(1)}, u32[]{:S(2)}, u32[]{:S(2)}) collective-permute-start(bf16[2,96,1024]{2,1,0:T(8,128)(2,1)S(1)} %collective-permute-done.21), channel_id=1, source_target_pairs={{0,1},{1,16},{2,35},{3,50},{4,69},{5,84},{6,103},{7,118},{8,65},{9... | collective-permute-start | bytes 1179656 | tf_op jit(solution)/shard_map/ppermute | solution.py:42
  144.3 2.1 collective-permute-start.22
  146.7 11.1 %collective-permute-done.23 = bf16[2,96,1024]{2,1,0:T(8,128)(2,1)S(1)} collective-permute-done((bf16[2,96,1024]{2,1,0:T(8,128)(2,1)S(1)}, bf16[2,96,1024]{2,1,0:T(8,128)(2,1)S(1)}, u32[]{:S(2)}, u32[]{:S(2)}) %collective-permute-start.23) | collective-permute-done | bytes 393248 | tf_op jit(solution)/shard_map/ppermute | solution.py:42
  157.9 6.8 %collective-permute-start.26 = (bf16[2,2,96,1024]{3,2,1,0:T(8,128)(2,1)S(1)}, bf16[2,2,96,1024]{3,2,1,0:T(8,128)(2,1)S(1)}, u32[]{:S(2)}, u32[]{:S(2)}) collective-permute-start(bf16[2,2,96,1024]{3,2,1,0:T(8,128)(2,1)S(1)} %pad_maximum_fusion.10), channel_id=1, source_target_pairs={{0,16},{1,17},{2,18},{3,19},{4,20},{5,21},{6,22},{7,23},{8,24},{9,... | collective-permute-start | bytes 2359304 | tf_op jit(solution)/shard_map/ppermute | solution.py:42
  164.7 1.3 collective-permute-start.27
  166.0 7.4 %collective-permute-start.28 = (bf16[2,2,96,1024]{3,2,1,0:T(8,128)(2,1)S(1)}, bf16[2,2,96,1024]{3,2,1,0:T(8,128)(2,1)S(1)}, u32[]{:S(2)}, u32[]{:S(2)}) collective-permute-start(bf16[2,2,96,1024]{3,2,1,0:T(8,128)(2,1)S(1)} %pad_maximum_fusion.9.refs_4_), channel_id=1, source_target_pairs={{0,2},{1,3},{2,0},{3,1},{4,6},{5,7},{6,4},{7,5},{8,10},{9,11},{10,... | collective-permute-start | bytes 2359304 | tf_op jit(solution)/shard_map/ppermute | solution.py:42
  174.1 3.1 %input_gram.1 = f32[512,1024]{1,0:T(8,128)} custom-call(bf16[1536,512]{1,0:T(8,128)(2,1)S(1)} %bitcast.101, bf16[1536,1024]{1,0:T(8,128)(2,1)S(1)} %bitcast.98), custom_call_target="tpu_custom_call" | custom-call | flops 1610612736 | bytes 6815744 | tf_op jit(solution)/shard_map/input_gram/pallas_call | solution.py:154
  177.2 5.5 %collective-permute-done.26 = bf16[2,2,96,1024]{3,2,1,0:T(8,128)(2,1)S(1)} collective-permute-done((bf16[2,2,96,1024]{3,2,1,0:T(8,128)(2,1)S(1)}, bf16[2,2,96,1024]{3,2,1,0:T(8,128)(2,1)S(1)}, u32[]{:S(2)}, u32[]{:S(2)}) %collective-permute-start.26) | collective-permute-done | bytes 786464 | tf_op jit(solution)/shard_map/ppermute | solution.py:42
  182.6 2.2 collective-permute-done.27
  184.8 6.0 %collective-permute-done.28.refs_5_ = bf16[2,2,96,1024]{3,2,1,0:T(8,128)(2,1)S(1)} collective-permute-done((bf16[2,2,96,1024]{3,2,1,0:T(8,128)(2,1)S(1)}, bf16[2,2,96,1024]{3,2,1,0:T(8,128)(2,1)S(1)}, u32[]{:S(2)}, u32[]{:S(2)}) %collective-permute-start.28) | collective-permute-done | bytes 786464 | tf_op jit(solution)/shard_map/ppermute | solution.py:42
  190.8 2.0 collective-permute-done.29.refs_8_
  193.1 1.7 collective-permute-start.34
  196.1 10.8 %collective-permute-done.30 = bf16[2,96,1024]{2,1,0:T(8,128)(2,1)S(1)} collective-permute-done((bf16[2,96,1024]{2,1,0:T(8,128)(2,1)S(1)}, bf16[2,96,1024]{2,1,0:T(8,128)(2,1)S(1)}, u32[]{:S(2)}, u32[]{:S(2)}) %collective-permute-start.30) | collective-permute-done | bytes 393248 | tf_op jit(solution)/shard_map/ppermute | solution.py:42
  208.2 1.7 collective-permute-start.35
  210.6 1.4 collective-permute-done.35.refs_3_
  212.0 13.2 %grad_gram.1 = f32[2048,1024]{1,0:T(8,128)} custom-call(s32[17]{0:T(128)} %stack.212.places, bf16[3,2,2,96,1024]{4,3,2,1,0:T(8,128)(2,1)} %copy-done, bf16[1,2,2,96,1024]{4,3,2,1,0:T(8,128)(2,1)} %copy-done.9, bf16[3,2,2,96,1024]{4,3,2,1,0:T(8,128)(2,1)} %collective-permute-done.34.refs_2_, bf16[1,2,2,96,1024]{4,3,2,1,0:T(8,128)(2,1)} %collective-permute-done.35.refs_3_, ...), custom_call_target="tpu_custom_call" | custom-call | flops 6442450944 | bytes 17825792 | tf_op jit(solution)/shard_map/grad_gram/pallas_call | solution.py:214
  (128 shorter events, 22.2 us)
Async XLA Ops:
  3.4 5.0 %copy-start.3 = (bf16[96,512]{1,0:T(8,128)(2,1)}, bf16[96,512]{1,0:T(8,128)(2,1)S(1)}, u32[]{:S(2)}) copy-start(bf16[96,512]{1,0:T(8,128)(2,1)S(1)} %get-tuple-element.188) | copy-start | bytes 294916
  3.4 3.8 %copy-start.1 = (bf16[512,2048]{1,0:T(8,128)(2,1)S(1)}, bf16[512,2048]{1,0:T(8,128)(2,1)}, u32[]{:S(2)}) copy-start(bf16[512,2048]{1,0:T(8,128)(2,1)} %param.6) | copy-start | bytes 6291460
  8.4 26.4 %collective-permute-start = (bf16[512,1024]{1,0:T(8,128)(2,1)}, bf16[512,1024]{1,0:T(8,128)(2,1)S(1)}, u32[]{:S(2)}, u32[]{:S(2)}) collective-permute-start(bf16[512,1024]{1,0:T(8,128)(2,1)} %get-tuple-element.134), channel_id=1, source_target_pairs={{0,64},{1,65},{2,66},{3,67},{4,68},{5,69},{6,70},{7,71},{8,72},{9,... | collective-permute-start | bytes 3145736 | tf_op jit(solution)/shard_map/ppermute | solution.py:42
  10.5 13.4 %collective-permute-start.1 = (bf16[96,2048]{1,0:T(8,128)(2,1)}, bf16[96,2048]{1,0:T(8,128)(2,1)}, u32[]{:S(2)}, u32[]{:S(2)}) collective-permute-start(bf16[96,2048]{1,0:T(8,128)(2,1)} %pad_maximum_fusion.11), channel_id=1, source_target_pairs={{0,65},{1,64},{2,67},{3,66},{4,69},{5,68},{6,71},{7,70},{8,73},{9,... | collective-permute-start | bytes 1179656 | tf_op jit(solution)/shard_map/ppermute | solution.py:42
  12.4 11.5 %collective-permute-start.2 = (bf16[96,2048]{1,0:T(8,128)(2,1)}, bf16[96,2048]{1,0:T(8,128)(2,1)S(1)}, u32[]{:S(2)}, u32[]{:S(2)}) collective-permute-start(bf16[96,2048]{1,0:T(8,128)(2,1)} %pad_maximum_fusion.12), channel_id=1, source_target_pairs={{0,16},{1,17},{2,18},{3,19},{4,20},{5,21},{6,22},{7,23},{8,24},{9,... | collective-permute-start | bytes 1179656 | tf_op jit(solution)/shard_map/ppermute | solution.py:42
  13.6 19.0 %collective-permute-start.3 = (bf16[96,2048]{1,0:T(8,128)(2,1)}, bf16[96,2048]{1,0:T(8,128)(2,1)S(1)}, u32[]{:S(2)}, u32[]{:S(2)}) collective-permute-start(bf16[96,2048]{1,0:T(8,128)(2,1)} %pad_maximum_fusion.13), channel_id=1, source_target_pairs={{0,32},{1,33},{2,34},{3,35},{4,36},{5,37},{6,38},{7,39},{8,40},{9,... | collective-permute-start | bytes 1179656 | tf_op jit(solution)/shard_map/ppermute | solution.py:42
  16.1 18.7 %collective-permute-start.4 = (bf16[96,2048]{1,0:T(8,128)(2,1)}, bf16[96,2048]{1,0:T(8,128)(2,1)S(1)}, u32[]{:S(2)}, u32[]{:S(2)}) collective-permute-start(bf16[96,2048]{1,0:T(8,128)(2,1)} %pad_maximum_fusion.14), channel_id=1, source_target_pairs={{0,48},{1,49},{2,50},{3,51},{4,52},{5,53},{6,54},{7,55},{8,56},{9,... | collective-permute-start | bytes 1179656 | tf_op jit(solution)/shard_map/ppermute | solution.py:42
  16.3 7.5 %copy-start.2 = (bf16[2048,512]{1,0:T(8,128)(2,1)S(1)}, bf16[2048,512]{1,0:T(8,128)(2,1)}, u32[]{:S(2)}) copy-start(bf16[2048,512]{1,0:T(8,128)(2,1)} %param.7) | copy-start | bytes 6291460
  34.9 3.8 %copy-start.4 = (bf16[96,512]{1,0:T(8,128)(2,1)S(1)}, bf16[96,512]{1,0:T(8,128)(2,1)}, u32[]{:S(2)}) copy-start(bf16[96,512]{1,0:T(8,128)(2,1)} %copy-done.3) | copy-start | bytes 294916
  34.9 3.8 %copy-start.6 = (bf16[96,512]{1,0:T(8,128)(2,1)S(1)}, bf16[96,512]{1,0:T(8,128)(2,1)}, u32[]{:S(2)}) copy-start(bf16[96,512]{1,0:T(8,128)(2,1)} %copy-done.5) | copy-start | bytes 294916
  34.9 9.4 %collective-permute-start.10 = (bf16[2,512,1024]{2,1,0:T(8,128)(2,1)S(1)}, bf16[2,512,1024]{2,1,0:T(8,128)(2,1)S(1)}, u32[]{:S(2)}, u32[]{:S(2)}) collective-permute-start(bf16[2,512,1024]{2,1,0:T(8,128)(2,1)S(1)} %pad_maximum_fusion.2), channel_id=1, source_target_pairs={{0,8},{1,9},{2,10},{3,11},{4,12},{5,13},{6,14},{7,15},{8,0},{9,1},... | collective-permute-start | bytes 6291464 | tf_op jit(solution)/shard_map/ppermute | solution.py:42
  37.8 4.0 %copy-start.13 = (bf16[96,3072]{1,0:T(8,128)(2,1)S(1)}, bf16[96,3072]{1,0:T(8,128)(2,1)}, u32[]{:S(2)}) copy-start(bf16[96,3072]{1,0:T(8,128)(2,1)} %get-tuple-element.57) | copy-start | bytes 1769476
  37.8 6.5 %copy-start.7 = (bf16[96,3072]{1,0:T(8,128)(2,1)S(1)}, bf16[96,3072]{1,0:T(8,128)(2,1)}, u32[]{:S(2)}) copy-start(bf16[96,3072]{1,0:T(8,128)(2,1)} %get-tuple-element.65) | copy-start | bytes 1769476
  37.9 6.5 %copy-start.12 = (bf16[96,3072]{1,0:T(8,128)(2,1)S(1)}, bf16[96,3072]{1,0:T(8,128)(2,1)}, u32[]{:S(2)}) copy-start(bf16[96,3072]{1,0:T(8,128)(2,1)} %get-tuple-element.58) | copy-start | bytes 1769476
  37.9 34.3 %collective-permute-start.9 = (bf16[288,2048]{1,0:T(8,128)(2,1)S(1)}, bf16[288,2048]{1,0:T(8,128)(2,1)S(1)}, u32[]{:S(2)}, u32[]{:S(2)}) collective-permute-start(bf16[288,2048]{1,0:T(8,128)(2,1)S(1)} %pad_maximum_fusion.8), channel_id=1, source_target_pairs={{0,65},{1,64},{2,67},{3,66},{4,69},{5,68},{6,71},{7,70},{8,73},{9,... | collective-permute-start | bytes 3538952 | tf_op jit(solution)/shard_map/ppermute | solution.py:42
  41.1 14.7 %collective-permute-start.5 = (bf16[96,3072]{1,0:T(8,128)(2,1)S(1)}, bf16[96,3072]{1,0:T(8,128)(2,1)S(1)}, u32[]{:S(2)}, u32[]{:S(2)}) collective-permute-start(bf16[96,3072]{1,0:T(8,128)(2,1)S(1)} %copy-done.14), channel_id=1, source_target_pairs={{0,16},{1,17},{2,18},{3,19},{4,20},{5,21},{6,22},{7,23},{8,24},{9,... | collective-permute-start | bytes 1769480 | tf_op jit(solution)/shard_map/ppermute | solution.py:42
  41.9 28.3 %collective-permute-start.6 = (bf16[96,3072]{1,0:T(8,128)(2,1)S(1)}, bf16[96,3072]{1,0:T(8,128)(2,1)S(1)}, u32[]{:S(2)}, u32[]{:S(2)}) collective-permute-start(bf16[96,3072]{1,0:T(8,128)(2,1)S(1)} %copy-done.13), channel_id=1, source_target_pairs={{0,32},{1,33},{2,34},{3,35},{4,36},{5,37},{6,38},{7,39},{8,40},{9,... | collective-permute-start | bytes 1769480 | tf_op jit(solution)/shard_map/ppermute | solution.py:42
  44.3 27.8 %collective-permute-start.8 = (bf16[1024,512]{1,0:T(8,128)(2,1)S(1)}, bf16[1024,512]{1,0:T(8,128)(2,1)S(1)}, u32[]{:S(2)}, u32[]{:S(2)}) collective-permute-start(bf16[1024,512]{1,0:T(8,128)(2,1)S(1)} %get-tuple-element.59), channel_id=1, source_target_pairs={{0,64},{1,65},{2,66},{3,67},{4,68},{5,69},{6,70},{7,71},{8,72},{9,... | collective-permute-start | bytes 3145736 | tf_op jit(solution)/shard_map/ppermute | solution.py:42
  44.4 27.8 %collective-permute-start.7 = (bf16[96,3072]{1,0:T(8,128)(2,1)S(1)}, bf16[96,3072]{1,0:T(8,128)(2,1)S(1)}, u32[]{:S(2)}, u32[]{:S(2)}) collective-permute-start(bf16[96,3072]{1,0:T(8,128)(2,1)S(1)} %copy-done.12), channel_id=1, source_target_pairs={{0,48},{1,49},{2,50},{3,51},{4,52},{5,53},{6,54},{7,55},{8,56},{9,... | collective-permute-start | bytes 1769480 | tf_op jit(solution)/shard_map/ppermute | solution.py:42
  72.3 5.8 %collective-permute-start.11 = (bf16[2,1024,512]{2,1,0:T(8,128)(2,1)S(1)}, bf16[2,1024,512]{2,1,0:T(8,128)(2,1)S(1)}, u32[]{:S(2)}, u32[]{:S(2)}) collective-permute-start(bf16[2,1024,512]{2,1,0:T(8,128)(2,1)S(1)} %pad_maximum_fusion.3), channel_id=1, source_target_pairs={{0,8},{1,9},{2,10},{3,11},{4,12},{5,13},{6,14},{7,15},{8,0},{9,1},... | collective-permute-start | bytes 6291464 | tf_op jit(solution)/shard_map/ppermute | solution.py:42
  75.7 19.2 %collective-permute-start.15 = (bf16[384,1024]{1,0:T(8,128)(2,1)S(1)}, bf16[384,1024]{1,0:T(8,128)(2,1)S(1)}, u32[]{:S(2)}, u32[]{:S(2)}) collective-permute-start(bf16[384,1024]{1,0:T(8,128)(2,1)S(1)} %get-tuple-element.71), channel_id=1, source_target_pairs={{0,64},{1,65},{2,66},{3,67},{4,68},{5,69},{6,70},{7,71},{8,72},{9,... | collective-permute-start | bytes 2359304 | tf_op jit(solution)/shard_map/ppermute | solution.py:42
  77.3 20.1 %collective-permute-start.16 = (bf16[384,1024]{1,0:T(8,128)(2,1)S(1)}, bf16[384,1024]{1,0:T(8,128)(2,1)S(1)}, u32[]{:S(2)}, u32[]{:S(2)}) collective-permute-start(bf16[384,1024]{1,0:T(8,128)(2,1)S(1)} %get-tuple-element.72), channel_id=1, source_target_pairs={{0,65},{1,64},{2,67},{3,66},{4,69},{5,68},{6,71},{7,70},{8,73},{9,... | collective-permute-start | bytes 2359304 | tf_op jit(solution)/shard_map/ppermute | solution.py:42
  81.9 15.4 %collective-permute-start.12 = (f16[96,2176]{1,0:T(8,128)(2,1)S(1)}, f16[96,2176]{1,0:T(8,128)(2,1)S(1)}, u32[]{:S(2)}, u32[]{:S(2)}) collective-permute-start(f16[96,2176]{1,0:T(8,128)(2,1)S(1)} %get-tuple-element.137), channel_id=1, source_target_pairs={{0,16},{1,17},{2,18},{3,19},{4,20},{5,21},{6,22},{7,23},{8,24},{9,... | collective-permute-start | bytes 1253384 | tf_op jit(solution)/shard_map/ppermute | solution.py:42
  82.0 15.4 %collective-permute-start.14 = (f16[96,2176]{1,0:T(8,128)(2,1)S(1)}, f16[96,2176]{1,0:T(8,128)(2,1)S(1)}, u32[]{:S(2)}, u32[]{:S(2)}) collective-permute-start(f16[96,2176]{1,0:T(8,128)(2,1)S(1)} %get-tuple-element.136), channel_id=1, source_target_pairs={{0,48},{1,49},{2,50},{3,51},{4,52},{5,53},{6,54},{7,55},{8,56},{9,... | collective-permute-start | bytes 1253384 | tf_op jit(solution)/shard_map/ppermute | solution.py:42
  84.1 26.6 %collective-permute-start.13 = (f16[96,2176]{1,0:T(8,128)(2,1)S(1)}, f16[96,2176]{1,0:T(8,128)(2,1)S(1)}, u32[]{:S(2)}, u32[]{:S(2)}) collective-permute-start(f16[96,2176]{1,0:T(8,128)(2,1)S(1)} %get-tuple-element.135), channel_id=1, source_target_pairs={{0,32},{1,33},{2,34},{3,35},{4,36},{5,37},{6,38},{7,39},{8,40},{9,... | collective-permute-start | bytes 1253384 | tf_op jit(solution)/shard_map/ppermute | solution.py:42
  100.2 24.1 %collective-permute-start.20 = (bf16[384,1024]{1,0:T(8,128)(2,1)S(1)}, bf16[384,1024]{1,0:T(8,128)(2,1)S(1)}, u32[]{:S(2)}, u32[]{:S(2)}) collective-permute-start(bf16[384,1024]{1,0:T(8,128)(2,1)S(1)} %get-tuple-element.83), channel_id=1, source_target_pairs={{0,64},{1,65},{2,66},{3,67},{4,68},{5,69},{6,70},{7,71},{8,72},{9,... | collective-permute-start | bytes 2359304 | tf_op jit(solution)/shard_map/ppermute | solution.py:42
  101.0 14.2 %collective-permute-start.17 = (f16[96,2176]{1,0:T(8,128)(2,1)S(1)}, f16[96,2176]{1,0:T(8,128)(2,1)S(1)}, u32[]{:S(2)}, u32[]{:S(2)}) collective-permute-start(f16[96,2176]{1,0:T(8,128)(2,1)S(1)} %get-tuple-element.141), channel_id=1, source_target_pairs={{0,16},{1,17},{2,18},{3,19},{4,20},{5,21},{6,22},{7,23},{8,24},{9,... | collective-permute-start | bytes 1253384 | tf_op jit(solution)/shard_map/ppermute | solution.py:42
  108.1 16.1 %collective-permute-start.18 = (f16[96,2176]{1,0:T(8,128)(2,1)S(1)}, f16[96,2176]{1,0:T(8,128)(2,1)S(1)}, u32[]{:S(2)}, u32[]{:S(2)}) collective-permute-start(f16[96,2176]{1,0:T(8,128)(2,1)S(1)} %get-tuple-element.140), channel_id=1, source_target_pairs={{0,32},{1,33},{2,34},{3,35},{4,36},{5,37},{6,38},{7,39},{8,40},{9,... | collective-permute-start | bytes 1253384 | tf_op jit(solution)/shard_map/ppermute | solution.py:42
  108.3 16.0 %collective-permute-start.19 = (f16[96,2176]{1,0:T(8,128)(2,1)S(1)}, f16[96,2176]{1,0:T(8,128)(2,1)S(1)}, u32[]{:S(2)}, u32[]{:S(2)}) collective-permute-start(f16[96,2176]{1,0:T(8,128)(2,1)S(1)} %get-tuple-element.139), channel_id=1, source_target_pairs={{0,48},{1,49},{2,50},{3,51},{4,52},{5,53},{6,54},{7,55},{8,56},{9,... | collective-permute-start | bytes 1253384 | tf_op jit(solution)/shard_map/ppermute | solution.py:42
  125.6 10.7 %collective-permute-start.21 = (bf16[2,96,1024]{2,1,0:T(8,128)(2,1)S(1)}, bf16[2,96,1024]{2,1,0:T(8,128)(2,1)S(1)}, u32[]{:S(2)}, u32[]{:S(2)}) collective-permute-start(bf16[2,96,1024]{2,1,0:T(8,128)(2,1)S(1)} %get-tuple-element.184), channel_id=1, source_target_pairs={{0,0},{1,1},{2,2},{3,3},{4,4},{5,5},{6,6},{7,7},{8,12},{9,13},{10,... | collective-permute-start | bytes 1179656 | tf_op jit(solution)/shard_map/ppermute | solution.py:42
  136.3 21.6 %collective-permute-start.25 = (bf16[2,384,1536]{2,1,0:T(8,128)(2,1)S(1)}, bf16[2,384,1536]{2,1,0:T(8,128)(2,1)S(1)}, u32[]{:S(2)}, u32[]{:S(2)}) collective-permute-start(bf16[2,384,1536]{2,1,0:T(8,128)(2,1)S(1)} %maximum_maximum_fusion), channel_id=1, source_target_pairs={{0,8},{1,9},{2,10},{3,11},{4,12},{5,13},{6,14},{7,15},{8,0},{9,1},... | collective-permute-start | bytes 7077896 | tf_op jit(solution)/shard_map/ppermute | solution.py:42
  136.3 10.4 %collective-permute-start.24 = (bf16[2,96,1024]{2,1,0:T(8,128)(2,1)S(1)}, bf16[2,96,1024]{2,1,0:T(8,128)(2,1)S(1)}, u32[]{:S(2)}, u32[]{:S(2)}) collective-permute-start(bf16[2,96,1024]{2,1,0:T(8,128)(2,1)S(1)} %get-tuple-element.184), channel_id=1, source_target_pairs={{0,64},{1,65},{2,66},{3,67},{4,68},{5,69},{6,70},{7,71},{8,72},{9,... | collective-permute-start | bytes 1179656 | tf_op jit(solution)/shard_map/ppermute | solution.py:42
  137.0 20.8 %collective-permute-start.23 = (bf16[2,96,1024]{2,1,0:T(8,128)(2,1)S(1)}, bf16[2,96,1024]{2,1,0:T(8,128)(2,1)S(1)}, u32[]{:S(2)}, u32[]{:S(2)}) collective-permute-start(bf16[2,96,1024]{2,1,0:T(8,128)(2,1)S(1)} %collective-permute-done.21), channel_id=1, source_target_pairs={{0,1},{1,16},{2,35},{3,50},{4,69},{5,84},{6,103},{7,118},{8,65},{9... | collective-permute-start | bytes 1179656 | tf_op jit(solution)/shard_map/ppermute | solution.py:42
  144.3 13.5 %collective-permute-start.22 = (bf16[2,96,1024]{2,1,0:T(8,128)(2,1)S(1)}, bf16[2,96,1024]{2,1,0:T(8,128)(2,1)S(1)}, u32[]{:S(2)}, u32[]{:S(2)}) collective-permute-start(bf16[2,96,1024]{2,1,0:T(8,128)(2,1)S(1)} %collective-permute-done.21), channel_id=1, source_target_pairs={{0,0},{1,17},{2,34},{3,51},{4,68},{5,85},{6,102},{7,119},{8,64},{9... | collective-permute-start | bytes 1179656 | tf_op jit(solution)/shard_map/ppermute | solution.py:42
  157.9 15.7 %copy-start.8 = (bf16[2,2,96,1024]{3,2,1,0:T(8,128)(2,1)}, bf16[2,2,96,1024]{3,2,1,0:T(8,128)(2,1)S(1)}, u32[]{:S(2)}) copy-start(bf16[2,2,96,1024]{3,2,1,0:T(8,128)(2,1)S(1)} %pad_maximum_fusion.9.refs_4_) | copy-start | bytes 2359300
  157.9 24.7 %collective-permute-start.26 = (bf16[2,2,96,1024]{3,2,1,0:T(8,128)(2,1)S(1)}, bf16[2,2,96,1024]{3,2,1,0:T(8,128)(2,1)S(1)}, u32[]{:S(2)}, u32[]{:S(2)}) collective-permute-start(bf16[2,2,96,1024]{3,2,1,0:T(8,128)(2,1)S(1)} %pad_maximum_fusion.10), channel_id=1, source_target_pairs={{0,16},{1,17},{2,18},{3,19},{4,20},{5,21},{6,22},{7,23},{8,24},{9,... | collective-permute-start | bytes 2359304 | tf_op jit(solution)/shard_map/ppermute | solution.py:42
  164.7 20.1 %collective-permute-start.27 = (bf16[2,2,96,1024]{3,2,1,0:T(8,128)(2,1)S(1)}, bf16[2,2,96,1024]{3,2,1,0:T(8,128)(2,1)S(1)}, u32[]{:S(2)}, u32[]{:S(2)}) collective-permute-start(bf16[2,2,96,1024]{3,2,1,0:T(8,128)(2,1)S(1)} %pad_maximum_fusion.10), channel_id=1, source_target_pairs={{0,48},{1,49},{2,50},{3,51},{4,52},{5,53},{6,54},{7,55},{8,56},{9,... | collective-permute-start | bytes 2359304 | tf_op jit(solution)/shard_map/ppermute | solution.py:42
  166.0 24.8 %collective-permute-start.28 = (bf16[2,2,96,1024]{3,2,1,0:T(8,128)(2,1)S(1)}, bf16[2,2,96,1024]{3,2,1,0:T(8,128)(2,1)S(1)}, u32[]{:S(2)}, u32[]{:S(2)}) collective-permute-start(bf16[2,2,96,1024]{3,2,1,0:T(8,128)(2,1)S(1)} %pad_maximum_fusion.9.refs_4_), channel_id=1, source_target_pairs={{0,2},{1,3},{2,0},{3,1},{4,6},{5,7},{6,4},{7,5},{8,10},{9,11},{10,... | collective-permute-start | bytes 2359304 | tf_op jit(solution)/shard_map/ppermute | solution.py:42
  173.3 19.5 %collective-permute-start.29 = (bf16[2,2,96,1024]{3,2,1,0:T(8,128)(2,1)S(1)}, bf16[2,2,96,1024]{3,2,1,0:T(8,128)(2,1)S(1)}, u32[]{:S(2)}, u32[]{:S(2)}) collective-permute-start(bf16[2,2,96,1024]{3,2,1,0:T(8,128)(2,1)S(1)} %pad_maximum_fusion.9.refs_4_), channel_id=1, source_target_pairs={{0,6},{1,7},{2,4},{3,5},{4,2},{5,3},{6,0},{7,1},{8,14},{9,15},{10,... | collective-permute-start | bytes 2359304 | tf_op jit(solution)/shard_map/ppermute | solution.py:42
  190.8 5.1 %copy-start.10 = (bf16[2,2,96,1024]{3,2,1,0:T(8,128)(2,1)}, bf16[2,2,96,1024]{3,2,1,0:T(8,128)(2,1)S(1)}, u32[]{:S(2)}) copy-start(bf16[2,2,96,1024]{3,2,1,0:T(8,128)(2,1)S(1)} %collective-permute-done.28.refs_5_) | copy-start | bytes 2359300
  193.1 15.1 %copy-start = (bf16[3,2,2,96,1024]{4,3,2,1,0:T(8,128)(2,1)}, bf16[3,2,2,96,1024]{4,3,2,1,0:T(8,128)(2,1)S(1)}, u32[]{:S(2)}) copy-start(bf16[3,2,2,96,1024]{4,3,2,1,0:T(8,128)(2,1)S(1)} %pad_maximum_fusion.1.refs_0_) | copy-start | bytes 7077892
  193.1 18.8 %collective-permute-start.34 = (bf16[3,2,2,96,1024]{4,3,2,1,0:T(8,128)(2,1)S(1)}, bf16[3,2,2,96,1024]{4,3,2,1,0:T(8,128)(2,1)}, u32[]{:S(2)}, u32[]{:S(2)}) collective-permute-start(bf16[3,2,2,96,1024]{4,3,2,1,0:T(8,128)(2,1)S(1)} %pad_maximum_fusion.1.refs_0_), channel_id=1, source_target_pairs={{0,8},{1,9},{2,10},{3,11},{4,12},{5,13},{6,14},{7,15},{8,0},{9,1},... | collective-permute-start | bytes 7077896 | tf_op jit(solution)/shard_map/ppermute | solution.py:42
  194.9 12.0 %collective-permute-start.30 = (bf16[2,96,1024]{2,1,0:T(8,128)(2,1)S(1)}, bf16[2,96,1024]{2,1,0:T(8,128)(2,1)S(1)}, u32[]{:S(2)}, u32[]{:S(2)}) collective-permute-start(bf16[2,96,1024]{2,1,0:T(8,128)(2,1)S(1)} %slice_bitcast_fusion.21), channel_id=1, source_target_pairs={{0,48},{1,49},{2,50},{3,51},{4,52},{5,53},{6,54},{7,55},{8,56},{9,... | collective-permute-start | bytes 1179656 | tf_op jit(solution)/shard_map/ppermute | solution.py:42
  195.1 11.8 %collective-permute-start.31 = (bf16[2,96,1024]{2,1,0:T(8,128)(2,1)S(1)}, bf16[2,96,1024]{2,1,0:T(8,128)(2,1)S(1)}, u32[]{:S(2)}, u32[]{:S(2)}) collective-permute-start(bf16[2,96,1024]{2,1,0:T(8,128)(2,1)S(1)} %slice_bitcast_fusion.20), channel_id=1, source_target_pairs={{0,16},{1,17},{2,18},{3,19},{4,20},{5,21},{6,22},{7,23},{8,24},{9,... | collective-permute-start | bytes 1179656 | tf_op jit(solution)/shard_map/ppermute | solution.py:42
  195.9 11.4 %collective-permute-start.32 = (bf16[2,96,1024]{2,1,0:T(8,128)(2,1)S(1)}, bf16[2,96,1024]{2,1,0:T(8,128)(2,1)S(1)}, u32[]{:S(2)}, u32[]{:S(2)}) collective-permute-start(bf16[2,96,1024]{2,1,0:T(8,128)(2,1)S(1)} %slice_bitcast_fusion.19), channel_id=1, source_target_pairs={{0,6},{1,7},{2,4},{3,5},{4,2},{5,3},{6,0},{7,1},{8,14},{9,15},{10,... | collective-permute-start | bytes 1179656 | tf_op jit(solution)/shard_map/ppermute | solution.py:42
  196.0 11.3 %collective-permute-start.33 = (bf16[2,96,1024]{2,1,0:T(8,128)(2,1)S(1)}, bf16[2,96,1024]{2,1,0:T(8,128)(2,1)S(1)}, u32[]{:S(2)}, u32[]{:S(2)}) collective-permute-start(bf16[2,96,1024]{2,1,0:T(8,128)(2,1)S(1)} %slice_bitcast_fusion.18), channel_id=1, source_target_pairs={{0,2},{1,3},{2,0},{3,1},{4,6},{5,7},{6,4},{7,5},{8,10},{9,11},{10,... | collective-permute-start | bytes 1179656 | tf_op jit(solution)/shard_map/ppermute | solution.py:42
  207.3 4.6 %copy-start.15 = (bf16[2,96,1024]{2,1,0:T(8,128)(2,1)}, bf16[2,96,1024]{2,1,0:T(8,128)(2,1)S(1)}, u32[]{:S(2)}) copy-start(bf16[2,96,1024]{2,1,0:T(8,128)(2,1)S(1)} %collective-permute-done.32) | copy-start | bytes 1179652
  208.2 3.8 %collective-permute-start.35 = (bf16[1,2,2,96,1024]{4,3,2,1,0:T(8,128)(2,1)S(1)}, bf16[1,2,2,96,1024]{4,3,2,1,0:T(8,128)(2,1)}, u32[]{:S(2)}, u32[]{:S(2)}) collective-permute-start(bf16[1,2,2,96,1024]{4,3,2,1,0:T(8,128)(2,1)S(1)} %maximum_bitcast_fusion.2.refs_1_), channel_id=1, source_target_pairs={{0,8},{1,9},{2,10},{3,11},{4,12},{5,13},{6,14},{7,15},{8,0},{9,1},... | collective-permute-start | bytes 2359304 | tf_op jit(solution)/shard_map/ppermute | solution.py:42
  (5 other events, 11.6 us)
